TPU v7x, 32 devices: a whole 2x2x4 slice. The times are simulated.
32 devices in a mesh: row: 8 (over z, y), col: 4 (over x, core).
Axes of the slice: x: 2, y: 2, z: 4, core: 2. Of those that a mesh axis runs over, the one named last changes fastest.
Arguments:
- features: bfloat16 [256, 32768], P('col', 'row'), may hold values from -6 to 6
- weight: bfloat16 [256, 256], replicated, may hold values from -0.375 to 0.375
- cotangent: bfloat16 [256, 32768], P('col', 'row'), may hold values from -6 to 6
- degree: int32 [32768], P('row'), may hold values from 8 to 256
- tile_src: int32 [256, 10], P('row'), may hold values from 0 to 255, as said below
- tile_count: int32 [256], P('row'), may hold values from 1 to 10, as said below
- tile_vals: bfloat16 [256, 10, 128, 128], P('row'), may hold values from -18 to 18
Outputs:
- output: bfloat16 [256, 32768], P('col', 'row')
- input_grad: float32 [256, 32768], P('col', 'row')
- weight_grad: float32 [256, 256], P(None, 'col')
Inputs may be any that keep to these rules, and one draw needn't show every extreme that they name: `tile_src`: slot 0 of every destination block names the block itself. Its other slots name distinct blocks other than itself, each held by the same index of row as the destination block or by one of the two next to it. `tile_count`: slots at or past this count are empty: their tile_src and tile_vals entries take no part. Every index of row holds a block with all 10 slots live.
All inputs are finite; a program needn't handle non-finite values.
Results may differ from a plain program's by a relative error of at most 0.0057.
Values may be sent and summed in bfloat16 or wider, within the bound.
No kernel may reach another device: no remote copies, remote signals or barrier semaphores. Data moves between devices by JAX's collectives and lax.ppermute only.
A program may use at most 64 MiB of HBM per device.

v0:
```python
import math

import jax
import jax.numpy as jnp
from jax import lax
from jax.sharding import PartitionSpec as P


def padded_2(block, sides, width):
    for axis, dim in sides:
        count = lax.axis_size(axis)
        forward = [(i, i + 1) for i in range(count - 1)]
        backward = [(target, source) for source, target in forward]
        low = lax.ppermute(
            lax.slice_in_dim(block, block.shape[dim] - width, None, axis=dim), axis, forward
        )
        high = lax.ppermute(lax.slice_in_dim(block, 0, width, axis=dim), axis, backward)
        block = jnp.concatenate([low, block, high], axis=dim)
    return block


def shards(features, weight, cotangent, degree, tile_src, tile_count, tile_vals):
    features_here = features.shape[0]
    nodes_here = features.shape[1]
    blocks_here = tile_src.shape[0]
    slot_count = tile_src.shape[1]
    tile_side = tile_vals.shape[2]
    row_index = lax.axis_index("row")
    col_index = lax.axis_index("col")
    node_total = nodes_here * lax.axis_size("row")
    inv_root = lax.rsqrt(degree.astype(jnp.float32))
    scaled = (features.astype(jnp.float32) * inv_root[None, :]).astype(jnp.bfloat16)
    padded = padded_2(scaled, (("row", 1),), nodes_here)
    window = padded.reshape(features_here, 3 * blocks_here, tile_side)
    local_src = tile_src - (row_index - 1) * blocks_here
    live_mask = jnp.arange(slot_count, dtype=jnp.int32)[None, :] < tile_count[:, None]
    sources = window[:, local_src] * live_mask.astype(jnp.bfloat16)[None, :, :, None]
    summed = jnp.einsum("fbtk,btjk->fbj", sources, tile_vals, preferred_element_type=jnp.float32)
    aggregated = (summed.reshape(features_here, nodes_here) * inv_root[None, :]).astype(
        jnp.bfloat16
    )
    first_col = col_index * features_here
    w_cols = lax.dynamic_slice_in_dim(weight, first_col, features_here, 1)
    contract_rows = (((0,), (0,)), ((), ()))
    contract_cols = (((1,), (1,)), ((), ()))
    agg_piece = lax.all_gather(aggregated, "col", axis=0, tiled=True)
    w_part = w_cols
    out_acc = lax.dot_general(w_part, agg_piece, contract_rows, preferred_element_type=jnp.float32)
    grad_rows = lax.dot_general(
        agg_piece, cotangent, contract_cols, preferred_element_type=jnp.float32
    )
    weight_acc = grad_rows
    out_acc, weight_acc = (out_acc, weight_acc)
    w_part = w_cols
    grad_acc = lax.psum_scatter(
        jnp.dot(w_part, cotangent, preferred_element_type=jnp.float32),
        "col",
        scatter_dimension=0,
        tiled=True,
    )
    output = out_acc.astype(jnp.bfloat16)
    weight_grad = lax.psum(weight_acc, "row") / math.sqrt(node_total)
    grad_scaled = (grad_acc * inv_root[None, :]).astype(jnp.bfloat16)
    grad_blocks = grad_scaled.reshape(features_here, blocks_here, tile_side)
    spread = jnp.einsum(
        "fbj,btjk->fbtk", grad_blocks, tile_vals, preferred_element_type=jnp.float32
    )
    spread = spread * live_mask.astype(jnp.float32)[None, :, :, None]
    partial_value = (
        jnp.zeros((features_here, 3 * blocks_here, tile_side), jnp.float32)
        .at[:, local_src]
        .add(spread)
    )
    outer_sums = jnp.concatenate(
        [partial_value[:, :blocks_here], partial_value[:, 2 * blocks_here :]], axis=1
    )
    returned = padded_2(outer_sums.astype(jnp.bfloat16), (("row", 1),), blocks_here).astype(
        outer_sums.dtype
    )
    own_sums = (
        partial_value[:, blocks_here : 2 * blocks_here]
        + returned[:, :blocks_here]
        + returned[:, 3 * blocks_here :]
    )
    input_grad = own_sums.reshape(features_here, nodes_here) * inv_root[None, :]
    return (output, input_grad, weight_grad)


def solution(mesh):
    placed = (
        P("col", "row"),
        P(),
        P("col", "row"),
        P("row"),
        P("row", None),
        P("row"),
        P("row", None, None, None),
    )
    return jax.shard_map(
        shards,
        mesh=mesh,
        in_specs=placed,
        out_specs=(P("col", "row"), P("col", "row"), P(None, "col")),
        check_vma=False,
    )
```

profile of v0, /device:TPU:0, one launch (start us, length us, event | category | flops | bytes accessed | tf_op | source)
XLA Modules:
  0.0 269.7 jit_solution(8999669821281039018)
XLA Ops:
  7.2 0.0 copy-start
  7.2 0.0 reduce-scatter.2.cloned.1.call-start
  7.2 1.0 copy-done
  8.2 3.6 %fusion.12 = f32[256,4096]{1,0:T(8,128)} fusion(bf16[64,4096]{1,0:T(8,128)(2,1)S(1)} %copy-done, bf16[256,256]{1,0:T(8,128)(2,1)} %param.8, s32[]{:T(128)S(6)} %select_n.7), kind=kOutput, calls=%fused_computation.24 | convolution fusion | flops 134217728 | bytes 4784132 | tf_op jit(solution)/shard_map/dot_general | solution.py:56
  11.8 0.0 copy-start.6
  11.8 0.0 copy-start.7
  11.8 0.0 copy-start.5
  11.8 0.0 copy-start.2
  11.8 0.0 reduce-scatter.2.cloned.1.call-update
  11.8 0.0 all-gather.2.cloned.1.call-start
  11.9 0.6 copy-done.6
  12.5 0.1 copy.13
  12.6 0.1 reshape.65
  12.7 0.0 copy-done.7
  12.7 0.1 fusion.15
  12.8 0.0 copy-done.5
  12.8 46.4 %reduce-scatter.2.cloned.1.call-done = f32[64,4096]{1,0:T(8,128)} async-done(((f32[256,4096]{1,0:T(8,128)}), f32[64,4096]{1,0:T(8,128)}) %reduce-scatter.2.cloned.1.call-update) | async-done | bytes 1048592 | tf_op jit(solution)/shard_map/reduce_scatter | solution.py:55
  59.1 0.0 copy-done.2
  59.2 1.4 fusion.10
  60.6 1.3 collective-permute-start.1
  61.9 5.4 %collective-permute-start = (bf16[64,4096]{1,0:T(8,128)(2,1)S(1)}, bf16[64,4096]{1,0:T(8,128)(2,1)}, u32[]{:S(2)}, u32[]{:S(2)}) collective-permute-start(bf16[64,4096]{1,0:T(8,128)(2,1)S(1)} %get-tuple-element.8), channel_id=1, source_target_pairs={{0,4},{4,8},{8,12},{12,16},{16,20},{20,24},{24,28},{1,5},{5,9},{9,... | collective-permute-start | bytes 1572872 | tf_op jit(solution)/shard_map/ppermute | solution.py:14
  67.2 0.1 copy.25
  67.3 9.9 %broadcast_multiply_fusion = f32[32,64,10,128]{3,1,2,0:T(8,128)} fusion(f32[32,10]{1,0:T(8,128)S(1)} %get-tuple-element.9, bf16[32,10,128,128]{3,2,1,0:T(8,128)(2,1)} %param.13, bf16[64,32,128,1]{2,1,0,3:T(8,128)(2,1)S(1)} %bitcast.42), kind=kOutput, calls=%fused_computation.5 | convolution fusion | flops 673710080 | bytes 21497088 | tf_op jit(solution)/shard_map/fbj,btjk->fbtk/dot_general | solution.py:65
  77.2 2.2 broadcast_in_dim.5
  79.4 50.2 %scatter_fusion = f32[64,96,128]{2,0,1:T(8,128)} fusion(f32[64,96,128]{2,0,1:T(8,128)} %broadcast_in_dim.5, s32[320]{0:T(512)S(1)} %reshape.65, f32[320,64,128]{2,1,0:T(8,128)} %bitcast.40), kind=kCustom, calls=%fused_computation.1 | custom fusion | flops 2621440 | bytes 31458560 | tf_op jit(solution)/shard_map/scatter-add | solution.py:72
  129.6 2.2 convert.6
  131.9 0.9 fusion.19
  132.8 4.3 %collective-permute-start.2 = (bf16[64,32,128]{2,0,1:T(8,128)(2,1)S(1)}, bf16[64,32,128]{2,0,1:T(8,128)(2,1)}, u32[]{:S(2)}, u32[]{:S(2)}) collective-permute-start(bf16[64,32,128]{2,0,1:T(8,128)(2,1)S(1)} %get-tuple-element.3), channel_id=1, source_target_pairs={{0,4},{4,8},{8,12},{12,16},{16,20},{20,24},{24,28},{1,5},{5,9},{9,... | collective-permute-start | bytes 1572872 | tf_op jit(solution)/shard_map/ppermute | solution.py:14
  137.1 1.3 collective-permute-start.3
  138.4 0.0 collective-permute-done.1
  138.4 0.0 copy-start.3
  138.4 0.8 copy-done.3
  139.2 0.0 collective-permute-done
  139.2 1.6 copy_bitcast_fusion
  140.8 13.3 %gather_fusion = bf16[320,64,128]{2,1,0:T(8,128)(2,1)} fusion(bf16[64,96,128]{2,0,1:T(8,128)(2,1)S(1)} %copy_bitcast_fusion, s32[1024]{0:T(1024)S(1)} %pad_clamp_fusion), kind=kCustom, calls=%fused_computation | custom fusion | bytes 10487040 | tf_op jit(solution)/shard_map/gather | solution.py:37
  154.2 9.3 %fusion.4 = f32[32,8,8,128]{3,2,1,0:T(8,128)S(1)} fusion(bf16[32,10,128,128]{3,2,1,0:T(8,128)(2,1)} %param.13, bf16[32,10,64,128]{3,2,1,0:T(8,128)(2,1)} %bitcast.41, bf16[32,10]{1,0:T(8,128)(2,1)S(1)} %get-tuple-element.10), kind=kOutput, calls=%fused_computation.10 | convolution fusion | flops 673710080 | bytes 16777856 | tf_op jit(solution)/shard_map/fbtk,btjk->fbj/dot_general | solution.py:38
  163.5 0.0 copy-start.4
  163.5 0.0 collective-permute-done.2
  163.5 0.0 collective-permute-done.3
  163.5 3.0 %bitcast_multiply_fusion = (f32[64,4096]{1,0:T(8,128)}, bf16[64,4096]{1,0:T(8,128)(2,1)}) fusion(f32[4096]{0:T(1024)S(1)} %convert_rsqrt_fusion, f32[32,8,8,128]{3,2,1,0:T(8,128)S(1)} %fusion.4, f32[64,96,128]{2,0,1:T(8,128)} %scatter_fusion, bf16[64,32,128]{2,0,1:T(8,128)(2,1)} %collective-permute-done.3, bf16[64,32,128]{2,0,1:T(8,128)(2,1)S(1)} %get-tuple-element.3, ...), kind=kLoop, calls=%fused_computation.11 | loop fusion | flops 3407872 | bytes 5783552 | tf_op jit(solution)/shard_map/mul | solution.py:85
  166.5 0.0 all-gather.2.cloned.1.call-update
  166.5 0.0 all-reduce.2.cloned.1.call-start
  166.6 22.2 %all-gather.2.cloned.1.call-done = bf16[256,4096]{1,0:T(8,128)(2,1)} async-done(((bf16[64,4096]{1,0:T(8,128)(2,1)}), bf16[256,4096]{1,0:T(8,128)(2,1)}) %all-gather.2.cloned.1.call-update) | async-done | bytes 2097168 | tf_op jit(solution)/shard_map/all_gather | solution.py:46
  188.8 0.0 copy-start.1
  188.8 3.1 %fusion.20 = f32[256,64]{0,1:T(8,128)} fusion(bf16[256,4096]{1,0:T(8,128)(2,1)} %all-gather.2.cloned.1.call-done, bf16[64,4096]{1,0:T(8,128)(2,1)S(1)} %copy-done), kind=kOutput, calls=%fused_computation.37 | convolution fusion | flops 134217728 | bytes 2686976 | tf_op jit(solution)/shard_map/dot_general | solution.py:49
  191.9 0.0 all-reduce.2.cloned.1.call-update
  191.9 0.0 copy-done.4
  191.9 0.0 copy-done.1
  192.0 1.4 convolution_convert_fusion
  193.3 68.3 %all-reduce.2.cloned.1.call-done = f32[256,64]{0,1:T(8,128)} async-done(((f32[256,64]{0,1:T(8,128)}), f32[256,64]{0,1:T(8,128)}) %all-reduce.2.cloned.1.call-update) | async-done | bytes 65552 | tf_op jit(solution)/shard_map/psum | solution.py:62
  261.7 1.5 broadcast_multiply_fusion.1
  (3 shorter events, 0.0 us)
Async XLA Ops:
  7.2 1.0 copy-start
  7.2 52.0 %reduce-scatter.2.cloned.1.call-start = ((), (), s32[]{:S(2)}) async-start(), calls=%async_computation.2 | async-start | bytes 5242880 | tf_op jit(solution)/shard_map/reduce_scatter | solution.py:55
  11.8 0.7 copy-start.6
  11.8 0.9 copy-start.7
  11.8 1.0 copy-start.5
  11.8 47.4 %copy-start.2 = (bf16[64,4096]{1,0:T(8,128)(2,1)S(1)}, bf16[64,4096]{1,0:T(8,128)(2,1)}, u32[]{:S(2)}) copy-start(bf16[64,4096]{1,0:T(8,128)(2,1)} %param.7) | copy-start | bytes 1572868
  11.8 177.0 %all-gather.2.cloned.1.call-start = ((), (), s32[]{:S(2)}) async-start(), calls=%async_computation.1 | async-start | bytes 2621440 | tf_op jit(solution)/shard_map/all_gather | solution.py:46
  60.6 77.8 %collective-permute-start.1 = (bf16[64,4096]{1,0:T(8,128)(2,1)S(1)}, bf16[64,4096]{1,0:T(8,128)(2,1)S(1)}, u32[]{:S(2)}, u32[]{:S(2)}) collective-permute-start(bf16[64,4096]{1,0:T(8,128)(2,1)S(1)} %get-tuple-element.8), channel_id=1, source_target_pairs={{4,0},{8,4},{12,8},{16,12},{20,16},{24,20},{28,24},{5,1},{9,5},{13... | collective-permute-start | bytes 1572872 | tf_op jit(solution)/shard_map/ppermute | solution.py:17
  61.9 77.3 %collective-permute-start = (bf16[64,4096]{1,0:T(8,128)(2,1)S(1)}, bf16[64,4096]{1,0:T(8,128)(2,1)}, u32[]{:S(2)}, u32[]{:S(2)}) collective-permute-start(bf16[64,4096]{1,0:T(8,128)(2,1)S(1)} %get-tuple-element.8), channel_id=1, source_target_pairs={{0,4},{4,8},{8,12},{12,16},{16,20},{20,24},{24,28},{1,5},{5,9},{9,... | collective-permute-start | bytes 1572872 | tf_op jit(solution)/shard_map/ppermute | solution.py:14
  132.8 30.8 %collective-permute-start.2 = (bf16[64,32,128]{2,0,1:T(8,128)(2,1)S(1)}, bf16[64,32,128]{2,0,1:T(8,128)(2,1)}, u32[]{:S(2)}, u32[]{:S(2)}) collective-permute-start(bf16[64,32,128]{2,0,1:T(8,128)(2,1)S(1)} %get-tuple-element.3), channel_id=1, source_target_pairs={{0,4},{4,8},{8,12},{12,16},{16,20},{20,24},{24,28},{1,5},{5,9},{9,... | collective-permute-start | bytes 1572872 | tf_op jit(solution)/shard_map/ppermute | solution.py:14
  137.1 26.4 %collective-permute-start.3 = (bf16[64,32,128]{2,0,1:T(8,128)(2,1)}, bf16[64,32,128]{2,0,1:T(8,128)(2,1)}, u32[]{:S(2)}, u32[]{:S(2)}) collective-permute-start(bf16[64,32,128]{2,0,1:T(8,128)(2,1)} %get-tuple-element.4), channel_id=1, source_target_pairs={{4,0},{8,4},{12,8},{16,12},{20,16},{24,20},{28,24},{5,1},{9,5},{13... | collective-permute-start | bytes 1572872 | tf_op jit(solution)/shard_map/ppermute | solution.py:17
  138.4 0.8 copy-start.3
  163.5 28.4 %copy-start.4 = (bf16[256,256]{1,0:T(8,128)(2,1)S(1)}, bf16[256,256]{1,0:T(8,128)(2,1)}, u32[]{:S(2)}) copy-start(bf16[256,256]{1,0:T(8,128)(2,1)} %param.8) | copy-start | bytes 393220
  166.5 95.1 %all-reduce.2.cloned.1.call-start = ((), (), s32[]{:S(2)}) async-start(), calls=%async_computation.3 | async-start | bytes 131072 | tf_op jit(solution)/shard_map/psum | solution.py:62
  188.8 3.2 %copy-start.1 = (bf16[256,4096]{1,0:T(8,128)(2,1)S(1)}, bf16[256,4096]{1,0:T(8,128)(2,1)}, u32[]{:S(2)}) copy-start(bf16[256,4096]{1,0:T(8,128)(2,1)} %all-gather.2.cloned.1.call-done) | copy-start | bytes 6291460
Sparse Core Ops, SparseCore 0:
  11.9 47.1 reduce-scatter.1
  166.6 22.0 all-gather.1
  193.1 68.4 all-reduce.1
where the time goes:
time: 271 us; the launch traced here: 270 us
  waiting for transfers between devices  137 us (51%)
  other arithmetic  60 us (22%)
  matrix products  27.3 us (10%)
  local copies, waits for them, and re-layouts  19.1 us (7%)
  between operations  13.9 us (5%)
  starting transfers between devices  12.4 us (5%)
    psum x1, waiting for transfers between devices, shards(): weight_grad = lax.psum(weight_acc, 'row') / math.sqrt(node_total)  68.3 us
    scatter-add x1, other arithmetic, shards(): partial_value = jnp.zeros((features_here, 3 * blocks_here, tile_side), jn...  50.2 us
    reduce_scatter x1, waiting for transfers between devices, shards(): lax.psum_scatter(jnp.dot(w_part, cotangent, preferred_element_type=jnp.fl...  46.4 us
    all_gather x1, waiting for transfers between devices, shards(): agg_piece = lax.all_gather(aggregated, 'col', axis=0, tiled=True)  22.2 us
    gather x1, local copies, waits for them, and re-layouts, shards(): window[:, local_src] * live_mask.astype(jnp.bfloat16)[None, :, :, None]  13.3 us
    dot_general x1, matrix products, shards(): jnp.einsum('fbj,btjk->fbtk', grad_blocks, tile_vals, preferred_element_ty...  9.94 us
    ppermute x2, starting transfers between devices, padded_2(): lax.ppermute(lax.slice_in_dim(block, block.shape[dim] - width, None, axis...  9.7 us
    dot_general x1, matrix products, shards(): jnp.einsum('fbtk,btjk->fbj', sources, tile_vals, preferred_element_type=j...  9.31 us
  transfers between devices with their start and end apart: 7, of which 3 were waited for; matrix products, arithmetic and copies ran while one was open for 34% of the time, Pallas kernels for 0%

commit v1 on v0

v1 whole, which is shorter than its diff:
```python
import functools
import math

import jax
import jax.numpy as jnp
from jax import lax
from jax.experimental import pallas as pl
from jax.experimental.pallas import tpu as pltpu
from jax.sharding import PartitionSpec as P

CONTRACT_LAST = (((1,), (1,)), ((), ()))
VMEM_BYTES = 40 * 1024 * 1024


def xor_pairs(count, bit):
    return [(i, i ^ bit) for i in range(count)]


def pair_offsets(count):
    offsets = [0]
    bit = count // 2
    while bit:
        offsets += [offset ^ bit for offset in offsets]
        bit //= 2
    return offsets


def gather_pieces(own, axis):
    count = lax.axis_size(axis)
    pieces = [own]
    bit = count // 2
    while bit:
        pieces += [lax.ppermute(piece, axis, xor_pairs(count, bit)) for piece in pieces]
        bit //= 2
    return pieces


def across(count, step):
    moves = []
    for i in range(count):
        target = i + step if i % 2 == 0 else i - step
        if 0 <= target < count:
            moves.append((i, target))
    return moves


def tile_copies(tiles_hbm, tiles, sems, count):
    for b in range(count):
        pltpu.make_async_copy(tiles_hbm.at[b], tiles.at[b], sems.at[b]).start()


def block_at(index, side):
    return pl.ds(pl.multiple_of(index * side, side), side)


def forward_kernel(slot_ref, own, pair, diag, inv, tiles_hbm, agg, window, tiles, sems):
    blocks, slots, side, _ = tiles.shape
    nodes = own.shape[1]
    tile_copies(tiles_hbm, tiles, sems, blocks)
    window[:, :nodes] = own[...]
    window[:, nodes : 2 * nodes] = pair[...]
    window[:, 2 * nodes : 3 * nodes] = diag[...]
    window[:, 3 * nodes :] = jnp.zeros((own.shape[0], side), window.dtype)

    def block(b, carry):
        pltpu.make_async_copy(tiles_hbm.at[b], tiles.at[b], sems.at[b]).wait()
        total = None
        for t in range(0, slots, 2):
            taken = range(t, min(t + 2, slots))
            source = jnp.concatenate(
                [window[:, block_at(slot_ref[b, s], side)] for s in taken], axis=1
            )
            edges = jnp.concatenate([tiles[b, s] for s in taken], axis=1)
            part = lax.dot_general(source, edges, CONTRACT_LAST, preferred_element_type=jnp.float32)
            total = part if total is None else total + part
        here = block_at(b, side)
        agg[:, here] = (total * inv[:, here]).astype(agg.dtype)
        return carry

    lax.fori_loop(0, blocks, block, 0)


def backward_kernel(slot_ref, weight, inv, *refs, pieces):
    cots = refs[:pieces]
    tiles_hbm, own, pair, diag, acc, scaled, tiles, sems = refs[pieces:]
    blocks, slots, side, _ = tiles.shape
    nodes = own.shape[1]
    tile_copies(tiles_hbm, tiles, sems, blocks)
    acc[...] = jnp.zeros_like(acc)
    wide = 4 * side

    def mix(i, carry):
        here = pl.ds(pl.multiple_of(i * wide, wide), wide)
        cot = jnp.concatenate([c[:, here] for c in cots], axis=0)
        grad = jnp.dot(weight[...], cot, preferred_element_type=jnp.float32)
        scaled[:, here] = (grad * inv[:, here]).astype(scaled.dtype)
        return carry

    lax.fori_loop(0, nodes // wide, mix, 0)

    def block(b, carry):
        pltpu.make_async_copy(tiles_hbm.at[b], tiles.at[b], sems.at[b]).wait()
        grad = scaled[:, block_at(b, side)]
        places = [block_at(slot_ref[b, s], side) for s in range(slots)]
        sums = [acc[:, place] for place in places]
        for t in range(0, slots, 2):
            taken = range(t, min(t + 2, slots))
            edges = jnp.concatenate([tiles[b, s] for s in taken], axis=1)
            part = jnp.dot(grad, edges, preferred_element_type=jnp.float32)
            for k, s in enumerate(taken):
                acc[:, places[s]] = sums[s] + part[:, k * side : (k + 1) * side]
        return carry

    lax.fori_loop(0, blocks, block, 0)

    own[...] = acc[:, :nodes]
    pair[...] = acc[:, nodes : 2 * nodes].astype(pair.dtype)
    diag[...] = acc[:, 2 * nodes : 3 * nodes].astype(diag.dtype)


def shards(features, weight, cotangent, degree, tile_src, tile_count, tile_vals):
    width, nodes = features.shape
    blocks, slots, side, _ = tile_vals.shape
    rows = lax.axis_size("row")
    cols = lax.axis_size("col")
    row = lax.axis_index("row")
    col = lax.axis_index("col")
    offsets = pair_offsets(cols)
    vmem = pl.BlockSpec(memory_space=pltpu.VMEM)
    smem = pl.BlockSpec(memory_space=pltpu.SMEM)
    hbm = pl.BlockSpec(memory_space=pl.ANY)

    inv_root = lax.rsqrt(degree.astype(jnp.float32))[None, :]
    scaled = (features.astype(jnp.float32) * inv_root).astype(jnp.bfloat16)
    pair_scaled = lax.ppermute(scaled, "row", xor_pairs(rows, 1))
    diag_scaled = lax.ppermute(pair_scaled, "row", across(rows, 2))
    cots = gather_pieces(cotangent, "col")

    source_row = tile_src // blocks
    group = jnp.where(source_row == row, 0, jnp.where(source_row == (row ^ 1), 1, 2))
    live = jnp.arange(slots, dtype=jnp.int32)[None, :] < tile_count[:, None]
    slot_at = jnp.where(live, group * blocks + tile_src % blocks, 3 * blocks)

    def piece_of(offset):
        return (col ^ offset) * width

    mine = col * width
    weight_rows = lax.dynamic_slice_in_dim(weight, mine, width, 0)
    weight_cols = lax.dynamic_slice_in_dim(weight, mine, width, 1)
    weight_back = jnp.concatenate(
        [lax.dynamic_slice_in_dim(weight_rows, piece_of(o), width, 1) for o in offsets], axis=1
    )
    weight_out = jnp.concatenate(
        [lax.dynamic_slice_in_dim(weight_cols, piece_of(o), width, 0) for o in offsets], axis=0
    )

    params = pltpu.CompilerParams(vmem_limit_bytes=VMEM_BYTES)
    tile_scratch = [
        pltpu.VMEM(tile_vals.shape, tile_vals.dtype),
        pltpu.SemaphoreType.DMA((blocks,)),
    ]
    narrow = jax.ShapeDtypeStruct((width, nodes), jnp.bfloat16)
    full = jax.ShapeDtypeStruct((width, nodes), jnp.float32)
    own_grad, pair_grad, diag_grad = pl.pallas_call(
        functools.partial(backward_kernel, pieces=cols),
        out_shape=(full, narrow, narrow),
        in_specs=[smem, vmem, vmem] + [vmem] * cols + [hbm],
        out_specs=(vmem, vmem, vmem),
        scratch_shapes=[
            pltpu.VMEM((width, 3 * nodes + side), jnp.float32),
            pltpu.VMEM((width, nodes), jnp.bfloat16),
        ]
        + tile_scratch,
        compiler_params=params,
        name="backward_tiles",
    )(slot_at, weight_back, inv_root, *cots, tile_vals)
    relayed = lax.ppermute(diag_grad, "row", [(t, s) for s, t in across(rows, 2)])
    joined = (pair_grad.astype(jnp.float32) + relayed.astype(jnp.float32)).astype(jnp.bfloat16)
    returned = lax.ppermute(joined, "row", xor_pairs(rows, 1))

    aggregated = pl.pallas_call(
        forward_kernel,
        out_shape=narrow,
        in_specs=[smem, vmem, vmem, vmem, vmem, hbm],
        out_specs=vmem,
        scratch_shapes=[pltpu.VMEM((width, 3 * nodes + side), jnp.bfloat16)] + tile_scratch,
        compiler_params=params,
        name="forward_tiles",
    )(slot_at, scaled, pair_scaled, diag_scaled, inv_root, tile_vals)

    agg_pieces = gather_pieces(aggregated, "col")
    output = lax.dot_general(
        weight_out,
        jnp.concatenate(agg_pieces, axis=0),
        (((0,), (0,)), ((), ())),
        preferred_element_type=jnp.float32,
    ).astype(jnp.bfloat16)

    partial = [
        lax.dot_general(aggregated, c, CONTRACT_LAST, preferred_element_type=jnp.float32)
        for c in cots
    ]
    total = jnp.stack(partial)
    if rows & (rows - 1) == 0:
        bit = 1
        while bit < rows:
            total = total + lax.ppermute(total, "row", xor_pairs(rows, bit))
            bit *= 2
    else:
        total = lax.psum(total, "row")
    total = total / math.sqrt(nodes * rows)
    weight_grad = jnp.zeros((width * cols, width), jnp.float32)
    for k, offset in enumerate(offsets):
        block = total[k] if offset == 0 else lax.ppermute(total[k], "col", xor_pairs(cols, offset))
        weight_grad = lax.dynamic_update_slice_in_dim(weight_grad, block, piece_of(offset), 0)

    input_grad = (own_grad + returned.astype(jnp.float32)) * inv_root
    return (output, input_grad, weight_grad)


def solution(mesh):
    placed = (
        P("col", "row"),
        P(),
        P("col", "row"),
        P("row"),
        P("row", None),
        P("row"),
        P("row", None, None, None),
    )
    return jax.shard_map(
        shards,
        mesh=mesh,
        in_specs=placed,
        out_specs=(P("col", "row"), P("col", "row"), P(None, "col")),
        check_vma=False,
    )
```

time: 271 us -> 122 us (0.45)
  waiting for transfers between devices: 137 us -> 67.9 us
  other arithmetic: 60 us -> 2.93 us
  matrix products: 27.3 us -> 2.44 us
  Pallas kernels: 0 us -> 21.6 us
  local copies, waits for them, and re-layouts: 19.1 us -> 4.59 us
  between operations: 13.9 us -> 0.8 us
  starting transfers between devices: 12.4 us -> 20.9 us
    psum x1 -> x0, waiting for transfers between devices: 68.3 us -> none  [shards(): weight_grad = lax.psum(weight_acc, 'row') / math.sqrt(node_total)]
    ppermute x4 -> x16, waiting for transfers between devices: 0.01 us -> 67.9 us  [the longest x1 14.7 us: shards(): lax.ppermute(diag_grad, 'row', [(t, s) for s, t in across(rows, 2)])]
    scatter-add x1 -> x0, other arithmetic: 50.2 us -> none  [shards(): partial_value = jnp.zeros((features_here, 3 * blocks_here, tile_side), jn...]
    reduce_scatter x1 -> x0, waiting for transfers between devices: 46.4 us -> none  [shards(): lax.psum_scatter(jnp.dot(w_part, cotangent, preferred_element_type=jnp.fl...]
    dot_general x5, matrix products: 27.3 us -> 2.44 us  [the longest x1 1.3 us: shards(): lax.dot_general(weight_out, jnp.concatenate(agg_pieces, axis=0), (((0,),...]
    all_gather x1 -> x0, waiting for transfers between devices: 22.2 us -> none  [shards(): agg_piece = lax.all_gather(aggregated, 'col', axis=0, tiled=True)]
    pallas_call x0 -> x2, Pallas kernels: none -> 21.6 us  [the longest x1 12.4 us: shards(): pl.pallas_call(forward_kernel, out_shape=narrow, in_specs=[smem, vmem, vm...]
    gather x1 -> x0, local copies, waits for them, and re-layouts: 13.3 us -> none  [shards(): window[:, local_src] * live_mask.astype(jnp.bfloat16)[None, :, :, None]]
  transfers between devices with their start and end apart: 7 -> 16, of which waited for: 3 -> 11; matrix products, arithmetic and copies ran while one was open for 34% -> 4% of each run, Pallas kernels for 0% -> 0%
where the time goes in v1:
time: 122 us; the launch traced here: 121 us
  waiting for transfers between devices  67.9 us (56%)
  Pallas kernels  21.6 us (18%)
  starting transfers between devices  20.9 us (17%)
  local copies, waits for them, and re-layouts  4.59 us (4%)
  other arithmetic  2.93 us (2%)
  matrix products  2.44 us (2%)
    ppermute x1, waiting for transfers between devices, shards(): lax.ppermute(diag_grad, 'row', [(t, s) for s, t in across(rows, 2)])  14.7 us
    ppermute x1, waiting for transfers between devices, shards(): returned = lax.ppermute(joined, 'row', xor_pairs(rows, 1))  12.5 us
    pallas_call x1, Pallas kernels, shards(): pl.pallas_call(forward_kernel, out_shape=narrow, in_specs=[smem, vmem, vm...  12.4 us
    ppermute x1, waiting for transfers between devices, shards(): pair_scaled = lax.ppermute(scaled, 'row', xor_pairs(rows, 1))  11.6 us
    ppermute x6, waiting for transfers between devices, gather_pieces(): lax.ppermute(piece, axis, xor_pairs(count, bit))  10.6 us
    pallas_call x1, Pallas kernels, shards(): pl.pallas_call(functools.partial(backward_kernel, pieces=cols), out_shape...  9.21 us
    ppermute x1, waiting for transfers between devices, shards(): diag_scaled = lax.ppermute(pair_scaled, 'row', across(rows, 2))  8.78 us
    ppermute x3, waiting for transfers between devices, shards(): total = total + lax.ppermute(total, 'row', xor_pairs(rows, bit))  8.3 us
  transfers between devices with their start and end apart: 16, of which 11 were waited for; matrix products, arithmetic and copies ran while one was open for 4% of the time, Pallas kernels for 0%

profile of v1, /device:TPU:0, one launch (start us, length us, event | category | flops | bytes accessed | tf_op | source)
XLA Modules:
  0.0 121.2 jit_solution(11306935860830057139)
XLA Ops:
  0.6 3.0 %collective-permute-start.5 = (bf16[64,4096]{1,0:T(8,128)(2,1)}, bf16[64,4096]{1,0:T(8,128)(2,1)S(1)}, u32[]{:S(2)}, u32[]{:S(2)}) collective-permute-start(bf16[64,4096]{1,0:T(8,128)(2,1)} %refs_0_.1), channel_id=1, source_target_pairs={{0,2},{1,3},{2,0},{3,1},{4,6},{5,7},{6,4},{7,5},{8,10},{9,11},{10,... | collective-permute-start | bytes 1572872 | tf_op jit(solution)/shard_map/ppermute | solution.py:33
  3.6 0.0 collective-permute-start.6
  3.6 0.8 copy.10
  4.4 1.1 fusion.19
  5.5 10.3 %collective-permute-done.5.refs_1_ = bf16[64,4096]{1,0:T(8,128)(2,1)S(1)} collective-permute-done((bf16[64,4096]{1,0:T(8,128)(2,1)}, bf16[64,4096]{1,0:T(8,128)(2,1)S(1)}, u32[]{:S(2)}, u32[]{:S(2)}) %collective-permute-start.5) | collective-permute-done | bytes 524320 | tf_op jit(solution)/shard_map/ppermute | solution.py:33
  15.8 0.0 collective-permute-start.7
  15.8 0.1 pad_maximum_fusion.1.weight
  15.9 0.7 convert_rsqrt_fusion
  16.6 0.7 fusion.15.slot_ref
  17.3 0.0 collective-permute-done.6.refs_2_
  17.3 0.4 collective-permute-done.7.refs_3_
  17.7 0.0 copy-start.1
  17.7 1.0 copy-done.1
  18.7 0.0 copy-start.2
  18.7 0.0 copy-start
  18.7 9.2 %backward_tiles.1 = (f32[64,4096]{1,0:T(8,128)S(1)}, bf16[64,4096]{1,0:T(8,128)(2,1)S(1)}, bf16[64,4096]{1,0:T(8,128)(2,1)S(1)}) custom-call(s32[32,10]{1,0:T(8,128)S(1)} %fusion.15.slot_ref, bf16[64,256]{1,0:T(8,128)(2,1)S(1)} %pad_maximum_fusion.1.weight, f32[1,4096]{1,0:T(1,128)S(1)} %bitcast.25, bf16[64,4096]{1,0:T(8,128)(2,1)S(1)} %copy-done.1, ...), custom_call_target="tpu_custom_call" | custom-call | tf_op jit(solution)/shard_map/backward_tiles/pallas_call | solution.py:164
  27.9 1.3 %collective-permute-start.8 = (bf16[64,4096]{1,0:T(8,128)(2,1)S(1)}, bf16[64,4096]{1,0:T(8,128)(2,1)S(1)}, u32[]{:S(2)}, u32[]{:S(2)}) collective-permute-start(bf16[64,4096]{1,0:T(8,128)(2,1)S(1)} %get-tuple-element.8), channel_id=1, source_target_pairs={{8,0},{16,8},{4,12},{24,16},{12,20},{20,28},{9,1},{17,9},{5,13},{2... | collective-permute-start | bytes 1572872 | tf_op jit(solution)/shard_map/ppermute | solution.py:177
  29.2 14.7 %collective-permute-done.8 = bf16[64,4096]{1,0:T(8,128)(2,1)S(1)} collective-permute-done((bf16[64,4096]{1,0:T(8,128)(2,1)S(1)}, bf16[64,4096]{1,0:T(8,128)(2,1)S(1)}, u32[]{:S(2)}, u32[]{:S(2)}) %collective-permute-start.8) | collective-permute-done | bytes 524320 | tf_op jit(solution)/shard_map/ppermute | solution.py:177
  43.9 0.1 add_convert_fusion
  44.0 0.8 collective-permute-start.9
  44.9 12.5 %collective-permute-done.9 = bf16[64,4096]{1,0:T(8,128)(2,1)S(1)} collective-permute-done((bf16[64,4096]{1,0:T(8,128)(2,1)S(1)}, bf16[64,4096]{1,0:T(8,128)(2,1)S(1)}, u32[]{:S(2)}, u32[]{:S(2)}) %collective-permute-start.9) | collective-permute-done | bytes 524320 | tf_op jit(solution)/shard_map/ppermute | solution.py:179
  57.3 0.0 copy-done.2
  57.3 1.2 add_multiply_fusion
  58.5 0.7 collective-permute-start
  59.2 11.6 %collective-permute-done.pair = bf16[64,4096]{1,0:T(8,128)(2,1)S(1)} collective-permute-done((bf16[64,4096]{1,0:T(8,128)(2,1)S(1)}, bf16[64,4096]{1,0:T(8,128)(2,1)S(1)}, u32[]{:S(2)}, u32[]{:S(2)}) %collective-permute-start) | collective-permute-done | bytes 524320 | tf_op jit(solution)/shard_map/ppermute | solution.py:135
  70.8 3.5 %collective-permute-start.1 = (bf16[64,4096]{1,0:T(8,128)(2,1)S(1)}, bf16[64,4096]{1,0:T(8,128)(2,1)S(1)}, u32[]{:S(2)}, u32[]{:S(2)}) collective-permute-start(bf16[64,4096]{1,0:T(8,128)(2,1)S(1)} %collective-permute-done.pair), channel_id=1, source_target_pairs={{0,8},{8,16},{12,4},{16,24},{20,12},{28,20},{1,9},{9,17},{13,5},{1... | collective-permute-start | bytes 1572872 | tf_op jit(solution)/shard_map/ppermute | solution.py:136
  74.3 8.8 %collective-permute-done.1.diag = bf16[64,4096]{1,0:T(8,128)(2,1)S(1)} collective-permute-done((bf16[64,4096]{1,0:T(8,128)(2,1)S(1)}, bf16[64,4096]{1,0:T(8,128)(2,1)S(1)}, u32[]{:S(2)}, u32[]{:S(2)}) %collective-permute-start.1) | collective-permute-done | bytes 524320 | tf_op jit(solution)/shard_map/ppermute | solution.py:136
  83.1 0.0 copy-done
  83.1 12.4 %forward_tiles.1 = bf16[64,4096]{1,0:T(8,128)(2,1)S(1)} custom-call(s32[32,10]{1,0:T(8,128)S(1)} %fusion.15.slot_ref, bf16[64,4096]{1,0:T(8,128)(2,1)S(1)} %get-tuple-element.21.own, bf16[64,4096]{1,0:T(8,128)(2,1)S(1)} %collective-permute-done.pair, bf16[64,4096]{1,0:T(8,128)(2,1)S(1)} %collective-permute-done.1.diag, f32[1,4096]{1,0:T(1,128)S(1)} %bitcast.26, ...), custom_call_target="tpu_custom_call" | custom-call | tf_op jit(solution)/shard_map/forward_tiles/pallas_call | solution.py:181
  95.5 0.3 convolution_bitcast_fusion.3
  95.8 0.3 convolution_bitcast_fusion
  96.1 0.3 convolution_bitcast_fusion.1
  96.4 0.3 convolution_bitcast_fusion.2
  96.7 2.3 %collective-permute-start.10 = (f32[4,64,64]{1,2,0:T(8,128)S(1)}, f32[4,64,64]{1,2,0:T(8,128)S(1)}, u32[]{:S(2)}, u32[]{:S(2)}) collective-permute-start(f32[4,64,64]{1,2,0:T(8,128)S(1)} %pad_maximum_fusion), channel_id=1, source_target_pairs={{0,4},{4,0},{8,12},{12,8},{16,20},{20,16},{24,28},{28,24},{1,5},{5... | collective-permute-start | bytes 196616 | tf_op jit(solution)/shard_map/ppermute | solution.py:207
  99.1 1.5 %collective-permute-start.2 = (bf16[64,4096]{1,0:T(8,128)(2,1)S(1)}, bf16[64,4096]{1,0:T(8,128)(2,1)S(1)}, u32[]{:S(2)}, u32[]{:S(2)}) collective-permute-start(bf16[64,4096]{1,0:T(8,128)(2,1)S(1)} %forward_tiles.1), channel_id=1, source_target_pairs={{0,2},{1,3},{2,0},{3,1},{4,6},{5,7},{6,4},{7,5},{8,10},{9,11},{10,... | collective-permute-start | bytes 1572872 | tf_op jit(solution)/shard_map/ppermute | solution.py:33
  100.6 1.4 %collective-permute-done.10 = f32[4,64,64]{1,2,0:T(8,128)S(1)} collective-permute-done((f32[4,64,64]{1,2,0:T(8,128)S(1)}, f32[4,64,64]{1,2,0:T(8,128)S(1)}, u32[]{:S(2)}, u32[]{:S(2)}) %collective-permute-start.10) | collective-permute-done | bytes 65568 | tf_op jit(solution)/shard_map/ppermute | solution.py:207
  102.0 2.3 %collective-permute-start.11 = (f32[4,64,64]{1,2,0:T(8,128)S(1)}, f32[4,64,64]{1,2,0:T(8,128)S(1)}, u32[]{:S(2)}, u32[]{:S(2)}) collective-permute-start(f32[4,64,64]{1,2,0:T(8,128)S(1)} %fusion.18), channel_id=1, source_target_pairs={{0,8},{4,12},{8,0},{12,4},{16,24},{20,28},{24,16},{28,20},{1,9},{5... | collective-permute-start | bytes 196616 | tf_op jit(solution)/shard_map/ppermute | solution.py:207
  104.3 4.2 %collective-permute-done.11 = f32[4,64,64]{1,2,0:T(8,128)S(1)} collective-permute-done((f32[4,64,64]{1,2,0:T(8,128)S(1)}, f32[4,64,64]{1,2,0:T(8,128)S(1)}, u32[]{:S(2)}, u32[]{:S(2)}) %collective-permute-start.11) | collective-permute-done | bytes 65568 | tf_op jit(solution)/shard_map/ppermute | solution.py:207
  108.5 2.7 %collective-permute-start.12 = (f32[4,64,64]{1,2,0:T(8,128)S(1)}, f32[4,64,64]{1,2,0:T(8,128)S(1)}, u32[]{:S(2)}, u32[]{:S(2)}) collective-permute-start(f32[4,64,64]{1,2,0:T(8,128)S(1)} %fusion.28), channel_id=1, source_target_pairs={{0,16},{4,20},{8,24},{12,28},{16,0},{20,4},{24,8},{28,12},{1,17},{... | collective-permute-start | bytes 196616 | tf_op jit(solution)/shard_map/ppermute | solution.py:207
  111.2 0.0 collective-permute-start.3
  111.2 0.0 collective-permute-done.2
  111.3 0.5 collective-permute-start.4
  111.8 2.7 %collective-permute-done.12 = f32[4,64,64]{1,2,0:T(8,128)S(1)} collective-permute-done((f32[4,64,64]{1,2,0:T(8,128)S(1)}, f32[4,64,64]{1,2,0:T(8,128)S(1)}, u32[]{:S(2)}, u32[]{:S(2)}) %collective-permute-start.12) | collective-permute-done | bytes 65568 | tf_op jit(solution)/shard_map/ppermute | solution.py:207
  114.5 1.6 %collective-permute-start.13 = (f32[64,64]{0,1:T(8,128)S(1)}, f32[64,64]{0,1:T(8,128)S(1)}, u32[]{:S(2)}, u32[]{:S(2)}) collective-permute-start(f32[64,64]{0,1:T(8,128)S(1)} %get-tuple-element.11), channel_id=1, source_target_pairs={{0,2},{1,3},{2,0},{3,1},{4,6},{5,7},{6,4},{7,5},{8,10},{9,11},{10,... | collective-permute-start | bytes 49160 | tf_op jit(solution)/shard_map/ppermute | solution.py:214
  116.1 0.0 collective-permute-start.14
  116.1 0.6 collective-permute-start.15
  116.7 0.4 dynamic_update_slice.12
  117.1 1.4 %collective-permute-done.13 = f32[64,64]{0,1:T(8,128)S(1)} collective-permute-done((f32[64,64]{0,1:T(8,128)S(1)}, f32[64,64]{0,1:T(8,128)S(1)}, u32[]{:S(2)}, u32[]{:S(2)}) %collective-permute-start.13) | collective-permute-done | bytes 16416 | tf_op jit(solution)/shard_map/ppermute | solution.py:214
  118.5 0.2 dynamic_update_slice.13
  118.7 0.0 collective-permute-done.14
  118.7 0.6 dynamic_update_slice.14
  119.3 0.1 collective-permute-done.15
  119.4 0.4 dynamic_update_slice.15
  119.8 0.0 copy-start.3
  119.8 0.0 collective-permute-done.3
  119.8 0.0 collective-permute-done.4
  119.9 1.3 %convolution_convert_fusion = bf16[64,4096]{1,0:T(8,128)(2,1)} fusion(bf16[64,4096]{1,0:T(8,128)(2,1)S(1)} %collective-permute-done.4, bf16[64,4096]{1,0:T(8,128)(2,1)S(1)} %collective-permute-done.3, bf16[64,4096]{1,0:T(8,128)(2,1)S(1)} %collective-permute-done.2, bf16[64,4096]{1,0:T(8,128)(2,1)S(1)} %forward_tiles.1, ...), kind=kOutput, calls=%fused_computation | convolution fusion | flops 142999552 | bytes 2654208 | tf_op jit(solution)/shard_map/dot_general | solution.py:192
  121.2 0.0 copy-done.3
  (6 shorter events, 0.1 us)
Async XLA Ops:
  0.6 15.1 %collective-permute-start.5 = (bf16[64,4096]{1,0:T(8,128)(2,1)}, bf16[64,4096]{1,0:T(8,128)(2,1)S(1)}, u32[]{:S(2)}, u32[]{:S(2)}) collective-permute-start(bf16[64,4096]{1,0:T(8,128)(2,1)} %refs_0_.1), channel_id=1, source_target_pairs={{0,2},{1,3},{2,0},{3,1},{4,6},{5,7},{6,4},{7,5},{8,10},{9,11},{10,... | collective-permute-start | bytes 1572872 | tf_op jit(solution)/shard_map/ppermute | solution.py:33
  3.6 13.7 %collective-permute-start.6 = (bf16[64,4096]{1,0:T(8,128)(2,1)}, bf16[64,4096]{1,0:T(8,128)(2,1)S(1)}, u32[]{:S(2)}, u32[]{:S(2)}) collective-permute-start(bf16[64,4096]{1,0:T(8,128)(2,1)} %refs_0_.1), channel_id=1, source_target_pairs={{0,1},{1,0},{2,3},{3,2},{4,5},{5,4},{6,7},{7,6},{8,9},{9,8},{10,11... | collective-permute-start | bytes 1572872 | tf_op jit(solution)/shard_map/ppermute | solution.py:33
  15.8 1.9 %collective-permute-start.7 = (bf16[64,4096]{1,0:T(8,128)(2,1)S(1)}, bf16[64,4096]{1,0:T(8,128)(2,1)S(1)}, u32[]{:S(2)}, u32[]{:S(2)}) collective-permute-start(bf16[64,4096]{1,0:T(8,128)(2,1)S(1)} %collective-permute-done.5.refs_1_), channel_id=1, source_target_pairs={{0,1},{1,0},{2,3},{3,2},{4,5},{5,4},{6,7},{7,6},{8,9},{9,8},{10,11... | collective-permute-start | bytes 1572872 | tf_op jit(solution)/shard_map/ppermute | solution.py:33
  17.7 1.0 copy-start.1
  18.7 38.6 %copy-start.2 = (bf16[64,4096]{1,0:T(8,128)(2,1)S(1)}, bf16[64,4096]{1,0:T(8,128)(2,1)}, u32[]{:S(2)}) copy-start(bf16[64,4096]{1,0:T(8,128)(2,1)} %param.7) | copy-start | bytes 1572868
  18.7 64.4 %copy-start = (bf16[32,10,128,128]{3,2,1,0:T(8,128)(2,1)S(1)}, bf16[32,10,128,128]{3,2,1,0:T(8,128)(2,1)}, u32[]{:S(2)}) copy-start(bf16[32,10,128,128]{3,2,1,0:T(8,128)(2,1)} %refs_4_.1) | copy-start | bytes 31457284
  27.9 16.0 %collective-permute-start.8 = (bf16[64,4096]{1,0:T(8,128)(2,1)S(1)}, bf16[64,4096]{1,0:T(8,128)(2,1)S(1)}, u32[]{:S(2)}, u32[]{:S(2)}) collective-permute-start(bf16[64,4096]{1,0:T(8,128)(2,1)S(1)} %get-tuple-element.8), channel_id=1, source_target_pairs={{8,0},{16,8},{4,12},{24,16},{12,20},{20,28},{9,1},{17,9},{5,13},{2... | collective-permute-start | bytes 1572872 | tf_op jit(solution)/shard_map/ppermute | solution.py:177
  44.0 13.3 %collective-permute-start.9 = (bf16[64,4096]{1,0:T(8,128)(2,1)S(1)}, bf16[64,4096]{1,0:T(8,128)(2,1)S(1)}, u32[]{:S(2)}, u32[]{:S(2)}) collective-permute-start(bf16[64,4096]{1,0:T(8,128)(2,1)S(1)} %add_convert_fusion), channel_id=1, source_target_pairs={{0,4},{4,0},{8,12},{12,8},{16,20},{20,16},{24,28},{28,24},{1,5},{5... | collective-permute-start | bytes 1572872 | tf_op jit(solution)/shard_map/ppermute | solution.py:179
  58.5 12.3 %collective-permute-start = (bf16[64,4096]{1,0:T(8,128)(2,1)S(1)}, bf16[64,4096]{1,0:T(8,128)(2,1)S(1)}, u32[]{:S(2)}, u32[]{:S(2)}) collective-permute-start(bf16[64,4096]{1,0:T(8,128)(2,1)S(1)} %get-tuple-element.21.own), channel_id=1, source_target_pairs={{0,4},{4,0},{8,12},{12,8},{16,20},{20,16},{24,28},{28,24},{1,5},{5... | collective-permute-start | bytes 1572872 | tf_op jit(solution)/shard_map/ppermute | solution.py:135
  70.8 12.3 %collective-permute-start.1 = (bf16[64,4096]{1,0:T(8,128)(2,1)S(1)}, bf16[64,4096]{1,0:T(8,128)(2,1)S(1)}, u32[]{:S(2)}, u32[]{:S(2)}) collective-permute-start(bf16[64,4096]{1,0:T(8,128)(2,1)S(1)} %collective-permute-done.pair), channel_id=1, source_target_pairs={{0,8},{8,16},{12,4},{16,24},{20,12},{28,20},{1,9},{9,17},{13,5},{1... | collective-permute-start | bytes 1572872 | tf_op jit(solution)/shard_map/ppermute | solution.py:136
  96.7 5.3 %collective-permute-start.10 = (f32[4,64,64]{1,2,0:T(8,128)S(1)}, f32[4,64,64]{1,2,0:T(8,128)S(1)}, u32[]{:S(2)}, u32[]{:S(2)}) collective-permute-start(f32[4,64,64]{1,2,0:T(8,128)S(1)} %pad_maximum_fusion), channel_id=1, source_target_pairs={{0,4},{4,0},{8,12},{12,8},{16,20},{20,16},{24,28},{28,24},{1,5},{5... | collective-permute-start | bytes 196616 | tf_op jit(solution)/shard_map/ppermute | solution.py:207
  99.1 12.2 %collective-permute-start.2 = (bf16[64,4096]{1,0:T(8,128)(2,1)S(1)}, bf16[64,4096]{1,0:T(8,128)(2,1)S(1)}, u32[]{:S(2)}, u32[]{:S(2)}) collective-permute-start(bf16[64,4096]{1,0:T(8,128)(2,1)S(1)} %forward_tiles.1), channel_id=1, source_target_pairs={{0,2},{1,3},{2,0},{3,1},{4,6},{5,7},{6,4},{7,5},{8,10},{9,11},{10,... | collective-permute-start | bytes 1572872 | tf_op jit(solution)/shard_map/ppermute | solution.py:33
  102.0 6.5 %collective-permute-start.11 = (f32[4,64,64]{1,2,0:T(8,128)S(1)}, f32[4,64,64]{1,2,0:T(8,128)S(1)}, u32[]{:S(2)}, u32[]{:S(2)}) collective-permute-start(f32[4,64,64]{1,2,0:T(8,128)S(1)} %fusion.18), channel_id=1, source_target_pairs={{0,8},{4,12},{8,0},{12,4},{16,24},{20,28},{24,16},{28,20},{1,9},{5... | collective-permute-start | bytes 196616 | tf_op jit(solution)/shard_map/ppermute | solution.py:207
  108.5 5.9 %collective-permute-start.12 = (f32[4,64,64]{1,2,0:T(8,128)S(1)}, f32[4,64,64]{1,2,0:T(8,128)S(1)}, u32[]{:S(2)}, u32[]{:S(2)}) collective-permute-start(f32[4,64,64]{1,2,0:T(8,128)S(1)} %fusion.28), channel_id=1, source_target_pairs={{0,16},{4,20},{8,24},{12,28},{16,0},{20,4},{24,8},{28,12},{1,17},{... | collective-permute-start | bytes 196616 | tf_op jit(solution)/shard_map/ppermute | solution.py:207
  111.2 8.6 %collective-permute-start.3 = (bf16[64,4096]{1,0:T(8,128)(2,1)S(1)}, bf16[64,4096]{1,0:T(8,128)(2,1)S(1)}, u32[]{:S(2)}, u32[]{:S(2)}) collective-permute-start(bf16[64,4096]{1,0:T(8,128)(2,1)S(1)} %forward_tiles.1), channel_id=1, source_target_pairs={{0,1},{1,0},{2,3},{3,2},{4,5},{5,4},{6,7},{7,6},{8,9},{9,8},{10,11... | collective-permute-start | bytes 1572872 | tf_op jit(solution)/shard_map/ppermute | solution.py:33
  111.3 8.6 %collective-permute-start.4 = (bf16[64,4096]{1,0:T(8,128)(2,1)S(1)}, bf16[64,4096]{1,0:T(8,128)(2,1)S(1)}, u32[]{:S(2)}, u32[]{:S(2)}) collective-permute-start(bf16[64,4096]{1,0:T(8,128)(2,1)S(1)} %collective-permute-done.2), channel_id=1, source_target_pairs={{0,1},{1,0},{2,3},{3,2},{4,5},{5,4},{6,7},{7,6},{8,9},{9,8},{10,11... | collective-permute-start | bytes 1572872 | tf_op jit(solution)/shard_map/ppermute | solution.py:33
  114.5 4.0 %collective-permute-start.13 = (f32[64,64]{0,1:T(8,128)S(1)}, f32[64,64]{0,1:T(8,128)S(1)}, u32[]{:S(2)}, u32[]{:S(2)}) collective-permute-start(f32[64,64]{0,1:T(8,128)S(1)} %get-tuple-element.11), channel_id=1, source_target_pairs={{0,2},{1,3},{2,0},{3,1},{4,6},{5,7},{6,4},{7,5},{8,10},{9,11},{10,... | collective-permute-start | bytes 49160 | tf_op jit(solution)/shard_map/ppermute | solution.py:214
  116.1 2.7 %collective-permute-start.14 = (f32[64,64]{0,1:T(8,128)S(1)}, f32[64,64]{0,1:T(8,128)S(1)}, u32[]{:S(2)}, u32[]{:S(2)}) collective-permute-start(f32[64,64]{0,1:T(8,128)S(1)} %get-tuple-element.10), channel_id=1, source_target_pairs={{0,1},{1,0},{2,3},{3,2},{4,5},{5,4},{6,7},{7,6},{8,9},{9,8},{10,11... | collective-permute-start | bytes 49160 | tf_op jit(solution)/shard_map/ppermute | solution.py:214
  116.1 3.3 %collective-permute-start.15 = (f32[64,64]{0,1:T(8,128)S(1)}, f32[64,64]{0,1:T(8,128)S(1)}, u32[]{:S(2)}, u32[]{:S(2)}) collective-permute-start(f32[64,64]{0,1:T(8,128)S(1)} %get-tuple-element.9), channel_id=1, source_target_pairs={{0,3},{1,2},{2,1},{3,0},{4,7},{5,6},{6,5},{7,4},{8,11},{9,10},{10,... | collective-permute-start | bytes 49160 | tf_op jit(solution)/shard_map/ppermute | solution.py:214
  119.8 1.3 %copy-start.3 = (f32[256,64]{0,1:T(8,128)}, f32[256,64]{0,1:T(8,128)S(1)}, u32[]{:S(2)}) copy-start(f32[256,64]{0,1:T(8,128)S(1)} %dynamic_update_slice.15) | copy-start | bytes 196612

commit v2 on v1

v2 whole, which is shorter than its diff:
```python
import functools
import math

import jax
import jax.numpy as jnp
from jax import lax
from jax.experimental import pallas as pl
from jax.experimental.pallas import tpu as pltpu
from jax.sharding import PartitionSpec as P

CONTRACT_LAST = (((1,), (1,)), ((), ()))
VMEM_BYTES = 40 * 1024 * 1024


def xor_pairs(count, bit):
    return [(i, i ^ bit) for i in range(count)]


def across(count, step):
    moves = []
    for i in range(count):
        target = i + step if i % 2 == 0 else i - step
        if 0 <= target < count:
            moves.append((i, target))
    return moves


def bits_of(count):
    bits = []
    bit = count // 2
    while bit:
        bits.append(bit)
        bit //= 2
    return bits


def pair_offsets(count):
    offsets = [0]
    for bit in bits_of(count):
        offsets += [offset ^ bit for offset in offsets]
    return offsets


def gather_pieces(own, axis, others=()):
    count = lax.axis_size(axis)
    pieces = [own]
    for bit in bits_of(count):
        sent = pieces[:1] + list(tied(pieces[1:], others)) if others else pieces
        pieces = pieces + [lax.ppermute(piece, axis, xor_pairs(count, bit)) for piece in sent]
    return pieces


def tied(values, others):
    return lax.optimization_barrier((tuple(values), tuple(others)))[0]


def far(value):
    return pltpu.with_memory_space_constraint(value, pltpu.HBM)


def block_at(index, side):
    return pl.ds(pl.multiple_of(index * side, side), side)


def slot_groups(slots):
    return [range(t, min(t + 2, slots)) for t in range(0, slots, 2)]


def start_tiles(tiles_hbm, tiles, sems):
    for b in range(tiles.shape[0]):
        pltpu.make_async_copy(tiles_hbm.at[b], tiles.at[b], sems.at[b]).start()


def each_block(block, tiles_hbm, tiles, sems, together):
    def step(i, carry):
        for k in range(together):
            b = i * together + k
            pltpu.make_async_copy(tiles_hbm.at[b], tiles.at[b], sems.at[b]).wait()
        for k in range(together):
            block(i * together + k)
        return carry

    lax.fori_loop(0, tiles.shape[0] // together, step, 0)


def backward_kernel(slot_ref, inv, weight_hbm, *refs, offsets, together):
    cots, refs = refs[: len(offsets)], refs[len(offsets) :]
    tiles_hbm, own_grad, pair_grad, diag_grad, acc, cot, scaled, weight, tiles, sems, in_sems = refs
    blocks, slots, side, _ = tiles.shape
    width, nodes = own_grad.shape
    col = lax.axis_index("col")
    arrivals = [pltpu.make_async_copy(weight_hbm.at[block_at(col, width)], weight, in_sems.at[0])]
    for k, (value, offset) in enumerate(zip(cots, offsets)):
        place = cot.at[block_at(col ^ offset, width)]
        arrivals.append(pltpu.make_async_copy(value, place, in_sems.at[k + 1]))
    for copy in arrivals:
        copy.start()
    start_tiles(tiles_hbm, tiles, sems)
    acc[...] = jnp.zeros_like(acc)
    for copy in arrivals:
        copy.wait()
    wide = 4 * side

    def mix(i, carry):
        here = pl.ds(pl.multiple_of(i * wide, wide), wide)
        grad = jnp.dot(weight[...], cot[:, here], preferred_element_type=jnp.float32)
        scaled[:, here] = (grad * inv[:, here]).astype(scaled.dtype)
        return carry

    lax.fori_loop(0, nodes // wide, mix, 0)

    def block(b):
        places = [block_at(slot_ref[b, s], side) for s in range(slots)]
        grad = scaled[:, block_at(b, side)]
        sums = [acc[:, place] for place in places]
        for group in slot_groups(slots):
            edges = jnp.concatenate([tiles[b, s] for s in group], axis=1)
            spread = jnp.dot(grad, edges, preferred_element_type=jnp.float32)
            for k, s in enumerate(group):
                acc[:, places[s]] = sums[s] + spread[:, k * side : (k + 1) * side]

    each_block(block, tiles_hbm, tiles, sems, together)
    diag_grad[...] = acc[:, 2 * nodes : 3 * nodes].astype(diag_grad.dtype)
    pair_grad[...] = acc[:, nodes : 2 * nodes].astype(pair_grad.dtype)
    own_grad[...] = acc[:, :nodes]


def forward_kernel(slot_ref, inv, own, pair, diag, tiles_hbm, agg, window, tiles, sems, in_sems, *, together):
    blocks, slots, side, _ = tiles.shape
    width, nodes = agg.shape
    arrivals = [
        pltpu.make_async_copy(value, window.at[:, k * nodes : (k + 1) * nodes], in_sems.at[k])
        for k, value in enumerate((own, pair, diag))
    ]
    for copy in arrivals:
        copy.start()
    start_tiles(tiles_hbm, tiles, sems)
    window[:, 3 * nodes :] = jnp.zeros((width, side), window.dtype)
    for copy in arrivals:
        copy.wait()

    def block(b):
        places = [block_at(slot_ref[b, s], side) for s in range(slots)]
        total = None
        for group in slot_groups(slots):
            source = jnp.concatenate([window[:, places[s]] for s in group], axis=1)
            edges = jnp.concatenate([tiles[b, s] for s in group], axis=1)
            part = lax.dot_general(source, edges, CONTRACT_LAST, preferred_element_type=jnp.float32)
            total = part if total is None else total + part
        here = block_at(b, side)
        agg[:, here] = (total * inv[:, here]).astype(agg.dtype)

    each_block(block, tiles_hbm, tiles, sems, together)


def outer_kernel(*refs):
    cots, agg, out = refs[:-2], refs[-2], refs[-1]
    out[...] = jnp.concatenate(
        [
            lax.dot_general(c[...], agg[...], CONTRACT_LAST, preferred_element_type=jnp.float32)
            for c in cots
        ],
        axis=1,
    )


def shards(features, weight, cotangent, degree, tile_src, tile_count, tile_vals):
    width, nodes = features.shape
    blocks, slots, side, _ = tile_vals.shape
    rows = lax.axis_size("row")
    cols = lax.axis_size("col")
    row = lax.axis_index("row")
    col = lax.axis_index("col")
    offsets = pair_offsets(cols)
    vmem = pl.BlockSpec(memory_space=pltpu.VMEM)
    smem = pl.BlockSpec(memory_space=pltpu.SMEM)
    hbm = pl.BlockSpec(memory_space=pl.ANY)
    params = pltpu.CompilerParams(vmem_limit_bytes=VMEM_BYTES)
    light = pl.CostEstimate(flops=1, bytes_accessed=1, transcendentals=0)
    narrow = jax.ShapeDtypeStruct((width, nodes), jnp.bfloat16)
    full = jax.ShapeDtypeStruct((width, nodes), jnp.float32)
    together = 2 if blocks % 2 == 0 else 1
    tile_scratch = [
        pltpu.VMEM(tile_vals.shape, tile_vals.dtype),
        pltpu.SemaphoreType.DMA((blocks,)),
    ]
    pairs = xor_pairs(rows, 1)
    outward = across(rows, 2)
    inward = [(target, source) for source, target in outward]

    inv_root = lax.rsqrt(degree.astype(jnp.float32))[None, :]
    scaled = (features.astype(jnp.float32) * inv_root).astype(jnp.bfloat16)
    pair_scaled = lax.ppermute(scaled, "row", pairs)
    diag_scaled = lax.ppermute(pair_scaled, "row", outward)
    cots = gather_pieces(cotangent, "col")

    source_row = tile_src // blocks
    group = jnp.where(source_row == row, 0, jnp.where(source_row == (row ^ 1), 1, 2))
    live = jnp.arange(slots, dtype=jnp.int32)[None, :] < tile_count[:, None]
    slot_at = jnp.where(live, group * blocks + tile_src % blocks, 3 * blocks)
    weight_cols = lax.dynamic_slice_in_dim(weight, col * width, width, 1)

    cots_here = tied(cots[1:], (pair_scaled,))
    own_grad, pair_grad, diag_grad = pl.pallas_call(
        functools.partial(backward_kernel, offsets=offsets, together=together),
        out_shape=(full, narrow, narrow),
        in_specs=[smem, vmem] + [hbm] * (cols + 2),
        out_specs=(vmem,) * 3,
        scratch_shapes=[
            pltpu.VMEM((width, 3 * nodes + side), jnp.float32),
            pltpu.VMEM((width * cols, nodes), jnp.bfloat16),
            pltpu.VMEM((width, nodes), jnp.bfloat16),
            pltpu.VMEM((width, width * cols), jnp.bfloat16),
        ]
        + tile_scratch
        + [pltpu.SemaphoreType.DMA((cols + 1,))],
        compiler_params=params,
        cost_estimate=light,
        name="backward_tiles",
    )(slot_at, inv_root, far(weight), far(cotangent), *cots_here, far(tile_vals))

    halos = tied((scaled, pair_scaled, diag_scaled), (diag_grad,))
    aggregated = pl.pallas_call(
        functools.partial(forward_kernel, together=together),
        out_shape=narrow,
        in_specs=[smem, vmem] + [hbm] * 4,
        out_specs=vmem,
        scratch_shapes=[pltpu.VMEM((width, 3 * nodes + side), jnp.bfloat16)]
        + tile_scratch
        + [pltpu.SemaphoreType.DMA((3,))],
        compiler_params=params,
        cost_estimate=light,
        name="forward_tiles",
    )(slot_at, inv_root, *halos, far(tile_vals))

    relayed = lax.ppermute(diag_grad, "row", inward)
    (relayed,) = tied((relayed,), (aggregated,))
    joined = (pair_grad.astype(jnp.float32) + relayed.astype(jnp.float32)).astype(jnp.bfloat16)
    returned = lax.ppermute(joined, "row", pairs)
    input_grad = (own_grad + returned.astype(jnp.float32)) * inv_root

    agg_pieces = gather_pieces(aggregated, "col")
    weight_parts = jnp.stack(
        [lax.dynamic_slice_in_dim(weight_cols, (col ^ o) * width, width, 0) for o in offsets]
    )
    output = lax.dot_general(
        weight_parts.reshape(cols * width, width),
        jnp.concatenate(agg_pieces, axis=0),
        (((0,), (0,)), ((), ())),
        preferred_element_type=jnp.float32,
    ).astype(jnp.bfloat16)

    (late,) = tied((aggregated,), (joined,))
    outer = pl.pallas_call(
        outer_kernel,
        out_shape=jax.ShapeDtypeStruct((width, cols * width), jnp.float32),
        in_specs=[vmem] * (cols + 1),
        out_specs=vmem,
        compiler_params=pltpu.CompilerParams(vmem_limit_bytes=VMEM_BYTES // 4),
        cost_estimate=light,
        name="outer_product",
    )(*cots, late)
    row_bits = bits_of(rows) if rows & (rows - 1) == 0 else []
    if not row_bits:
        outer = lax.psum(outer, "row")
    for bit in row_bits[-2::-1]:
        outer = outer + lax.ppermute(outer, "row", xor_pairs(rows, bit))
    known = [0]
    blocks_of = {o: outer[:, k * width : (k + 1) * width] for k, o in enumerate(offsets)}
    for bit in reversed(bits_of(cols)):
        kept = [o for o in blocks_of if not o & bit]
        sent = jnp.stack([blocks_of[o | bit] for o in kept])
        (sent,) = tied((sent,), (agg_pieces[1], returned))
        other = lax.ppermute(sent, "col", xor_pairs(cols, bit))
        blocks_of = {o: jnp.concatenate([blocks_of[o], other[k]], axis=1) for k, o in enumerate(kept)}
        known = known + [o ^ bit for o in known]
    total = blocks_of[0]
    if row_bits:
        total = total + lax.ppermute(total, "row", pairs)
    place = jnp.asarray([known.index(o) for o in range(cols)], jnp.int32)
    weight_grad = jnp.concatenate(
        [
            lax.dynamic_slice_in_dim(total, place[col ^ c] * width, width, 1)
            for c in range(cols)
        ],
        axis=1,
    ) / math.sqrt(nodes * rows)
    return (output, input_grad, weight_grad.T)


def solution(mesh):
    placed = (
        P("col", "row"),
        P(),
        P("col", "row"),
        P("row"),
        P("row", None),
        P("row"),
        P("row", None, None, None),
    )
    return jax.shard_map(
        shards,
        mesh=mesh,
        in_specs=placed,
        out_specs=(P("col", "row"), P("col", "row"), P(None, "col")),
        check_vma=False,
    )
```

time: 122 us -> 70.8 us (0.58)
  waiting for transfers between devices: 67.9 us -> 21.7 us
  Pallas kernels: 21.6 us -> 16.5 us
  other arithmetic: 2.93 us -> 6.65 us
  local copies, waits for them, and re-layouts: 4.59 us -> 2.07 us
    ppermute x10 -> x9, waiting for transfers between devices: 57.3 us -> 13 us  [the longest x2 4.44 us: shards(): outer = outer + lax.ppermute(outer, 'row', xor_pairs(rows, bit))]
    pallas_call x2 -> x3, Pallas kernels: 21.6 us -> 16.5 us  [the longest x1 7.88 us: shards(): pl.pallas_call(functools.partial(backward_kernel, offsets=offsets, togeth...]
    ppermute x6, waiting for transfers between devices: 10.6 us -> 8.7 us  [gather_pieces(): lax.ppermute(piece, axis, xor_pairs(count, bit))]
    dynamic_update_slice x4 -> x0, local copies, waits for them, and re-layouts: 1.66 us -> none  [shards(): lax.dynamic_update_slice_in_dim(weight_grad, block, piece_of(offset), 0)]
    ppermute x10 -> x9, starting transfers between devices: 15.8 us -> 15.1 us  [the longest x2 5.62 us: shards(): outer = outer + lax.ppermute(outer, 'row', xor_pairs(rows, bit))]
    dot_general x5 -> x1, matrix products: 2.44 us -> 2.34 us  [shards(): lax.dot_general(weight_parts.reshape(cols * width, width), jnp.concatenat...]
  transfers between devices with their start and end apart: 16 -> 15, of which waited for: 11 -> 9; matrix products, arithmetic and copies ran while one was open for 4% -> 13% of each run, Pallas kernels for 0% -> 23%
where the time goes in v2:
time: 70.8 us; the launch traced here: 70.4 us
  waiting for transfers between devices  21.7 us (31%)
  starting transfers between devices  20.3 us (29%)
  Pallas kernels  16.5 us (23%)
  other arithmetic  6.65 us (9%)
  matrix products  2.34 us (3%)
  local copies, waits for them, and re-layouts  2.07 us (3%)
  between operations  0.84 us (1%)
    ppermute x6, waiting for transfers between devices, gather_pieces(): lax.ppermute(piece, axis, xor_pairs(count, bit))  8.7 us
    pallas_call x1, Pallas kernels, shards(): pl.pallas_call(functools.partial(backward_kernel, offsets=offsets, togeth...  7.88 us
    pallas_call x1, Pallas kernels, shards(): pl.pallas_call(functools.partial(forward_kernel, together=together), out_...  7.83 us
    ppermute x2, starting transfers between devices, shards(): outer = outer + lax.ppermute(outer, 'row', xor_pairs(rows, bit))  5.62 us
    ppermute x6, starting transfers between devices, gather_pieces(): lax.ppermute(piece, axis, xor_pairs(count, bit))  5.2 us
    ppermute x2, waiting for transfers between devices, shards(): outer = outer + lax.ppermute(outer, 'row', xor_pairs(rows, bit))  4.44 us
    ppermute x1, waiting for transfers between devices, shards(): relayed = lax.ppermute(diag_grad, 'row', inward)  3.73 us
    ppermute x1, starting transfers between devices, shards(): diag_scaled = lax.ppermute(pair_scaled, 'row', outward)  3.5 us
  transfers between devices with their start and end apart: 15, of which 9 were waited for; matrix products, arithmetic and copies ran while one was open for 13% of the time, Pallas kernels for 23%

profile of v2, /device:TPU:0, one launch (start us, length us, event | category | flops | bytes accessed | tf_op | source)
XLA Modules:
  0.0 70.4 jit_solution(13047783233935907946)
XLA Ops:
  0.6 3.0 %collective-permute-start.2 = (bf16[64,4096]{1,0:T(8,128)(2,1)}, bf16[64,4096]{1,0:T(8,128)(2,1)S(1)}, u32[]{:S(2)}, u32[]{:S(2)}) collective-permute-start(bf16[64,4096]{1,0:T(8,128)(2,1)} %refs_0_.3), channel_id=1, source_target_pairs={{0,2},{1,3},{2,0},{3,1},{4,6},{5,7},{6,4},{7,5},{8,10},{9,11},{10,... | collective-permute-start | bytes 1572872 | tf_op jit(solution)/shard_map/ppermute | solution.py:49
  3.6 0.7 %convert_rsqrt_fusion = f32[4096]{0:T(1024)S(1)} fusion(s32[4096]{0:T(1024)} %param.11), kind=kLoop, calls=%fused_computation.28 | loop fusion | flops 4096 | bytes 32768 | tf_op jit(solution)/shard_map/rsqrt | solution.py:191
  4.4 1.1 %multiply_convert_fusion.own = bf16[64,4096]{1,0:T(8,128)(2,1)S(1)} fusion(bf16[64,4096]{1,0:T(8,128)(2,1)} %param.8, f32[4096]{0:T(1024)S(1)} %convert_rsqrt_fusion), kind=kLoop, calls=%fused_computation.10 | loop fusion | flops 786432 | bytes 1064960 | tf_op jit(solution)/shard_map/convert_element_type | solution.py:192
  5.5 1.6 %collective-permute-start = (bf16[64,4096]{1,0:T(8,128)(2,1)S(1)}, bf16[64,4096]{1,0:T(8,128)(2,1)S(1)}, u32[]{:S(2)}, u32[]{:S(2)}) collective-permute-start(bf16[64,4096]{1,0:T(8,128)(2,1)S(1)} %multiply_convert_fusion.own), channel_id=1, source_target_pairs={{0,4},{4,0},{8,12},{12,8},{16,20},{20,16},{24,28},{28,24},{1,5},{5... | collective-permute-start | bytes 1572872 | tf_op jit(solution)/shard_map/ppermute | solution.py:193
  7.1 0.0 collective-permute-start.3
  7.1 8.7 %collective-permute-done.2.refs_1_ = bf16[64,4096]{1,0:T(8,128)(2,1)S(1)} collective-permute-done((bf16[64,4096]{1,0:T(8,128)(2,1)}, bf16[64,4096]{1,0:T(8,128)(2,1)S(1)}, u32[]{:S(2)}, u32[]{:S(2)}) %collective-permute-start.2) | collective-permute-done | bytes 524320 | tf_op jit(solution)/shard_map/ppermute | solution.py:49
  15.8 0.0 collective-permute-start.4
  15.8 0.8 %copy.11 = s32[32,10]{1,0:T(8,128)S(1)} copy(s32[32,10]{0,1:T(8,128)} %param.12) | data formatting | bytes 2560 | tf_op args[4]
  16.5 0.7 %fusion.9.slot_ref = s32[32,10]{1,0:T(8,128)S(1)} fusion(s32[32,10]{1,0:T(8,128)S(1)} %copy.11, s32[]{:T(128)S(6)} %xor.18, s32[]{:T(128)S(6)} %axis_index.25, s32[32]{0:T(128)} %param.13), kind=kLoop, calls=%fused_computation.27 | loop fusion | flops 8640 | bytes 2696 | tf_op jit(solution)/shard_map/jit(_where)/select_n | solution.py:200
  17.3 1.7 %collective-permute-done.pair = bf16[64,4096]{1,0:T(8,128)(2,1)S(1)} collective-permute-done((bf16[64,4096]{1,0:T(8,128)(2,1)S(1)}, bf16[64,4096]{1,0:T(8,128)(2,1)S(1)}, u32[]{:S(2)}, u32[]{:S(2)}) %collective-permute-start) | collective-permute-done | bytes 524320 | tf_op jit(solution)/shard_map/ppermute | solution.py:193
  18.9 3.5 %collective-permute-start.1 = (bf16[64,4096]{1,0:T(8,128)(2,1)S(1)}, bf16[64,4096]{1,0:T(8,128)(2,1)S(1)}, u32[]{:S(2)}, u32[]{:S(2)}) collective-permute-start(bf16[64,4096]{1,0:T(8,128)(2,1)S(1)} %collective-permute-done.pair), channel_id=1, source_target_pairs={{0,8},{8,16},{12,4},{16,24},{20,12},{28,20},{1,9},{9,17},{13,5},{1... | collective-permute-start | bytes 1572872 | tf_op jit(solution)/shard_map/ppermute | solution.py:194
  22.5 0.0 collective-permute-done.3.refs_2_
  22.5 0.0 collective-permute-done.4.refs_3_
  22.5 7.9 %backward_tiles.1 = (f32[64,4096]{1,0:T(8,128)S(1)}, bf16[64,4096]{1,0:T(8,128)(2,1)S(1)}, bf16[64,4096]{1,0:T(8,128)(2,1)S(1)}) custom-call(s32[32,10]{1,0:T(8,128)S(1)} %fusion.9.slot_ref, f32[1,4096]{1,0:T(1,128)S(1)} %bitcast.24, bf16[256,256]{1,0:T(8,128)(2,1)} %weight_hbm.1, bf16[64,4096]{1,0:T(8,128)(2,1)} %refs_0_.3, ...), custom_call_target="tpu_custom_call" | custom-call | flops 1 | bytes 1 | tf_op jit(solution)/shard_map/backward_tiles/pallas_call | solution.py:204
  30.4 0.0 copy-start.1
  30.4 1.0 %copy-done.1 = f32[64,4096]{1,0:T(8,128)} copy-done((f32[64,4096]{1,0:T(8,128)}, f32[64,4096]{1,0:T(8,128)S(1)}, u32[]{:S(2)}) %copy-start.1) | copy-done | bytes 1048600
  31.3 0.0 copy-start
  31.3 1.4 %collective-permute-start.8 = (bf16[64,4096]{1,0:T(8,128)(2,1)S(1)}, bf16[64,4096]{1,0:T(8,128)(2,1)S(1)}, u32[]{:S(2)}, u32[]{:S(2)}) collective-permute-start(bf16[64,4096]{1,0:T(8,128)(2,1)S(1)} %get-tuple-element.19), channel_id=1, source_target_pairs={{8,0},{16,8},{4,12},{24,16},{12,20},{20,28},{9,1},{17,9},{5,13},{2... | collective-permute-start | bytes 1572872 | tf_op jit(solution)/shard_map/ppermute | solution.py:236
  32.8 0.1 collective-permute-done.1.diag
  32.8 7.8 %forward_tiles.1.refs_4_ = bf16[64,4096]{1,0:T(8,128)(2,1)S(1)} custom-call(s32[32,10]{1,0:T(8,128)S(1)} %fusion.9.slot_ref, f32[1,4096]{1,0:T(1,128)S(1)} %bitcast.25, bf16[64,4096]{1,0:T(8,128)(2,1)S(1)} %multiply_convert_fusion.own, bf16[64,4096]{1,0:T(8,128)(2,1)S(1)} %collective-permute-done.pair, bf16[64,4096]{1,0:T(8,128)(2,1)S(1)} %collective-permute-done.1.diag, ...), custom_call_target="tpu_custom_call" | custom-call | flops 1 | bytes 1 | tf_op jit(solution)/shard_map/forward_tiles/pallas_call | solution.py:223
  40.7 0.0 copy-start.3
  40.7 0.0 copy-start.2
  40.7 1.5 %collective-permute-start.5 = (bf16[64,4096]{1,0:T(8,128)(2,1)S(1)}, bf16[64,4096]{1,0:T(8,128)(2,1)}, u32[]{:S(2)}, u32[]{:S(2)}) collective-permute-start(bf16[64,4096]{1,0:T(8,128)(2,1)S(1)} %forward_tiles.1.refs_4_), channel_id=1, source_target_pairs={{0,2},{1,3},{2,0},{3,1},{4,6},{5,7},{6,4},{7,5},{8,10},{9,11},{10,... | collective-permute-start | bytes 1572872 | tf_op jit(solution)/shard_map/ppermute | solution.py:49
  42.2 3.7 %collective-permute-done.8 = bf16[64,4096]{1,0:T(8,128)(2,1)S(1)} collective-permute-done((bf16[64,4096]{1,0:T(8,128)(2,1)S(1)}, bf16[64,4096]{1,0:T(8,128)(2,1)S(1)}, u32[]{:S(2)}, u32[]{:S(2)}) %collective-permute-start.8) | collective-permute-done | bytes 524320 | tf_op jit(solution)/shard_map/ppermute | solution.py:236
  46.0 0.9 %add_convert_fusion = bf16[64,4096]{1,0:T(8,128)(2,1)} fusion(bf16[64,4096]{1,0:T(8,128)(2,1)S(1)} %collective-permute-done.8, bf16[64,4096]{1,0:T(8,128)(2,1)S(1)} %get-tuple-element.24), kind=kLoop, calls=%fused_computation.9 | loop fusion | flops 1048576 | bytes 1572864 | tf_op jit(solution)/shard_map/convert_element_type | solution.py:238
  46.9 0.0 collective-permute-start.9
  46.9 0.0 copy-done
  46.9 0.7 %outer_product.1 = f32[64,256]{1,0:T(8,128)S(1)} custom-call(bf16[64,4096]{1,0:T(8,128)(2,1)S(1)} %copy-done, bf16[64,4096]{1,0:T(8,128)(2,1)S(1)} %collective-permute-done.2.refs_1_, bf16[64,4096]{1,0:T(8,128)(2,1)S(1)} %collective-permute-done.3.refs_2_, bf16[64,4096]{1,0:T(8,128)(2,1)S(1)} %collective-permute-done.4.refs_3_, ...), custom_call_target="tpu_custom_call" | custom-call | flops 1 | bytes 1 | tf_op jit(solution)/shard_map/outer_product/pallas_call | solution.py:254
  47.7 2.0 %collective-permute-start.10 = (f32[64,256]{1,0:T(8,128)S(1)}, f32[64,256]{1,0:T(8,128)S(1)}, u32[]{:S(2)}, u32[]{:S(2)}) collective-permute-start(f32[64,256]{1,0:T(8,128)S(1)} %outer_product.1), channel_id=1, source_target_pairs={{0,8},{4,12},{8,0},{12,4},{16,24},{20,28},{24,16},{28,20},{1,9},{5... | collective-permute-start | bytes 196616 | tf_op jit(solution)/shard_map/ppermute | solution.py:267
  49.7 2.3 %collective-permute-done.10 = f32[64,256]{1,0:T(8,128)S(1)} collective-permute-done((f32[64,256]{1,0:T(8,128)S(1)}, f32[64,256]{1,0:T(8,128)S(1)}, u32[]{:S(2)}, u32[]{:S(2)}) %collective-permute-start.10) | collective-permute-done | bytes 65568 | tf_op jit(solution)/shard_map/ppermute | solution.py:267
  52.0 3.6 %collective-permute-start.11 = (f32[64,256]{1,0:T(8,128)S(1)}, f32[64,256]{1,0:T(8,128)S(1)}, u32[]{:S(2)}, u32[]{:S(2)}) collective-permute-start(f32[64,256]{1,0:T(8,128)S(1)} %add.78), channel_id=1, source_target_pairs={{0,16},{4,20},{8,24},{12,28},{16,0},{20,4},{24,8},{28,12},{1,17},{... | collective-permute-start | bytes 196616 | tf_op jit(solution)/shard_map/ppermute | solution.py:267
  55.6 0.0 copy-done.3
  55.6 0.1 dynamic-slice_bitcast_fusion.3
  55.7 2.1 %collective-permute-done.11 = f32[64,256]{1,0:T(8,128)S(1)} collective-permute-done((f32[64,256]{1,0:T(8,128)S(1)}, f32[64,256]{1,0:T(8,128)S(1)}, u32[]{:S(2)}, u32[]{:S(2)}) %collective-permute-start.11) | collective-permute-done | bytes 65568 | tf_op jit(solution)/shard_map/ppermute | solution.py:267
  57.9 0.1 fusion.12
  58.0 0.0 collective-permute-done.5
  58.0 0.9 %collective-permute-done.9 = bf16[64,4096]{1,0:T(8,128)(2,1)} collective-permute-done((bf16[64,4096]{1,0:T(8,128)(2,1)}, bf16[64,4096]{1,0:T(8,128)(2,1)}, u32[]{:S(2)}, u32[]{:S(2)}) %collective-permute-start.9) | collective-permute-done | bytes 524320 | tf_op jit(solution)/shard_map/ppermute | solution.py:239
  58.9 0.0 collective-permute-start.12
  59.0 0.6 collective-permute-start.6
  59.6 0.1 collective-permute-start.7
  59.6 0.5 collective-permute-done.12
  60.2 0.1 maximum_bitcast_fusion
  60.3 2.6 %collective-permute-start.13 = (f32[1,64,128]{2,1,0:T(8,128)S(1)}, f32[1,64,128]{2,1,0:T(8,128)S(1)}, u32[]{:S(2)}, u32[]{:S(2)}) collective-permute-start(f32[1,64,128]{2,1,0:T(8,128)S(1)} %maximum_bitcast_fusion), channel_id=1, source_target_pairs={{0,2},{1,3},{2,0},{3,1},{4,6},{5,7},{6,4},{7,5},{8,10},{9,11},{10,... | collective-permute-start | bytes 98312 | tf_op jit(solution)/shard_map/ppermute | solution.py:274
  62.9 0.0 copy-done.2
  62.9 2.1 %add_multiply_fusion = f32[64,4096]{1,0:T(8,128)} fusion(f32[64,4096]{1,0:T(8,128)S(1)} %copy-done.2, bf16[64,4096]{1,0:T(8,128)(2,1)} %collective-permute-done.9, f32[4096]{0:T(1024)S(1)} %convert_rsqrt_fusion), kind=kLoop, calls=%fused_computation.8 | loop fusion | flops 786432 | bytes 2637824 | tf_op jit(solution)/shard_map/mul | solution.py:240
  65.0 0.0 collective-permute-done.13
  65.0 0.1 pad_maximum_fusion.2
  65.1 0.3 collective-permute-start.14
  65.4 0.0 collective-permute-done.6
  65.4 0.0 collective-permute-done.7
  65.4 2.3 %convolution_convert_fusion = bf16[64,4096]{1,0:T(8,128)(2,1)} fusion(bf16[256,64]{1,0:T(8,128)(2,1)S(1)} %bitcast.28, bf16[64,4096]{1,0:T(8,128)(2,1)S(1)} %collective-permute-done.7, bf16[64,4096]{1,0:T(8,128)(2,1)S(1)} %collective-permute-done.6, bf16[64,4096]{1,0:T(8,128)(2,1)} %collective-permute-done.5, bf16[64,4096]{1,0:T(8,128)(2,1)S(1)} %forward_tiles.1.refs_4_), kind=kOutput, calls=%fused_computation | convolution fusion | flops 142868480 | bytes 2654208 | tf_op jit(solution)/shard_map/dot_general | solution.py:246
  67.8 1.6 %collective-permute-done.14 = f32[64,256]{1,0:T(8,128)S(1)} collective-permute-done((f32[64,256]{1,0:T(8,128)S(1)}, f32[64,256]{1,0:T(8,128)S(1)}, u32[]{:S(2)}, u32[]{:S(2)}) %collective-permute-start.14) | collective-permute-done | bytes 65568 | tf_op jit(solution)/shard_map/ppermute | solution.py:279
  69.4 0.1 fusion.14
  69.5 0.1 constant_dynamic-slice_fusion.3
  69.6 0.7 %fusion.7 = f32[256,64]{0,1:T(8,128)} fusion(f32[64,64]{1,0:T(8,128)S(1)} %get-tuple-element.34, f32[64,64]{1,0:T(8,128)S(1)} %get-tuple-element.35, f32[64,64]{1,0:T(8,128)S(1)} %get-tuple-element.36, f32[64,64]{1,0:T(8,128)S(1)} %get-tuple-element.33), kind=kLoop, calls=%fused_computation.15 | loop fusion | flops 65536 | bytes 131072 | tf_op jit(solution)/shard_map/transpose | solution.py:288
  (5 shorter events, 0.1 us)
Async XLA Ops:
  0.6 15.1 %collective-permute-start.2 = (bf16[64,4096]{1,0:T(8,128)(2,1)}, bf16[64,4096]{1,0:T(8,128)(2,1)S(1)}, u32[]{:S(2)}, u32[]{:S(2)}) collective-permute-start(bf16[64,4096]{1,0:T(8,128)(2,1)} %refs_0_.3), channel_id=1, source_target_pairs={{0,2},{1,3},{2,0},{3,1},{4,6},{5,7},{6,4},{7,5},{8,10},{9,11},{10,... | collective-permute-start | bytes 1572872 | tf_op jit(solution)/shard_map/ppermute | solution.py:49
  5.5 13.4 %collective-permute-start = (bf16[64,4096]{1,0:T(8,128)(2,1)S(1)}, bf16[64,4096]{1,0:T(8,128)(2,1)S(1)}, u32[]{:S(2)}, u32[]{:S(2)}) collective-permute-start(bf16[64,4096]{1,0:T(8,128)(2,1)S(1)} %multiply_convert_fusion.own), channel_id=1, source_target_pairs={{0,4},{4,0},{8,12},{12,8},{16,20},{20,16},{24,28},{28,24},{1,5},{5... | collective-permute-start | bytes 1572872 | tf_op jit(solution)/shard_map/ppermute | solution.py:193
  7.1 15.4 %collective-permute-start.3 = (bf16[64,4096]{1,0:T(8,128)(2,1)}, bf16[64,4096]{1,0:T(8,128)(2,1)S(1)}, u32[]{:S(2)}, u32[]{:S(2)}) collective-permute-start(bf16[64,4096]{1,0:T(8,128)(2,1)} %refs_0_.3), channel_id=1, source_target_pairs={{0,1},{1,0},{2,3},{3,2},{4,5},{5,4},{6,7},{7,6},{8,9},{9,8},{10,11... | collective-permute-start | bytes 1572872 | tf_op jit(solution)/shard_map/ppermute | solution.py:49
  15.8 6.7 %collective-permute-start.4 = (bf16[64,4096]{1,0:T(8,128)(2,1)S(1)}, bf16[64,4096]{1,0:T(8,128)(2,1)S(1)}, u32[]{:S(2)}, u32[]{:S(2)}) collective-permute-start(bf16[64,4096]{1,0:T(8,128)(2,1)S(1)} %collective-permute-done.2.refs_1_), channel_id=1, source_target_pairs={{0,1},{1,0},{2,3},{3,2},{4,5},{5,4},{6,7},{7,6},{8,9},{9,8},{10,11... | collective-permute-start | bytes 1572872 | tf_op jit(solution)/shard_map/ppermute | solution.py:49
  18.9 13.9 %collective-permute-start.1 = (bf16[64,4096]{1,0:T(8,128)(2,1)S(1)}, bf16[64,4096]{1,0:T(8,128)(2,1)S(1)}, u32[]{:S(2)}, u32[]{:S(2)}) collective-permute-start(bf16[64,4096]{1,0:T(8,128)(2,1)S(1)} %collective-permute-done.pair), channel_id=1, source_target_pairs={{0,8},{8,16},{12,4},{16,24},{20,12},{28,20},{1,9},{9,17},{13,5},{1... | collective-permute-start | bytes 1572872 | tf_op jit(solution)/shard_map/ppermute | solution.py:194
  30.4 1.0 %copy-start.1 = (f32[64,4096]{1,0:T(8,128)}, f32[64,4096]{1,0:T(8,128)S(1)}, u32[]{:S(2)}) copy-start(f32[64,4096]{1,0:T(8,128)S(1)} %get-tuple-element.23) | copy-start | bytes 3145732
  31.3 15.6 %copy-start = (bf16[64,4096]{1,0:T(8,128)(2,1)S(1)}, bf16[64,4096]{1,0:T(8,128)(2,1)}, u32[]{:S(2)}) copy-start(bf16[64,4096]{1,0:T(8,128)(2,1)} %refs_0_.3) | copy-start | bytes 1572868
  31.3 14.6 %collective-permute-start.8 = (bf16[64,4096]{1,0:T(8,128)(2,1)S(1)}, bf16[64,4096]{1,0:T(8,128)(2,1)S(1)}, u32[]{:S(2)}, u32[]{:S(2)}) collective-permute-start(bf16[64,4096]{1,0:T(8,128)(2,1)S(1)} %get-tuple-element.19), channel_id=1, source_target_pairs={{8,0},{16,8},{4,12},{24,16},{12,20},{20,28},{9,1},{17,9},{5,13},{2... | collective-permute-start | bytes 1572872 | tf_op jit(solution)/shard_map/ppermute | solution.py:236
  40.7 14.9 %copy-start.3 = (bf16[256,256]{1,0:T(8,128)(2,1)S(1)}, bf16[256,256]{1,0:T(8,128)(2,1)}, u32[]{:S(2)}) copy-start(bf16[256,256]{1,0:T(8,128)(2,1)} %weight_hbm.1) | copy-start | bytes 393220
  40.7 22.2 %copy-start.2 = (f32[64,4096]{1,0:T(8,128)S(1)}, f32[64,4096]{1,0:T(8,128)}, u32[]{:S(2)}) copy-start(f32[64,4096]{1,0:T(8,128)} %copy-done.1) | copy-start | bytes 3145732
  40.7 17.3 %collective-permute-start.5 = (bf16[64,4096]{1,0:T(8,128)(2,1)S(1)}, bf16[64,4096]{1,0:T(8,128)(2,1)}, u32[]{:S(2)}, u32[]{:S(2)}) collective-permute-start(bf16[64,4096]{1,0:T(8,128)(2,1)S(1)} %forward_tiles.1.refs_4_), channel_id=1, source_target_pairs={{0,2},{1,3},{2,0},{3,1},{4,6},{5,7},{6,4},{7,5},{8,10},{9,11},{10,... | collective-permute-start | bytes 1572872 | tf_op jit(solution)/shard_map/ppermute | solution.py:49
  46.9 12.0 %collective-permute-start.9 = (bf16[64,4096]{1,0:T(8,128)(2,1)}, bf16[64,4096]{1,0:T(8,128)(2,1)}, u32[]{:S(2)}, u32[]{:S(2)}) collective-permute-start(bf16[64,4096]{1,0:T(8,128)(2,1)} %add_convert_fusion), channel_id=1, source_target_pairs={{0,4},{4,0},{8,12},{12,8},{16,20},{20,16},{24,28},{28,24},{1,5},{5... | collective-permute-start | bytes 1572872 | tf_op jit(solution)/shard_map/ppermute | solution.py:239
  47.7 4.3 %collective-permute-start.10 = (f32[64,256]{1,0:T(8,128)S(1)}, f32[64,256]{1,0:T(8,128)S(1)}, u32[]{:S(2)}, u32[]{:S(2)}) collective-permute-start(f32[64,256]{1,0:T(8,128)S(1)} %outer_product.1), channel_id=1, source_target_pairs={{0,8},{4,12},{8,0},{12,4},{16,24},{20,28},{24,16},{28,20},{1,9},{5... | collective-permute-start | bytes 196616 | tf_op jit(solution)/shard_map/ppermute | solution.py:267
  52.0 5.9 %collective-permute-start.11 = (f32[64,256]{1,0:T(8,128)S(1)}, f32[64,256]{1,0:T(8,128)S(1)}, u32[]{:S(2)}, u32[]{:S(2)}) collective-permute-start(f32[64,256]{1,0:T(8,128)S(1)} %add.78), channel_id=1, source_target_pairs={{0,16},{4,20},{8,24},{12,28},{16,0},{20,4},{24,8},{28,12},{1,17},{... | collective-permute-start | bytes 196616 | tf_op jit(solution)/shard_map/ppermute | solution.py:267
  58.9 1.3 %collective-permute-start.12 = (f32[2,64,64]{2,1,0:T(8,128)S(1)}, f32[2,64,64]{2,1,0:T(8,128)S(1)}, u32[]{:S(2)}, u32[]{:S(2)}) collective-permute-start(f32[2,64,64]{2,1,0:T(8,128)S(1)} %pad_maximum_fusion.1), channel_id=1, source_target_pairs={{0,1},{1,0},{2,3},{3,2},{4,5},{5,4},{6,7},{7,6},{8,9},{9,8},{10,11... | collective-permute-start | bytes 98312 | tf_op jit(solution)/shard_map/ppermute | solution.py:274
  59.0 6.5 %collective-permute-start.6 = (bf16[64,4096]{1,0:T(8,128)(2,1)S(1)}, bf16[64,4096]{1,0:T(8,128)(2,1)S(1)}, u32[]{:S(2)}, u32[]{:S(2)}) collective-permute-start(bf16[64,4096]{1,0:T(8,128)(2,1)S(1)} %forward_tiles.1.refs_4_), channel_id=1, source_target_pairs={{0,1},{1,0},{2,3},{3,2},{4,5},{5,4},{6,7},{7,6},{8,9},{9,8},{10,11... | collective-permute-start | bytes 1572872 | tf_op jit(solution)/shard_map/ppermute | solution.py:49
  59.6 5.9 %collective-permute-start.7 = (bf16[64,4096]{1,0:T(8,128)(2,1)}, bf16[64,4096]{1,0:T(8,128)(2,1)S(1)}, u32[]{:S(2)}, u32[]{:S(2)}) collective-permute-start(bf16[64,4096]{1,0:T(8,128)(2,1)} %collective-permute-done.5), channel_id=1, source_target_pairs={{0,1},{1,0},{2,3},{3,2},{4,5},{5,4},{6,7},{7,6},{8,9},{9,8},{10,11... | collective-permute-start | bytes 1572872 | tf_op jit(solution)/shard_map/ppermute | solution.py:49
  60.3 4.7 %collective-permute-start.13 = (f32[1,64,128]{2,1,0:T(8,128)S(1)}, f32[1,64,128]{2,1,0:T(8,128)S(1)}, u32[]{:S(2)}, u32[]{:S(2)}) collective-permute-start(f32[1,64,128]{2,1,0:T(8,128)S(1)} %maximum_bitcast_fusion), channel_id=1, source_target_pairs={{0,2},{1,3},{2,0},{3,1},{4,6},{5,7},{6,4},{7,5},{8,10},{9,11},{10,... | collective-permute-start | bytes 98312 | tf_op jit(solution)/shard_map/ppermute | solution.py:274
  65.1 4.3 %collective-permute-start.14 = (f32[64,256]{1,0:T(8,128)S(1)}, f32[64,256]{1,0:T(8,128)S(1)}, u32[]{:S(2)}, u32[]{:S(2)}) collective-permute-start(f32[64,256]{1,0:T(8,128)S(1)} %pad_maximum_fusion.2), channel_id=1, source_target_pairs={{0,4},{4,0},{8,12},{12,8},{16,20},{20,16},{24,28},{28,24},{1,5},{5... | collective-permute-start | bytes 196616 | tf_op jit(solution)/shard_map/ppermute | solution.py:279

commit v3 on v2

--- a/solution.py
+++ b/solution.py
@@ -66,8 +66,8 @@
     return [range(t, min(t + 2, slots)) for t in range(0, slots, 2)]
 
 
-def start_tiles(tiles_hbm, tiles, sems):
-    for b in range(tiles.shape[0]):
+def start_tiles(tiles_hbm, tiles, sems, first, last):
+    for b in range(first, last):
         pltpu.make_async_copy(tiles_hbm.at[b], tiles.at[b], sems.at[b]).start()
 
 
@@ -95,7 +95,7 @@
         arrivals.append(pltpu.make_async_copy(value, place, in_sems.at[k + 1]))
     for copy in arrivals:
         copy.start()
-    start_tiles(tiles_hbm, tiles, sems)
+    start_tiles(tiles_hbm, tiles, sems, 0, blocks)
     acc[...] = jnp.zeros_like(acc)
     for copy in arrivals:
         copy.wait()
@@ -134,10 +134,11 @@
     ]
     for copy in arrivals:
         copy.start()
-    start_tiles(tiles_hbm, tiles, sems)
+    start_tiles(tiles_hbm, tiles, sems, 0, together)
     window[:, 3 * nodes :] = jnp.zeros((width, side), window.dtype)
     for copy in arrivals:
         copy.wait()
+    start_tiles(tiles_hbm, tiles, sems, together, blocks)
 
     def block(b):
         places = [block_at(slot_ref[b, s], side) for s in range(slots)]
@@ -179,7 +180,7 @@
     light = pl.CostEstimate(flops=1, bytes_accessed=1, transcendentals=0)
     narrow = jax.ShapeDtypeStruct((width, nodes), jnp.bfloat16)
     full = jax.ShapeDtypeStruct((width, nodes), jnp.float32)
-    together = 2 if blocks % 2 == 0 else 1
+    together = math.gcd(blocks, 8)
     tile_scratch = [
         pltpu.VMEM(tile_vals.shape, tile_vals.dtype),
         pltpu.SemaphoreType.DMA((blocks,)),
@@ -192,12 +193,11 @@
     scaled = (features.astype(jnp.float32) * inv_root).astype(jnp.bfloat16)
     pair_scaled = lax.ppermute(scaled, "row", pairs)
     diag_scaled = lax.ppermute(pair_scaled, "row", outward)
-    cots = gather_pieces(cotangent, "col")
-
     source_row = tile_src // blocks
     group = jnp.where(source_row == row, 0, jnp.where(source_row == (row ^ 1), 1, 2))
     live = jnp.arange(slots, dtype=jnp.int32)[None, :] < tile_count[:, None]
     slot_at = jnp.where(live, group * blocks + tile_src % blocks, 3 * blocks)
+    cots = gather_pieces(cotangent, "col", (slot_at,))
     weight_cols = lax.dynamic_slice_in_dim(weight, col * width, width, 1)
 
     cots_here = tied(cots[1:], (pair_scaled,))
@@ -250,7 +250,6 @@
         preferred_element_type=jnp.float32,
     ).astype(jnp.bfloat16)
 
-    (late,) = tied((aggregated,), (joined,))
     outer = pl.pallas_call(
         outer_kernel,
         out_shape=jax.ShapeDtypeStruct((width, cols * width), jnp.float32),
@@ -259,24 +258,44 @@
         compiler_params=pltpu.CompilerParams(vmem_limit_bytes=VMEM_BYTES // 4),
         cost_estimate=light,
         name="outer_product",
-    )(*cots, late)
+    )(*cots, aggregated)
     row_bits = bits_of(rows) if rows & (rows - 1) == 0 else []
     if not row_bits:
         outer = lax.psum(outer, "row")
-    for bit in row_bits[-2::-1]:
-        outer = outer + lax.ppermute(outer, "row", xor_pairs(rows, bit))
+
+    def over_rows(value, bits, after):
+        for bit, others in zip(bits, after):
+            if others:
+                (value,) = tied((value,), others)
+            value = value + lax.ppermute(value, "row", xor_pairs(rows, bit))
+        return value
+
+    def over_chips(value, bits, others):
+        if others:
+            (value,) = tied((value,), others)
+        steps = [0]
+        for bit in bits:
+            steps += [step | bit for step in steps]
+        return value + sum(
+            lax.ppermute(value, "row", xor_pairs(rows, step)) for step in steps[1:]
+        ) if steps[1:] else value
+
     known = [0]
+    outer = over_rows(outer, row_bits[-1:], [()] * len(row_bits))
     blocks_of = {o: outer[:, k * width : (k + 1) * width] for k, o in enumerate(offsets)}
     for bit in reversed(bits_of(cols)):
         kept = [o for o in blocks_of if not o & bit]
-        sent = jnp.stack([blocks_of[o | bit] for o in kept])
-        (sent,) = tied((sent,), (agg_pieces[1], returned))
-        other = lax.ppermute(sent, "col", xor_pairs(cols, bit))
-        blocks_of = {o: jnp.concatenate([blocks_of[o], other[k]], axis=1) for k, o in enumerate(kept)}
+        both = jnp.stack([blocks_of[o] for o in kept] + [blocks_of[o | bit] for o in kept])
+        if 2 * bit == cols:
+            both = over_rows(both, row_bits[-2::-1], [(joined,)] + [()] * len(row_bits))
+            (both,) = tied((both,), (agg_pieces[1], returned))
+        other = lax.ppermute(both[len(kept) :], "col", xor_pairs(cols, bit))
+        blocks_of = {
+            o: jnp.concatenate([both[k], other[k]], axis=1) for k, o in enumerate(kept)
+        }
         known = known + [o ^ bit for o in known]
     total = blocks_of[0]
-    if row_bits:
-        total = total + lax.ppermute(total, "row", pairs)
+    pass
     place = jnp.asarray([known.index(o) for o in range(cols)], jnp.int32)
     weight_grad = jnp.concatenate(
         [

time: 70.8 us -> 67.2 us (0.949)
  Pallas kernels: 16.5 us -> 15.3 us
  matrix products: 2.34 us -> 1.31 us
  starting transfers between devices: 20.3 us -> 19.5 us
    ppermute x1, waiting for transfers between devices: 3.73 us -> 0.01 us  [shards(): relayed = lax.ppermute(diag_grad, 'row', inward)]
    ppermute x5, waiting for transfers between devices: 6.6 us -> 8.93 us  [the longest x3 7.95 us: over_rows(): value = value + lax.ppermute(value, 'row', xor_pairs(rows, bit))]
    ppermute x1, starting transfers between devices: 0.01 us -> 2.09 us  [shards(): returned = lax.ppermute(joined, 'row', pairs)]
    ppermute x5, starting transfers between devices: 8.59 us -> 6.78 us  [the longest x3 6.17 us: over_rows(): value = value + lax.ppermute(value, 'row', xor_pairs(rows, bit))]
    ppermute x1, waiting for transfers between devices: 1.67 us -> 3.28 us  [shards(): pair_scaled = lax.ppermute(scaled, 'row', pairs)]
    ppermute x6, waiting for transfers between devices: 8.7 us -> 7.19 us  [gather_pieces(): lax.ppermute(piece, axis, xor_pairs(count, bit))]
    ppermute x1, waiting for transfers between devices: 0.94 us -> 2.17 us  [shards(): returned = lax.ppermute(joined, 'row', pairs)]
    ppermute x6, starting transfers between devices: 5.2 us -> 4.11 us  [gather_pieces(): lax.ppermute(piece, axis, xor_pairs(count, bit))]
  transfers between devices with their start and end apart: 15 -> 15, of which waited for: 9 -> 8; matrix products, arithmetic and copies ran while one was open for 13% -> 11% of each run, Pallas kernels for 23% -> 23%
where the time goes in v3:
time: 67.2 us; the launch traced here: 66.8 us
  waiting for transfers between devices  22.1 us (33%)
  starting transfers between devices  19.5 us (29%)
  Pallas kernels  15.3 us (23%)
  other arithmetic  6.02 us (9%)
  local copies, waits for them, and re-layouts  1.78 us (3%)
  matrix products  1.31 us (2%)
  between operations  0.82 us (1%)
    ppermute x3, waiting for transfers between devices, over_rows(): value = value + lax.ppermute(value, 'row', xor_pairs(rows, bit))  7.95 us
    pallas_call x1, Pallas kernels, shards(): pl.pallas_call(functools.partial(backward_kernel, offsets=offsets, togeth...  7.47 us
    ppermute x6, waiting for transfers between devices, gather_pieces(): lax.ppermute(piece, axis, xor_pairs(count, bit))  7.19 us
    pallas_call x1, Pallas kernels, shards(): pl.pallas_call(functools.partial(forward_kernel, together=together), out_...  7.12 us
    ppermute x3, starting transfers between devices, over_rows(): value = value + lax.ppermute(value, 'row', xor_pairs(rows, bit))  6.17 us
    ppermute x6, starting transfers between devices, gather_pieces(): lax.ppermute(piece, axis, xor_pairs(count, bit))  4.11 us
    ppermute x1, starting transfers between devices, shards(): diag_scaled = lax.ppermute(pair_scaled, 'row', outward)  3.5 us
    ppermute x1, waiting for transfers between devices, shards(): pair_scaled = lax.ppermute(scaled, 'row', pairs)  3.28 us
  transfers between devices with their start and end apart: 15, of which 8 were waited for; matrix products, arithmetic and copies ran while one was open for 11% of the time, Pallas kernels for 23%

profile of v3, /device:TPU:0, one launch (start us, length us, event | category | flops | bytes accessed | tf_op | source)
XLA Modules:
  0.0 66.8 jit_solution(2009992342377409588)
XLA Ops:
  0.6 3.0 %collective-permute-start.2 = (bf16[64,4096]{1,0:T(8,128)(2,1)}, bf16[64,4096]{1,0:T(8,128)(2,1)S(1)}, u32[]{:S(2)}, u32[]{:S(2)}) collective-permute-start(bf16[64,4096]{1,0:T(8,128)(2,1)} %refs_0_.3), channel_id=1, source_target_pairs={{0,2},{1,3},{2,0},{3,1},{4,6},{5,7},{6,4},{7,5},{8,10},{9,11},{10,... | collective-permute-start | bytes 1572872 | tf_op jit(solution)/shard_map/ppermute | solution.py:49
  3.6 0.7 %convert_rsqrt_fusion = f32[4096]{0:T(1024)S(1)} fusion(s32[4096]{0:T(1024)} %param.11), kind=kLoop, calls=%fused_computation.42 | loop fusion | flops 4096 | bytes 32768 | tf_op jit(solution)/shard_map/rsqrt | solution.py:192
  4.4 1.1 %multiply_convert_fusion.own = bf16[64,4096]{1,0:T(8,128)(2,1)S(1)} fusion(bf16[64,4096]{1,0:T(8,128)(2,1)} %param.8, f32[4096]{0:T(1024)S(1)} %convert_rsqrt_fusion), kind=kLoop, calls=%fused_computation.10 | loop fusion | flops 786432 | bytes 1064960 | tf_op jit(solution)/shard_map/convert_element_type | solution.py:193
  5.5 1.6 %collective-permute-start = (bf16[64,4096]{1,0:T(8,128)(2,1)S(1)}, bf16[64,4096]{1,0:T(8,128)(2,1)}, u32[]{:S(2)}, u32[]{:S(2)}) collective-permute-start(bf16[64,4096]{1,0:T(8,128)(2,1)S(1)} %multiply_convert_fusion.own), channel_id=1, source_target_pairs={{0,4},{4,0},{8,12},{12,8},{16,20},{20,16},{24,28},{28,24},{1,5},{5... | collective-permute-start | bytes 1572872 | tf_op jit(solution)/shard_map/ppermute | solution.py:194
  7.1 0.0 collective-permute-start.3
  7.1 0.8 %copy.11 = s32[32,10]{1,0:T(8,128)S(1)} copy(s32[32,10]{0,1:T(8,128)} %param.12) | data formatting | bytes 2560 | tf_op args[4]
  7.9 0.7 %fusion.13.slot_ref = s32[32,10]{1,0:T(8,128)S(1)} fusion(s32[32,10]{1,0:T(8,128)S(1)} %copy.11, s32[]{:T(128)S(6)} %xor.18, s32[]{:T(128)S(6)} %axis_index.25, s32[32]{0:T(128)} %param.13), kind=kLoop, calls=%fused_computation.41 | loop fusion | flops 8640 | bytes 2696 | tf_op jit(solution)/shard_map/jit(_where)/select_n | solution.py:199
  8.6 7.2 %collective-permute-done.2.refs_1_ = bf16[64,4096]{1,0:T(8,128)(2,1)S(1)} collective-permute-done((bf16[64,4096]{1,0:T(8,128)(2,1)}, bf16[64,4096]{1,0:T(8,128)(2,1)S(1)}, u32[]{:S(2)}, u32[]{:S(2)}) %collective-permute-start.2) | collective-permute-done | bytes 524320 | tf_op jit(solution)/shard_map/ppermute | solution.py:49
  15.8 0.0 collective-permute-start.4
  15.8 3.3 %collective-permute-done.pair = bf16[64,4096]{1,0:T(8,128)(2,1)} collective-permute-done((bf16[64,4096]{1,0:T(8,128)(2,1)S(1)}, bf16[64,4096]{1,0:T(8,128)(2,1)}, u32[]{:S(2)}, u32[]{:S(2)}) %collective-permute-start) | collective-permute-done | bytes 524320 | tf_op jit(solution)/shard_map/ppermute | solution.py:194
  19.1 3.5 %collective-permute-start.1 = (bf16[64,4096]{1,0:T(8,128)(2,1)}, bf16[64,4096]{1,0:T(8,128)(2,1)S(1)}, u32[]{:S(2)}, u32[]{:S(2)}) collective-permute-start(bf16[64,4096]{1,0:T(8,128)(2,1)} %collective-permute-done.pair), channel_id=1, source_target_pairs={{0,8},{8,16},{12,4},{16,24},{20,12},{28,20},{1,9},{9,17},{13,5},{1... | collective-permute-start | bytes 1572872 | tf_op jit(solution)/shard_map/ppermute | solution.py:195
  22.6 0.0 collective-permute-done.3.refs_2_
  22.6 0.0 collective-permute-done.4.refs_3_
  22.6 7.5 %backward_tiles.1 = (f32[64,4096]{1,0:T(8,128)S(1)}, bf16[64,4096]{1,0:T(8,128)(2,1)S(1)}, bf16[64,4096]{1,0:T(8,128)(2,1)}) custom-call(s32[32,10]{1,0:T(8,128)S(1)} %fusion.13.slot_ref, f32[1,4096]{1,0:T(1,128)S(1)} %bitcast.28, bf16[256,256]{1,0:T(8,128)(2,1)} %weight_hbm.1, bf16[64,4096]{1,0:T(8,128)(2,1)} %refs_0_.3, ...), custom_call_target="tpu_custom_call" | custom-call | flops 1 | bytes 1 | tf_op jit(solution)/shard_map/backward_tiles/pallas_call | solution.py:204
  30.1 0.0 copy-start.1
  30.1 0.8 %copy-done.1 = bf16[64,4096]{1,0:T(8,128)(2,1)} copy-done((bf16[64,4096]{1,0:T(8,128)(2,1)}, bf16[64,4096]{1,0:T(8,128)(2,1)S(1)}, u32[]{:S(2)}) %copy-start.1) | copy-done | bytes 524312
  30.9 0.0 copy-start
  30.9 1.4 %collective-permute-start.8 = (bf16[64,4096]{1,0:T(8,128)(2,1)}, bf16[64,4096]{1,0:T(8,128)(2,1)}, u32[]{:S(2)}, u32[]{:S(2)}) collective-permute-start(bf16[64,4096]{1,0:T(8,128)(2,1)} %get-tuple-element.20), channel_id=1, source_target_pairs={{8,0},{16,8},{4,12},{24,16},{12,20},{20,28},{9,1},{17,9},{5,13},{2... | collective-permute-start | bytes 1572872 | tf_op jit(solution)/shard_map/ppermute | solution.py:236
  32.3 0.5 collective-permute-done.1.diag
  32.8 7.1 %forward_tiles.1.refs_4_ = bf16[64,4096]{1,0:T(8,128)(2,1)S(1)} custom-call(s32[32,10]{1,0:T(8,128)S(1)} %fusion.13.slot_ref, f32[1,4096]{1,0:T(1,128)S(1)} %bitcast.29, bf16[64,4096]{1,0:T(8,128)(2,1)S(1)} %multiply_convert_fusion.own, bf16[64,4096]{1,0:T(8,128)(2,1)} %collective-permute-done.pair, bf16[64,4096]{1,0:T(8,128)(2,1)S(1)} %collective-permute-done.1.diag, ...), custom_call_target="tpu_custom_call" | custom-call | flops 1 | bytes 1 | tf_op jit(solution)/shard_map/forward_tiles/pallas_call | solution.py:223
  39.9 0.0 copy-done
  40.0 0.0 copy-start.2
  40.0 0.8 %outer_product.1 = f32[64,256]{1,0:T(8,128)S(1)} custom-call(bf16[64,4096]{1,0:T(8,128)(2,1)S(1)} %copy-done, bf16[64,4096]{1,0:T(8,128)(2,1)S(1)} %collective-permute-done.2.refs_1_, bf16[64,4096]{1,0:T(8,128)(2,1)S(1)} %collective-permute-done.3.refs_2_, bf16[64,4096]{1,0:T(8,128)(2,1)S(1)} %collective-permute-done.4.refs_3_, ...), custom_call_target="tpu_custom_call" | custom-call | flops 1 | bytes 1 | tf_op jit(solution)/shard_map/outer_product/pallas_call | solution.py:253
  40.7 2.9 %collective-permute-start.10 = (f32[64,256]{1,0:T(8,128)S(1)}, f32[64,256]{1,0:T(8,128)S(1)}, u32[]{:S(2)}, u32[]{:S(2)}) collective-permute-start(f32[64,256]{1,0:T(8,128)S(1)} %outer_product.1), channel_id=1, source_target_pairs={{0,4},{4,0},{8,12},{12,8},{16,20},{20,16},{24,28},{28,24},{1,5},{5... | collective-permute-start | bytes 196616 | tf_op jit(solution)/shard_map/ppermute | solution.py:270
  43.6 0.5 collective-permute-start.5
  44.1 1.7 %collective-permute-done.10 = f32[64,256]{1,0:T(8,128)S(1)} collective-permute-done((f32[64,256]{1,0:T(8,128)S(1)}, f32[64,256]{1,0:T(8,128)S(1)}, u32[]{:S(2)}, u32[]{:S(2)}) %collective-permute-start.10) | collective-permute-done | bytes 65568 | tf_op jit(solution)/shard_map/ppermute | solution.py:270
  45.9 0.1 fusion.17
  46.0 0.1 collective-permute-start.11
  46.0 0.0 collective-permute-done.8
  46.1 1.3 %add_convert_fusion = bf16[64,4096]{1,0:T(8,128)(2,1)S(1)} fusion(bf16[64,4096]{1,0:T(8,128)(2,1)} %collective-permute-done.8, bf16[64,4096]{1,0:T(8,128)(2,1)} %copy-done.1), kind=kLoop, calls=%fused_computation.9 | loop fusion | flops 1048576 | bytes 1572864 | tf_op jit(solution)/shard_map/convert_element_type | solution.py:238
  47.4 2.1 %collective-permute-start.9 = (bf16[64,4096]{1,0:T(8,128)(2,1)S(1)}, bf16[64,4096]{1,0:T(8,128)(2,1)S(1)}, u32[]{:S(2)}, u32[]{:S(2)}) collective-permute-start(bf16[64,4096]{1,0:T(8,128)(2,1)S(1)} %add_convert_fusion), channel_id=1, source_target_pairs={{0,4},{4,0},{8,12},{12,8},{16,20},{20,16},{24,28},{28,24},{1,5},{5... | collective-permute-start | bytes 1572872 | tf_op jit(solution)/shard_map/ppermute | solution.py:239
  49.5 0.0 collective-permute-done.11
  49.5 0.1 maximum_bitcast_fusion
  49.6 1.1 %collective-permute-start.12 = (f32[2,64,128]{2,1,0:T(8,128)S(1)}, f32[2,64,128]{2,1,0:T(8,128)S(1)}, u32[]{:S(2)}, u32[]{:S(2)}) collective-permute-start(f32[2,64,128]{2,1,0:T(8,128)S(1)} %pad_maximum_fusion.2), channel_id=1, source_target_pairs={{0,8},{4,12},{8,0},{12,4},{16,24},{20,28},{24,16},{28,20},{1,9},{5... | collective-permute-start | bytes 196616 | tf_op jit(solution)/shard_map/ppermute | solution.py:270
  50.7 0.0 copy-done.2
  50.7 0.1 dynamic-slice_bitcast_fusion.3
  50.8 3.1 %collective-permute-done.12 = f32[2,64,128]{2,1,0:T(8,128)S(1)} collective-permute-done((f32[2,64,128]{2,1,0:T(8,128)S(1)}, f32[2,64,128]{2,1,0:T(8,128)S(1)}, u32[]{:S(2)}, u32[]{:S(2)}) %collective-permute-start.12) | collective-permute-done | bytes 65568 | tf_op jit(solution)/shard_map/ppermute | solution.py:270
  53.9 2.2 %collective-permute-start.13 = (f32[2,64,128]{2,1,0:T(8,128)S(1)}, f32[2,64,128]{2,1,0:T(8,128)S(1)}, u32[]{:S(2)}, u32[]{:S(2)}) collective-permute-start(f32[2,64,128]{2,1,0:T(8,128)S(1)} %add.79), channel_id=1, source_target_pairs={{0,16},{4,20},{8,24},{12,28},{16,0},{20,4},{24,8},{28,12},{1,17},{... | collective-permute-start | bytes 196616 | tf_op jit(solution)/shard_map/ppermute | solution.py:270
  56.1 0.1 collective-permute-start.6
  56.2 0.0 collective-permute-done.5
  56.2 0.5 collective-permute-start.7
  56.7 3.2 %collective-permute-done.13 = f32[2,64,128]{2,1,0:T(8,128)S(1)} collective-permute-done((f32[2,64,128]{2,1,0:T(8,128)S(1)}, f32[2,64,128]{2,1,0:T(8,128)S(1)}, u32[]{:S(2)}, u32[]{:S(2)}) %collective-permute-start.13) | collective-permute-done | bytes 65568 | tf_op jit(solution)/shard_map/ppermute | solution.py:270
  59.9 2.2 %collective-permute-done.9 = bf16[64,4096]{1,0:T(8,128)(2,1)S(1)} collective-permute-done((bf16[64,4096]{1,0:T(8,128)(2,1)S(1)}, bf16[64,4096]{1,0:T(8,128)(2,1)S(1)}, u32[]{:S(2)}, u32[]{:S(2)}) %collective-permute-start.9) | collective-permute-done | bytes 524320 | tf_op jit(solution)/shard_map/ppermute | solution.py:239
  62.0 0.5 collective-permute-start.14
  62.6 1.1 %add_multiply_fusion = f32[64,4096]{1,0:T(8,128)} fusion(f32[64,4096]{1,0:T(8,128)S(1)} %get-tuple-element.24, bf16[64,4096]{1,0:T(8,128)(2,1)S(1)} %collective-permute-done.9, f32[4096]{0:T(1024)S(1)} %convert_rsqrt_fusion), kind=kLoop, calls=%fused_computation.8 | loop fusion | flops 786432 | bytes 2637824 | tf_op jit(solution)/shard_map/mul | solution.py:240
  63.7 0.0 collective-permute-done.6
  63.7 0.0 collective-permute-done.7
  63.7 1.3 %convolution_convert_fusion = bf16[64,4096]{1,0:T(8,128)(2,1)} fusion(bf16[256,64]{1,0:T(8,128)(2,1)S(1)} %bitcast.30, bf16[64,4096]{1,0:T(8,128)(2,1)S(1)} %collective-permute-done.7, bf16[64,4096]{1,0:T(8,128)(2,1)S(1)} %collective-permute-done.6, bf16[64,4096]{1,0:T(8,128)(2,1)S(1)} %collective-permute-done.5, bf16[64,4096]{1,0:T(8,128)(2,1)S(1)} %forward_tiles.1.refs_4_), kind=kOutput, calls=%fused_computation | convolution fusion | flops 142868480 | bytes 2654208 | tf_op jit(solution)/shard_map/dot_general | solution.py:246
  65.0 1.0 %collective-permute-done.14 = f32[1,64,128]{2,1,0:T(8,128)S(1)} collective-permute-done((f32[1,64,128]{2,1,0:T(8,128)S(1)}, f32[1,64,128]{2,1,0:T(8,128)S(1)}, u32[]{:S(2)}, u32[]{:S(2)}) %collective-permute-start.14) | collective-permute-done | bytes 32800 | tf_op jit(solution)/shard_map/ppermute | solution.py:292
  66.0 0.1 fusion.9
  66.1 0.7 %fusion.7 = f32[256,64]{0,1:T(8,128)} fusion(f32[64,64]{1,0:T(8,128)S(1)} %get-tuple-element.36, f32[64,64]{1,0:T(8,128)S(1)} %get-tuple-element.35, f32[64,64]{1,0:T(8,128)S(1)} %get-tuple-element.34, f32[64,64]{1,0:T(8,128)S(1)} %get-tuple-element.33), kind=kLoop, calls=%fused_computation.23 | loop fusion | flops 65536 | bytes 131072 | tf_op jit(solution)/shard_map/transpose | solution.py:307
  (8 shorter events, 0.1 us)
Async XLA Ops:
  0.6 15.1 %collective-permute-start.2 = (bf16[64,4096]{1,0:T(8,128)(2,1)}, bf16[64,4096]{1,0:T(8,128)(2,1)S(1)}, u32[]{:S(2)}, u32[]{:S(2)}) collective-permute-start(bf16[64,4096]{1,0:T(8,128)(2,1)} %refs_0_.3), channel_id=1, source_target_pairs={{0,2},{1,3},{2,0},{3,1},{4,6},{5,7},{6,4},{7,5},{8,10},{9,11},{10,... | collective-permute-start | bytes 1572872 | tf_op jit(solution)/shard_map/ppermute | solution.py:49
  5.5 13.6 %collective-permute-start = (bf16[64,4096]{1,0:T(8,128)(2,1)S(1)}, bf16[64,4096]{1,0:T(8,128)(2,1)}, u32[]{:S(2)}, u32[]{:S(2)}) collective-permute-start(bf16[64,4096]{1,0:T(8,128)(2,1)S(1)} %multiply_convert_fusion.own), channel_id=1, source_target_pairs={{0,4},{4,0},{8,12},{12,8},{16,20},{20,16},{24,28},{28,24},{1,5},{5... | collective-permute-start | bytes 1572872 | tf_op jit(solution)/shard_map/ppermute | solution.py:194
  7.1 15.5 %collective-permute-start.3 = (bf16[64,4096]{1,0:T(8,128)(2,1)}, bf16[64,4096]{1,0:T(8,128)(2,1)S(1)}, u32[]{:S(2)}, u32[]{:S(2)}) collective-permute-start(bf16[64,4096]{1,0:T(8,128)(2,1)} %refs_0_.3), channel_id=1, source_target_pairs={{0,1},{1,0},{2,3},{3,2},{4,5},{5,4},{6,7},{7,6},{8,9},{9,8},{10,11... | collective-permute-start | bytes 1572872 | tf_op jit(solution)/shard_map/ppermute | solution.py:49
  15.8 6.8 %collective-permute-start.4 = (bf16[64,4096]{1,0:T(8,128)(2,1)S(1)}, bf16[64,4096]{1,0:T(8,128)(2,1)S(1)}, u32[]{:S(2)}, u32[]{:S(2)}) collective-permute-start(bf16[64,4096]{1,0:T(8,128)(2,1)S(1)} %collective-permute-done.2.refs_1_), channel_id=1, source_target_pairs={{0,1},{1,0},{2,3},{3,2},{4,5},{5,4},{6,7},{7,6},{8,9},{9,8},{10,11... | collective-permute-start | bytes 1572872 | tf_op jit(solution)/shard_map/ppermute | solution.py:49
  19.1 13.8 %collective-permute-start.1 = (bf16[64,4096]{1,0:T(8,128)(2,1)}, bf16[64,4096]{1,0:T(8,128)(2,1)S(1)}, u32[]{:S(2)}, u32[]{:S(2)}) collective-permute-start(bf16[64,4096]{1,0:T(8,128)(2,1)} %collective-permute-done.pair), channel_id=1, source_target_pairs={{0,8},{8,16},{12,4},{16,24},{20,12},{28,20},{1,9},{9,17},{13,5},{1... | collective-permute-start | bytes 1572872 | tf_op jit(solution)/shard_map/ppermute | solution.py:195
  30.1 0.8 %copy-start.1 = (bf16[64,4096]{1,0:T(8,128)(2,1)}, bf16[64,4096]{1,0:T(8,128)(2,1)S(1)}, u32[]{:S(2)}) copy-start(bf16[64,4096]{1,0:T(8,128)(2,1)S(1)} %get-tuple-element.25) | copy-start | bytes 1572868
  30.9 9.1 %copy-start = (bf16[64,4096]{1,0:T(8,128)(2,1)S(1)}, bf16[64,4096]{1,0:T(8,128)(2,1)}, u32[]{:S(2)}) copy-start(bf16[64,4096]{1,0:T(8,128)(2,1)} %refs_0_.3) | copy-start | bytes 1572868
  30.9 15.2 %collective-permute-start.8 = (bf16[64,4096]{1,0:T(8,128)(2,1)}, bf16[64,4096]{1,0:T(8,128)(2,1)}, u32[]{:S(2)}, u32[]{:S(2)}) collective-permute-start(bf16[64,4096]{1,0:T(8,128)(2,1)} %get-tuple-element.20), channel_id=1, source_target_pairs={{8,0},{16,8},{4,12},{24,16},{12,20},{20,28},{9,1},{17,9},{5,13},{2... | collective-permute-start | bytes 1572872 | tf_op jit(solution)/shard_map/ppermute | solution.py:236
  40.0 10.8 %copy-start.2 = (bf16[256,256]{1,0:T(8,128)(2,1)S(1)}, bf16[256,256]{1,0:T(8,128)(2,1)}, u32[]{:S(2)}) copy-start(bf16[256,256]{1,0:T(8,128)(2,1)} %weight_hbm.1) | copy-start | bytes 393220
  40.7 5.1 %collective-permute-start.10 = (f32[64,256]{1,0:T(8,128)S(1)}, f32[64,256]{1,0:T(8,128)S(1)}, u32[]{:S(2)}, u32[]{:S(2)}) collective-permute-start(f32[64,256]{1,0:T(8,128)S(1)} %outer_product.1), channel_id=1, source_target_pairs={{0,4},{4,0},{8,12},{12,8},{16,20},{20,16},{24,28},{28,24},{1,5},{5... | collective-permute-start | bytes 196616 | tf_op jit(solution)/shard_map/ppermute | solution.py:270
  43.6 12.6 %collective-permute-start.5 = (bf16[64,4096]{1,0:T(8,128)(2,1)S(1)}, bf16[64,4096]{1,0:T(8,128)(2,1)S(1)}, u32[]{:S(2)}, u32[]{:S(2)}) collective-permute-start(bf16[64,4096]{1,0:T(8,128)(2,1)S(1)} %forward_tiles.1.refs_4_), channel_id=1, source_target_pairs={{0,2},{1,3},{2,0},{3,1},{4,6},{5,7},{6,4},{7,5},{8,10},{9,11},{10,... | collective-permute-start | bytes 1572872 | tf_op jit(solution)/shard_map/ppermute | solution.py:49
  46.0 3.5 %collective-permute-start.11 = (f32[2,64,64]{2,1,0:T(8,128)S(1)}, f32[2,64,64]{2,1,0:T(8,128)S(1)}, u32[]{:S(2)}, u32[]{:S(2)}) collective-permute-start(f32[2,64,64]{2,1,0:T(8,128)S(1)} %pad_maximum_fusion.1), channel_id=1, source_target_pairs={{0,1},{1,0},{2,3},{3,2},{4,5},{5,4},{6,7},{7,6},{8,9},{9,8},{10,11... | collective-permute-start | bytes 98312 | tf_op jit(solution)/shard_map/ppermute | solution.py:292
  47.4 14.7 %collective-permute-start.9 = (bf16[64,4096]{1,0:T(8,128)(2,1)S(1)}, bf16[64,4096]{1,0:T(8,128)(2,1)S(1)}, u32[]{:S(2)}, u32[]{:S(2)}) collective-permute-start(bf16[64,4096]{1,0:T(8,128)(2,1)S(1)} %add_convert_fusion), channel_id=1, source_target_pairs={{0,4},{4,0},{8,12},{12,8},{16,20},{20,16},{24,28},{28,24},{1,5},{5... | collective-permute-start | bytes 1572872 | tf_op jit(solution)/shard_map/ppermute | solution.py:239
  49.6 4.3 %collective-permute-start.12 = (f32[2,64,128]{2,1,0:T(8,128)S(1)}, f32[2,64,128]{2,1,0:T(8,128)S(1)}, u32[]{:S(2)}, u32[]{:S(2)}) collective-permute-start(f32[2,64,128]{2,1,0:T(8,128)S(1)} %pad_maximum_fusion.2), channel_id=1, source_target_pairs={{0,8},{4,12},{8,0},{12,4},{16,24},{20,28},{24,16},{28,20},{1,9},{5... | collective-permute-start | bytes 196616 | tf_op jit(solution)/shard_map/ppermute | solution.py:270
  53.9 5.9 %collective-permute-start.13 = (f32[2,64,128]{2,1,0:T(8,128)S(1)}, f32[2,64,128]{2,1,0:T(8,128)S(1)}, u32[]{:S(2)}, u32[]{:S(2)}) collective-permute-start(f32[2,64,128]{2,1,0:T(8,128)S(1)} %add.79), channel_id=1, source_target_pairs={{0,16},{4,20},{8,24},{12,28},{16,0},{20,4},{24,8},{28,12},{1,17},{... | collective-permute-start | bytes 196616 | tf_op jit(solution)/shard_map/ppermute | solution.py:270
  56.1 7.6 %collective-permute-start.6 = (bf16[64,4096]{1,0:T(8,128)(2,1)S(1)}, bf16[64,4096]{1,0:T(8,128)(2,1)S(1)}, u32[]{:S(2)}, u32[]{:S(2)}) collective-permute-start(bf16[64,4096]{1,0:T(8,128)(2,1)S(1)} %forward_tiles.1.refs_4_), channel_id=1, source_target_pairs={{0,1},{1,0},{2,3},{3,2},{4,5},{5,4},{6,7},{7,6},{8,9},{9,8},{10,11... | collective-permute-start | bytes 1572872 | tf_op jit(solution)/shard_map/ppermute | solution.py:49
  56.2 7.5 %collective-permute-start.7 = (bf16[64,4096]{1,0:T(8,128)(2,1)S(1)}, bf16[64,4096]{1,0:T(8,128)(2,1)S(1)}, u32[]{:S(2)}, u32[]{:S(2)}) collective-permute-start(bf16[64,4096]{1,0:T(8,128)(2,1)S(1)} %collective-permute-done.5), channel_id=1, source_target_pairs={{0,1},{1,0},{2,3},{3,2},{4,5},{5,4},{6,7},{7,6},{8,9},{9,8},{10,11... | collective-permute-start | bytes 1572872 | tf_op jit(solution)/shard_map/ppermute | solution.py:49
  62.0 3.9 %collective-permute-start.14 = (f32[1,64,128]{2,1,0:T(8,128)S(1)}, f32[1,64,128]{2,1,0:T(8,128)S(1)}, u32[]{:S(2)}, u32[]{:S(2)}) collective-permute-start(f32[1,64,128]{2,1,0:T(8,128)S(1)} %get-tuple-element.37), channel_id=1, source_target_pairs={{0,2},{1,3},{2,0},{3,1},{4,6},{5,7},{6,4},{7,5},{8,10},{9,11},{10,... | collective-permute-start | bytes 98312 | tf_op jit(solution)/shard_map/ppermute | solution.py:292

commit v4 on v3

--- a/solution.py
+++ b/solution.py
@@ -71,21 +71,42 @@
         pltpu.make_async_copy(tiles_hbm.at[b], tiles.at[b], sems.at[b]).start()
 
 
-def each_block(block, tiles_hbm, tiles, sems, together):
+def each_block(block, tiles_hbm, tiles, sems, together, before=None):
+    side = tiles.shape[2]
+
     def step(i, carry):
+        given = before(i * together) if before else None
         for k in range(together):
             b = i * together + k
             pltpu.make_async_copy(tiles_hbm.at[b], tiles.at[b], sems.at[b]).wait()
         for k in range(together):
-            block(i * together + k)
+            if before:
+                block(i * together + k, given[:, k * side : (k + 1) * side])
+            else:
+                block(i * together + k)
         return carry
 
     lax.fori_loop(0, tiles.shape[0] // together, step, 0)
+
+
+def scale_kernel(degree_hbm, features_hbm, scaled, inv, degree, features, sems):
+    width = scaled.shape[0]
+    halves = [slice(0, width // 2), slice(width // 2, width)]
+    copies = [pltpu.make_async_copy(degree_hbm, degree, sems.at[0])]
+    for k, half in enumerate(halves):
+        copies.append(pltpu.make_async_copy(features_hbm.at[half], features.at[half], sems.at[k + 1]))
+    for copy in copies:
+        copy.start()
+    copies[0].wait()
+    inv[...] = lax.rsqrt(degree[...].astype(jnp.float32))
+    for copy, half in zip(copies[1:], halves):
+        copy.wait()
+        scaled[half, :] = (features[half, :].astype(jnp.float32) * inv[...]).astype(scaled.dtype)
 
 
 def backward_kernel(slot_ref, inv, weight_hbm, *refs, offsets, together):
     cots, refs = refs[: len(offsets)], refs[len(offsets) :]
-    tiles_hbm, own_grad, pair_grad, diag_grad, acc, cot, scaled, weight, tiles, sems, in_sems = refs
+    tiles_hbm, own_grad, pair_grad, diag_grad, acc, cot, weight, near, tiles, sems, in_sems, out_sems = refs
     blocks, slots, side, _ = tiles.shape
     width, nodes = own_grad.shape
     col = lax.axis_index("col")
@@ -99,19 +120,13 @@
     acc[...] = jnp.zeros_like(acc)
     for copy in arrivals:
         copy.wait()
-    wide = 4 * side
-
-    def mix(i, carry):
-        here = pl.ds(pl.multiple_of(i * wide, wide), wide)
+    def mixed(first):
+        here = pl.ds(pl.multiple_of(first * side, together * side), together * side)
         grad = jnp.dot(weight[...], cot[:, here], preferred_element_type=jnp.float32)
-        scaled[:, here] = (grad * inv[:, here]).astype(scaled.dtype)
-        return carry
-
-    lax.fori_loop(0, nodes // wide, mix, 0)
-
-    def block(b):
+        return (grad * inv[:, here]).astype(cot.dtype)
+
+    def block(b, grad):
         places = [block_at(slot_ref[b, s], side) for s in range(slots)]
-        grad = scaled[:, block_at(b, side)]
         sums = [acc[:, place] for place in places]
         for group in slot_groups(slots):
             edges = jnp.concatenate([tiles[b, s] for s in group], axis=1)
@@ -119,10 +134,15 @@
             for k, s in enumerate(group):
                 acc[:, places[s]] = sums[s] + spread[:, k * side : (k + 1) * side]
 
-    each_block(block, tiles_hbm, tiles, sems, together)
+    each_block(block, tiles_hbm, tiles, sems, together, mixed)
+    own_copy = pltpu.make_async_copy(acc.at[:, :nodes], own_grad, out_sems.at[0])
+    own_copy.start()
+    near[...] = acc[:, nodes : 2 * nodes].astype(near.dtype)
+    near_copy = pltpu.make_async_copy(near, pair_grad, out_sems.at[1])
+    near_copy.start()
     diag_grad[...] = acc[:, 2 * nodes : 3 * nodes].astype(diag_grad.dtype)
-    pair_grad[...] = acc[:, nodes : 2 * nodes].astype(pair_grad.dtype)
-    own_grad[...] = acc[:, :nodes]
+    own_copy.wait()
+    near_copy.wait()
 
 
 def forward_kernel(slot_ref, inv, own, pair, diag, tiles_hbm, agg, window, tiles, sems, in_sems, *, together):
@@ -189,8 +209,20 @@
     outward = across(rows, 2)
     inward = [(target, source) for source, target in outward]
 
-    inv_root = lax.rsqrt(degree.astype(jnp.float32))[None, :]
-    scaled = (features.astype(jnp.float32) * inv_root).astype(jnp.bfloat16)
+    scaled, inv_root = pl.pallas_call(
+        scale_kernel,
+        out_shape=(narrow, jax.ShapeDtypeStruct((1, nodes), jnp.float32)),
+        in_specs=[hbm, hbm],
+        out_specs=(vmem, vmem),
+        scratch_shapes=[
+            pltpu.VMEM((1, nodes), degree.dtype),
+            pltpu.VMEM((width, nodes), features.dtype),
+            pltpu.SemaphoreType.DMA((3,)),
+        ],
+        compiler_params=pltpu.CompilerParams(vmem_limit_bytes=VMEM_BYTES // 8),
+        cost_estimate=light,
+        name="scale",
+    )(far(degree[None, :]), far(features))
     pair_scaled = lax.ppermute(scaled, "row", pairs)
     diag_scaled = lax.ppermute(pair_scaled, "row", outward)
     source_row = tile_src // blocks
@@ -203,17 +235,21 @@
     cots_here = tied(cots[1:], (pair_scaled,))
     own_grad, pair_grad, diag_grad = pl.pallas_call(
         functools.partial(backward_kernel, offsets=offsets, together=together),
-        out_shape=(full, narrow, narrow),
+        out_shape=(
+            pltpu.HBM(full.shape, full.dtype),
+            pltpu.HBM(narrow.shape, narrow.dtype),
+            narrow,
+        ),
         in_specs=[smem, vmem] + [hbm] * (cols + 2),
-        out_specs=(vmem,) * 3,
+        out_specs=(hbm, hbm, vmem),
         scratch_shapes=[
             pltpu.VMEM((width, 3 * nodes + side), jnp.float32),
             pltpu.VMEM((width * cols, nodes), jnp.bfloat16),
+            pltpu.VMEM((width, width * cols), jnp.bfloat16),
             pltpu.VMEM((width, nodes), jnp.bfloat16),
-            pltpu.VMEM((width, width * cols), jnp.bfloat16),
         ]
         + tile_scratch
-        + [pltpu.SemaphoreType.DMA((cols + 1,))],
+        + [pltpu.SemaphoreType.DMA((cols + 1,)), pltpu.SemaphoreType.DMA((2,))],
         compiler_params=params,
         cost_estimate=light,
         name="backward_tiles",
@@ -269,16 +305,6 @@
                 (value,) = tied((value,), others)
             value = value + lax.ppermute(value, "row", xor_pairs(rows, bit))
         return value
-
-    def over_chips(value, bits, others):
-        if others:
-            (value,) = tied((value,), others)
-        steps = [0]
-        for bit in bits:
-            steps += [step | bit for step in steps]
-        return value + sum(
-            lax.ppermute(value, "row", xor_pairs(rows, step)) for step in steps[1:]
-        ) if steps[1:] else value
 
     known = [0]
     outer = over_rows(outer, row_bits[-1:], [()] * len(row_bits))
@@ -295,7 +321,6 @@
         }
         known = known + [o ^ bit for o in known]
     total = blocks_of[0]
-    pass
     place = jnp.asarray([known.index(o) for o in range(cols)], jnp.int32)
     weight_grad = jnp.concatenate(
         [

time: 67.2 us -> 65.6 us (0.976)
  other arithmetic: 6.02 us -> 4.16 us
  waiting for transfers between devices: 22.1 us -> 20.6 us
  starting transfers between devices: 19.5 us -> 20.9 us
  Pallas kernels: 15.3 us -> 16.5 us
  local copies, waits for them, and re-layouts: 1.78 us -> 1.01 us
    ppermute x3, waiting for transfers between devices: 7.95 us -> 6.02 us  [over_rows(): value = value + lax.ppermute(value, 'row', xor_pairs(rows, bit))]
    convert_element_type x1 -> x0, other arithmetic: 1.13 us -> none  [shards(): scaled = (features.astype(jnp.float32) * inv_root).astype(jnp.bfloat16)]
    pallas_call x0 -> x1, Pallas kernels: none -> 1.12 us  [shards(): pl.pallas_call(scale_kernel, out_shape=(narrow, jax.ShapeDtypeStruct((1,...]
    ppermute x1, waiting for transfers between devices: 3.28 us -> 2.43 us  [shards(): pair_scaled = lax.ppermute(scaled, 'row', pairs)]
    unnamed x7, local copies, waits for them, and re-layouts: 1.57 us -> 0.79 us
    ppermute x6, waiting for transfers between devices: 7.19 us -> 7.93 us  [gather_pieces(): lax.ppermute(piece, axis, xor_pairs(count, bit))]
    rsqrt x1 -> x0, other arithmetic: 0.72 us -> none  [shards(): inv_root = lax.rsqrt(degree.astype(jnp.float32))[None, :]]
    ppermute x1, waiting for transfers between devices: 2.17 us -> 2.87 us  [shards(): returned = lax.ppermute(joined, 'row', pairs)]
  transfers between devices with their start and end apart: 15 -> 15, of which waited for: 8 -> 8; matrix products, arithmetic and copies ran while one was open for 11% -> 9% of each run, Pallas kernels for 23% -> 25%
where the time goes in v4:
time: 65.6 us; the launch traced here: 65.3 us
  starting transfers between devices  20.9 us (32%)
  waiting for transfers between devices  20.6 us (31%)
  Pallas kernels  16.5 us (25%)
  other arithmetic  4.16 us (6%)
  matrix products  1.31 us (2%)
  local copies, waits for them, and re-layouts  1.01 us (2%)
  between operations  0.82 us (1%)
    ppermute x6, waiting for transfers between devices, gather_pieces(): lax.ppermute(piece, axis, xor_pairs(count, bit))  7.93 us
    pallas_call x1, Pallas kernels, shards(): pl.pallas_call(functools.partial(backward_kernel, offsets=offsets, togeth...  7.65 us
    pallas_call x1, Pallas kernels, shards(): pl.pallas_call(functools.partial(forward_kernel, together=together), out_...  6.97 us
    ppermute x3, starting transfers between devices, over_rows(): value = value + lax.ppermute(value, 'row', xor_pairs(rows, bit))  6.66 us
    ppermute x3, waiting for transfers between devices, over_rows(): value = value + lax.ppermute(value, 'row', xor_pairs(rows, bit))  6.02 us
    ppermute x6, starting transfers between devices, gather_pieces(): lax.ppermute(piece, axis, xor_pairs(count, bit))  4.6 us
    ppermute x1, starting transfers between devices, shards(): diag_scaled = lax.ppermute(pair_scaled, 'row', outward)  3.5 us
    ppermute x1, waiting for transfers between devices, shards(): returned = lax.ppermute(joined, 'row', pairs)  2.87 us
  transfers between devices with their start and end apart: 15, of which 8 were waited for; matrix products, arithmetic and copies ran while one was open for 9% of the time, Pallas kernels for 25%

profile of v4, /device:TPU:0, one launch (start us, length us, event | category | flops | bytes accessed | tf_op | source)
XLA Modules:
  0.0 65.3 jit_solution(2670203224304691053)
XLA Ops:
  0.6 3.0 %collective-permute-start.2 = (bf16[64,4096]{1,0:T(8,128)(2,1)}, bf16[64,4096]{1,0:T(8,128)(2,1)S(1)}, u32[]{:S(2)}, u32[]{:S(2)}) collective-permute-start(bf16[64,4096]{1,0:T(8,128)(2,1)} %refs_0_.3), channel_id=1, source_target_pairs={{0,2},{1,3},{2,0},{3,1},{4,6},{5,7},{6,4},{7,5},{8,10},{9,11},{10,... | collective-permute-start | bytes 1572872 | tf_op jit(solution)/shard_map/ppermute | solution.py:49
  3.6 1.1 %scale.1 = (bf16[64,4096]{1,0:T(8,128)(2,1)S(1)}, f32[1,4096]{1,0:T(1,128)S(1)}) custom-call(s32[1,4096]{1,0:T(1,128)} %bitcast.32, bf16[64,4096]{1,0:T(8,128)(2,1)} %features_hbm.1), custom_call_target="tpu_custom_call" | custom-call | flops 1 | bytes 1 | tf_op jit(solution)/shard_map/scale/pallas_call | solution.py:212
  4.8 1.6 %collective-permute-start = (bf16[64,4096]{1,0:T(8,128)(2,1)S(1)}, bf16[64,4096]{1,0:T(8,128)(2,1)S(1)}, u32[]{:S(2)}, u32[]{:S(2)}) collective-permute-start(bf16[64,4096]{1,0:T(8,128)(2,1)S(1)} %get-tuple-element.25.own), channel_id=1, source_target_pairs={{0,4},{4,0},{8,12},{12,8},{16,20},{20,16},{24,28},{28,24},{1,5},{5... | collective-permute-start | bytes 1572872 | tf_op jit(solution)/shard_map/ppermute | solution.py:226
  6.3 0.0 collective-permute-start.3
  6.3 0.8 %copy.11 = s32[32,10]{1,0:T(8,128)S(1)} copy(s32[32,10]{0,1:T(8,128)} %param.12) | data formatting | bytes 2560 | tf_op args[4]
  7.1 0.7 %fusion.13.slot_ref = s32[32,10]{1,0:T(8,128)S(1)} fusion(s32[32,10]{1,0:T(8,128)S(1)} %copy.11, s32[]{:T(128)S(6)} %xor.18, s32[]{:T(128)S(6)} %axis_index.25, s32[32]{0:T(128)} %param.13), kind=kLoop, calls=%fused_computation.40 | loop fusion | flops 8640 | bytes 2696 | tf_op jit(solution)/shard_map/jit(_where)/select_n | solution.py:231
  7.8 7.9 %collective-permute-done.2.refs_1_ = bf16[64,4096]{1,0:T(8,128)(2,1)S(1)} collective-permute-done((bf16[64,4096]{1,0:T(8,128)(2,1)}, bf16[64,4096]{1,0:T(8,128)(2,1)S(1)}, u32[]{:S(2)}, u32[]{:S(2)}) %collective-permute-start.2) | collective-permute-done | bytes 524320 | tf_op jit(solution)/shard_map/ppermute | solution.py:49
  15.8 0.0 collective-permute-start.4
  15.8 2.4 %collective-permute-done.pair = bf16[64,4096]{1,0:T(8,128)(2,1)S(1)} collective-permute-done((bf16[64,4096]{1,0:T(8,128)(2,1)S(1)}, bf16[64,4096]{1,0:T(8,128)(2,1)S(1)}, u32[]{:S(2)}, u32[]{:S(2)}) %collective-permute-start) | collective-permute-done | bytes 524320 | tf_op jit(solution)/shard_map/ppermute | solution.py:226
  18.2 3.5 %collective-permute-start.1 = (bf16[64,4096]{1,0:T(8,128)(2,1)S(1)}, bf16[64,4096]{1,0:T(8,128)(2,1)S(1)}, u32[]{:S(2)}, u32[]{:S(2)}) collective-permute-start(bf16[64,4096]{1,0:T(8,128)(2,1)S(1)} %collective-permute-done.pair), channel_id=1, source_target_pairs={{0,8},{8,16},{12,4},{16,24},{20,12},{28,20},{1,9},{9,17},{13,5},{1... | collective-permute-start | bytes 1572872 | tf_op jit(solution)/shard_map/ppermute | solution.py:227
  21.7 0.0 collective-permute-done.3.refs_2_
  21.7 0.0 collective-permute-done.4.refs_3_
  21.7 7.6 %backward_tiles.1 = (f32[64,4096]{1,0:T(8,128)}, bf16[64,4096]{1,0:T(8,128)(2,1)}, bf16[64,4096]{1,0:T(8,128)(2,1)S(1)}) custom-call(s32[32,10]{1,0:T(8,128)S(1)} %fusion.13.slot_ref, f32[1,4096]{1,0:T(1,128)S(1)} %get-tuple-element.18.inv, bf16[256,256]{1,0:T(8,128)(2,1)} %weight_hbm.1, bf16[64,4096]{1,0:T(8,128)(2,1)} %refs_0_.3, ...), custom_call_target="tpu_custom_call" | custom-call | flops 1 | bytes 1 | tf_op jit(solution)/shard_map/backward_tiles/pallas_call | solution.py:236
  29.4 0.0 copy-start
  29.4 1.4 %collective-permute-start.8 = (bf16[64,4096]{1,0:T(8,128)(2,1)S(1)}, bf16[64,4096]{1,0:T(8,128)(2,1)}, u32[]{:S(2)}, u32[]{:S(2)}) collective-permute-start(bf16[64,4096]{1,0:T(8,128)(2,1)S(1)} %get-tuple-element.24), channel_id=1, source_target_pairs={{8,0},{16,8},{4,12},{24,16},{12,20},{20,28},{9,1},{17,9},{5,13},{2... | collective-permute-start | bytes 1572872 | tf_op jit(solution)/shard_map/ppermute | solution.py:272
  30.8 0.8 %collective-permute-done.1.diag = bf16[64,4096]{1,0:T(8,128)(2,1)S(1)} collective-permute-done((bf16[64,4096]{1,0:T(8,128)(2,1)S(1)}, bf16[64,4096]{1,0:T(8,128)(2,1)S(1)}, u32[]{:S(2)}, u32[]{:S(2)}) %collective-permute-start.1) | collective-permute-done | bytes 524320 | tf_op jit(solution)/shard_map/ppermute | solution.py:227
  31.7 7.0 %forward_tiles.1.refs_4_ = bf16[64,4096]{1,0:T(8,128)(2,1)S(1)} custom-call(s32[32,10]{1,0:T(8,128)S(1)} %fusion.13.slot_ref, f32[1,4096]{1,0:T(1,128)S(1)} %get-tuple-element.18.inv, bf16[64,4096]{1,0:T(8,128)(2,1)S(1)} %get-tuple-element.25.own, bf16[64,4096]{1,0:T(8,128)(2,1)S(1)} %collective-permute-done.pair, ...), custom_call_target="tpu_custom_call" | custom-call | flops 1 | bytes 1 | tf_op jit(solution)/shard_map/forward_tiles/pallas_call | solution.py:259
  38.6 0.0 copy-done
  38.6 0.0 copy-start.2
  38.7 0.8 %outer_product.1 = f32[64,256]{1,0:T(8,128)S(1)} custom-call(bf16[64,4096]{1,0:T(8,128)(2,1)S(1)} %copy-done, bf16[64,4096]{1,0:T(8,128)(2,1)S(1)} %collective-permute-done.2.refs_1_, bf16[64,4096]{1,0:T(8,128)(2,1)S(1)} %collective-permute-done.3.refs_2_, bf16[64,4096]{1,0:T(8,128)(2,1)S(1)} %collective-permute-done.4.refs_3_, ...), custom_call_target="tpu_custom_call" | custom-call | flops 1 | bytes 1 | tf_op jit(solution)/shard_map/outer_product/pallas_call | solution.py:289
  39.4 0.0 copy-start.1
  39.4 2.6 %collective-permute-start.10 = (f32[64,256]{1,0:T(8,128)S(1)}, f32[64,256]{1,0:T(8,128)S(1)}, u32[]{:S(2)}, u32[]{:S(2)}) collective-permute-start(f32[64,256]{1,0:T(8,128)S(1)} %outer_product.1), channel_id=1, source_target_pairs={{0,4},{4,0},{8,12},{12,8},{16,20},{20,16},{24,28},{28,24},{1,5},{5... | collective-permute-start | bytes 196616 | tf_op jit(solution)/shard_map/ppermute | solution.py:306
  42.1 1.0 %collective-permute-start.5 = (bf16[64,4096]{1,0:T(8,128)(2,1)S(1)}, bf16[64,4096]{1,0:T(8,128)(2,1)S(1)}, u32[]{:S(2)}, u32[]{:S(2)}) collective-permute-start(bf16[64,4096]{1,0:T(8,128)(2,1)S(1)} %forward_tiles.1.refs_4_), channel_id=1, source_target_pairs={{0,2},{1,3},{2,0},{3,1},{4,6},{5,7},{6,4},{7,5},{8,10},{9,11},{10,... | collective-permute-start | bytes 1572872 | tf_op jit(solution)/shard_map/ppermute | solution.py:49
  43.1 1.2 %collective-permute-done.10 = f32[64,256]{1,0:T(8,128)S(1)} collective-permute-done((f32[64,256]{1,0:T(8,128)S(1)}, f32[64,256]{1,0:T(8,128)S(1)}, u32[]{:S(2)}, u32[]{:S(2)}) %collective-permute-start.10) | collective-permute-done | bytes 65568 | tf_op jit(solution)/shard_map/ppermute | solution.py:306
  44.3 0.1 fusion.17
  44.4 0.1 collective-permute-start.11
  44.5 0.0 collective-permute-done.8
  44.5 1.3 %add_convert_fusion = bf16[64,4096]{1,0:T(8,128)(2,1)S(1)} fusion(bf16[64,4096]{1,0:T(8,128)(2,1)} %collective-permute-done.8, bf16[64,4096]{1,0:T(8,128)(2,1)} %get-tuple-element.29), kind=kLoop, calls=%fused_computation.9 | loop fusion | flops 1048576 | bytes 1572864 | tf_op jit(solution)/shard_map/convert_element_type | solution.py:274
  45.8 2.1 %collective-permute-start.9 = (bf16[64,4096]{1,0:T(8,128)(2,1)S(1)}, bf16[64,4096]{1,0:T(8,128)(2,1)S(1)}, u32[]{:S(2)}, u32[]{:S(2)}) collective-permute-start(bf16[64,4096]{1,0:T(8,128)(2,1)S(1)} %add_convert_fusion), channel_id=1, source_target_pairs={{0,4},{4,0},{8,12},{12,8},{16,20},{20,16},{24,28},{28,24},{1,5},{5... | collective-permute-start | bytes 1572872 | tf_op jit(solution)/shard_map/ppermute | solution.py:275
  47.9 0.0 collective-permute-done.11
  47.9 0.1 maximum_bitcast_fusion
  48.0 1.5 %collective-permute-start.12 = (f32[2,64,128]{2,1,0:T(8,128)S(1)}, f32[2,64,128]{2,1,0:T(8,128)S(1)}, u32[]{:S(2)}, u32[]{:S(2)}) collective-permute-start(f32[2,64,128]{2,1,0:T(8,128)S(1)} %pad_maximum_fusion.2), channel_id=1, source_target_pairs={{0,8},{4,12},{8,0},{12,4},{16,24},{20,28},{24,16},{28,20},{1,9},{5... | collective-permute-start | bytes 196616 | tf_op jit(solution)/shard_map/ppermute | solution.py:306
  49.5 0.0 copy-done.2
  49.5 0.1 dynamic-slice_bitcast_fusion.3
  49.7 2.7 %collective-permute-done.12 = f32[2,64,128]{2,1,0:T(8,128)S(1)} collective-permute-done((f32[2,64,128]{2,1,0:T(8,128)S(1)}, f32[2,64,128]{2,1,0:T(8,128)S(1)}, u32[]{:S(2)}, u32[]{:S(2)}) %collective-permute-start.12) | collective-permute-done | bytes 65568 | tf_op jit(solution)/shard_map/ppermute | solution.py:306
  52.4 2.5 %collective-permute-start.13 = (f32[2,64,128]{2,1,0:T(8,128)S(1)}, f32[2,64,128]{2,1,0:T(8,128)S(1)}, u32[]{:S(2)}, u32[]{:S(2)}) collective-permute-start(f32[2,64,128]{2,1,0:T(8,128)S(1)} %add.79), channel_id=1, source_target_pairs={{0,16},{4,20},{8,24},{12,28},{16,0},{20,4},{24,8},{28,12},{1,17},{... | collective-permute-start | bytes 196616 | tf_op jit(solution)/shard_map/ppermute | solution.py:306
  54.9 0.1 collective-permute-start.6
  55.0 0.0 collective-permute-done.5
  55.0 0.5 collective-permute-start.7
  55.5 2.1 %collective-permute-done.13 = f32[2,64,128]{2,1,0:T(8,128)S(1)} collective-permute-done((f32[2,64,128]{2,1,0:T(8,128)S(1)}, f32[2,64,128]{2,1,0:T(8,128)S(1)}, u32[]{:S(2)}, u32[]{:S(2)}) %collective-permute-start.13) | collective-permute-done | bytes 65568 | tf_op jit(solution)/shard_map/ppermute | solution.py:306
  57.6 2.9 %collective-permute-done.9 = bf16[64,4096]{1,0:T(8,128)(2,1)S(1)} collective-permute-done((bf16[64,4096]{1,0:T(8,128)(2,1)S(1)}, bf16[64,4096]{1,0:T(8,128)(2,1)S(1)}, u32[]{:S(2)}, u32[]{:S(2)}) %collective-permute-start.9) | collective-permute-done | bytes 524320 | tf_op jit(solution)/shard_map/ppermute | solution.py:275
  60.5 1.0 %collective-permute-start.14 = (f32[1,64,128]{2,1,0:T(8,128)S(1)}, f32[1,64,128]{2,1,0:T(8,128)S(1)}, u32[]{:S(2)}, u32[]{:S(2)}) collective-permute-start(f32[1,64,128]{2,1,0:T(8,128)S(1)} %get-tuple-element.41), channel_id=1, source_target_pairs={{0,2},{1,3},{2,0},{3,1},{4,6},{5,7},{6,4},{7,5},{8,10},{9,11},{10,... | collective-permute-start | bytes 98312 | tf_op jit(solution)/shard_map/ppermute | solution.py:318
  61.5 0.0 copy-done.1
  61.5 1.1 %add_multiply_fusion = f32[64,4096]{1,0:T(8,128)} fusion(f32[64,4096]{1,0:T(8,128)S(1)} %copy-done.1, bf16[64,4096]{1,0:T(8,128)(2,1)S(1)} %collective-permute-done.9, f32[4096]{0:T(1024)S(1)} %bitcast.29), kind=kLoop, calls=%fused_computation.8 | loop fusion | flops 786432 | bytes 2637824 | tf_op jit(solution)/shard_map/mul | solution.py:276
  62.6 0.0 collective-permute-done.6
  62.6 0.0 collective-permute-done.7
  62.6 1.3 %convolution_convert_fusion = bf16[64,4096]{1,0:T(8,128)(2,1)} fusion(bf16[256,64]{1,0:T(8,128)(2,1)S(1)} %bitcast.30, bf16[64,4096]{1,0:T(8,128)(2,1)S(1)} %collective-permute-done.7, bf16[64,4096]{1,0:T(8,128)(2,1)S(1)} %collective-permute-done.6, bf16[64,4096]{1,0:T(8,128)(2,1)S(1)} %collective-permute-done.5, bf16[64,4096]{1,0:T(8,128)(2,1)S(1)} %forward_tiles.1.refs_4_), kind=kOutput, calls=%fused_computation | convolution fusion | flops 142868480 | bytes 2654208 | tf_op jit(solution)/shard_map/dot_general | solution.py:282
  63.9 0.5 collective-permute-done.14
  64.4 0.1 fusion.9
  64.6 0.7 %fusion.7 = f32[256,64]{0,1:T(8,128)} fusion(f32[64,64]{1,0:T(8,128)S(1)} %get-tuple-element.40, f32[64,64]{1,0:T(8,128)S(1)} %get-tuple-element.39, f32[64,64]{1,0:T(8,128)S(1)} %get-tuple-element.38, f32[64,64]{1,0:T(8,128)S(1)} %get-tuple-element.37), kind=kLoop, calls=%fused_computation.22 | loop fusion | flops 65536 | bytes 131072 | tf_op jit(solution)/shard_map/transpose | solution.py:332
  (8 shorter events, 0.1 us)
Async XLA Ops:
  0.6 15.1 %collective-permute-start.2 = (bf16[64,4096]{1,0:T(8,128)(2,1)}, bf16[64,4096]{1,0:T(8,128)(2,1)S(1)}, u32[]{:S(2)}, u32[]{:S(2)}) collective-permute-start(bf16[64,4096]{1,0:T(8,128)(2,1)} %refs_0_.3), channel_id=1, source_target_pairs={{0,2},{1,3},{2,0},{3,1},{4,6},{5,7},{6,4},{7,5},{8,10},{9,11},{10,... | collective-permute-start | bytes 1572872 | tf_op jit(solution)/shard_map/ppermute | solution.py:49
  4.8 13.4 %collective-permute-start = (bf16[64,4096]{1,0:T(8,128)(2,1)S(1)}, bf16[64,4096]{1,0:T(8,128)(2,1)S(1)}, u32[]{:S(2)}, u32[]{:S(2)}) collective-permute-start(bf16[64,4096]{1,0:T(8,128)(2,1)S(1)} %get-tuple-element.25.own), channel_id=1, source_target_pairs={{0,4},{4,0},{8,12},{12,8},{16,20},{20,16},{24,28},{28,24},{1,5},{5... | collective-permute-start | bytes 1572872 | tf_op jit(solution)/shard_map/ppermute | solution.py:226
  6.3 15.4 %collective-permute-start.3 = (bf16[64,4096]{1,0:T(8,128)(2,1)}, bf16[64,4096]{1,0:T(8,128)(2,1)S(1)}, u32[]{:S(2)}, u32[]{:S(2)}) collective-permute-start(bf16[64,4096]{1,0:T(8,128)(2,1)} %refs_0_.3), channel_id=1, source_target_pairs={{0,1},{1,0},{2,3},{3,2},{4,5},{5,4},{6,7},{7,6},{8,9},{9,8},{10,11... | collective-permute-start | bytes 1572872 | tf_op jit(solution)/shard_map/ppermute | solution.py:49
  15.8 6.0 %collective-permute-start.4 = (bf16[64,4096]{1,0:T(8,128)(2,1)S(1)}, bf16[64,4096]{1,0:T(8,128)(2,1)S(1)}, u32[]{:S(2)}, u32[]{:S(2)}) collective-permute-start(bf16[64,4096]{1,0:T(8,128)(2,1)S(1)} %collective-permute-done.2.refs_1_), channel_id=1, source_target_pairs={{0,1},{1,0},{2,3},{3,2},{4,5},{5,4},{6,7},{7,6},{8,9},{9,8},{10,11... | collective-permute-start | bytes 1572872 | tf_op jit(solution)/shard_map/ppermute | solution.py:49
  18.2 13.5 %collective-permute-start.1 = (bf16[64,4096]{1,0:T(8,128)(2,1)S(1)}, bf16[64,4096]{1,0:T(8,128)(2,1)S(1)}, u32[]{:S(2)}, u32[]{:S(2)}) collective-permute-start(bf16[64,4096]{1,0:T(8,128)(2,1)S(1)} %collective-permute-done.pair), channel_id=1, source_target_pairs={{0,8},{8,16},{12,4},{16,24},{20,12},{28,20},{1,9},{9,17},{13,5},{1... | collective-permute-start | bytes 1572872 | tf_op jit(solution)/shard_map/ppermute | solution.py:227
  29.4 9.2 %copy-start = (bf16[64,4096]{1,0:T(8,128)(2,1)S(1)}, bf16[64,4096]{1,0:T(8,128)(2,1)}, u32[]{:S(2)}) copy-start(bf16[64,4096]{1,0:T(8,128)(2,1)} %refs_0_.3) | copy-start | bytes 1572868
  29.4 15.1 %collective-permute-start.8 = (bf16[64,4096]{1,0:T(8,128)(2,1)S(1)}, bf16[64,4096]{1,0:T(8,128)(2,1)}, u32[]{:S(2)}, u32[]{:S(2)}) collective-permute-start(bf16[64,4096]{1,0:T(8,128)(2,1)S(1)} %get-tuple-element.24), channel_id=1, source_target_pairs={{8,0},{16,8},{4,12},{24,16},{12,20},{20,28},{9,1},{17,9},{5,13},{2... | collective-permute-start | bytes 1572872 | tf_op jit(solution)/shard_map/ppermute | solution.py:272
  38.6 10.9 %copy-start.2 = (bf16[256,256]{1,0:T(8,128)(2,1)S(1)}, bf16[256,256]{1,0:T(8,128)(2,1)}, u32[]{:S(2)}) copy-start(bf16[256,256]{1,0:T(8,128)(2,1)} %weight_hbm.1) | copy-start | bytes 393220
  39.4 22.1 %copy-start.1 = (f32[64,4096]{1,0:T(8,128)S(1)}, f32[64,4096]{1,0:T(8,128)}, u32[]{:S(2)}) copy-start(f32[64,4096]{1,0:T(8,128)} %get-tuple-element.28) | copy-start | bytes 3145732
  39.4 4.9 %collective-permute-start.10 = (f32[64,256]{1,0:T(8,128)S(1)}, f32[64,256]{1,0:T(8,128)S(1)}, u32[]{:S(2)}, u32[]{:S(2)}) collective-permute-start(f32[64,256]{1,0:T(8,128)S(1)} %outer_product.1), channel_id=1, source_target_pairs={{0,4},{4,0},{8,12},{12,8},{16,20},{20,16},{24,28},{28,24},{1,5},{5... | collective-permute-start | bytes 196616 | tf_op jit(solution)/shard_map/ppermute | solution.py:306
  42.1 12.9 %collective-permute-start.5 = (bf16[64,4096]{1,0:T(8,128)(2,1)S(1)}, bf16[64,4096]{1,0:T(8,128)(2,1)S(1)}, u32[]{:S(2)}, u32[]{:S(2)}) collective-permute-start(bf16[64,4096]{1,0:T(8,128)(2,1)S(1)} %forward_tiles.1.refs_4_), channel_id=1, source_target_pairs={{0,2},{1,3},{2,0},{3,1},{4,6},{5,7},{6,4},{7,5},{8,10},{9,11},{10,... | collective-permute-start | bytes 1572872 | tf_op jit(solution)/shard_map/ppermute | solution.py:49
  44.4 3.5 %collective-permute-start.11 = (f32[2,64,64]{2,1,0:T(8,128)S(1)}, f32[2,64,64]{2,1,0:T(8,128)S(1)}, u32[]{:S(2)}, u32[]{:S(2)}) collective-permute-start(f32[2,64,64]{2,1,0:T(8,128)S(1)} %pad_maximum_fusion.1), channel_id=1, source_target_pairs={{0,1},{1,0},{2,3},{3,2},{4,5},{5,4},{6,7},{7,6},{8,9},{9,8},{10,11... | collective-permute-start | bytes 98312 | tf_op jit(solution)/shard_map/ppermute | solution.py:318
  45.8 14.7 %collective-permute-start.9 = (bf16[64,4096]{1,0:T(8,128)(2,1)S(1)}, bf16[64,4096]{1,0:T(8,128)(2,1)S(1)}, u32[]{:S(2)}, u32[]{:S(2)}) collective-permute-start(bf16[64,4096]{1,0:T(8,128)(2,1)S(1)} %add_convert_fusion), channel_id=1, source_target_pairs={{0,4},{4,0},{8,12},{12,8},{16,20},{20,16},{24,28},{28,24},{1,5},{5... | collective-permute-start | bytes 1572872 | tf_op jit(solution)/shard_map/ppermute | solution.py:275
  48.0 4.3 %collective-permute-start.12 = (f32[2,64,128]{2,1,0:T(8,128)S(1)}, f32[2,64,128]{2,1,0:T(8,128)S(1)}, u32[]{:S(2)}, u32[]{:S(2)}) collective-permute-start(f32[2,64,128]{2,1,0:T(8,128)S(1)} %pad_maximum_fusion.2), channel_id=1, source_target_pairs={{0,8},{4,12},{8,0},{12,4},{16,24},{20,28},{24,16},{28,20},{1,9},{5... | collective-permute-start | bytes 196616 | tf_op jit(solution)/shard_map/ppermute | solution.py:306
  52.4 5.2 %collective-permute-start.13 = (f32[2,64,128]{2,1,0:T(8,128)S(1)}, f32[2,64,128]{2,1,0:T(8,128)S(1)}, u32[]{:S(2)}, u32[]{:S(2)}) collective-permute-start(f32[2,64,128]{2,1,0:T(8,128)S(1)} %add.79), channel_id=1, source_target_pairs={{0,16},{4,20},{8,24},{12,28},{16,0},{20,4},{24,8},{28,12},{1,17},{... | collective-permute-start | bytes 196616 | tf_op jit(solution)/shard_map/ppermute | solution.py:306
  54.9 7.7 %collective-permute-start.6 = (bf16[64,4096]{1,0:T(8,128)(2,1)S(1)}, bf16[64,4096]{1,0:T(8,128)(2,1)S(1)}, u32[]{:S(2)}, u32[]{:S(2)}) collective-permute-start(bf16[64,4096]{1,0:T(8,128)(2,1)S(1)} %forward_tiles.1.refs_4_), channel_id=1, source_target_pairs={{0,1},{1,0},{2,3},{3,2},{4,5},{5,4},{6,7},{7,6},{8,9},{9,8},{10,11... | collective-permute-start | bytes 1572872 | tf_op jit(solution)/shard_map/ppermute | solution.py:49
  55.0 7.6 %collective-permute-start.7 = (bf16[64,4096]{1,0:T(8,128)(2,1)S(1)}, bf16[64,4096]{1,0:T(8,128)(2,1)S(1)}, u32[]{:S(2)}, u32[]{:S(2)}) collective-permute-start(bf16[64,4096]{1,0:T(8,128)(2,1)S(1)} %collective-permute-done.5), channel_id=1, source_target_pairs={{0,1},{1,0},{2,3},{3,2},{4,5},{5,4},{6,7},{7,6},{8,9},{9,8},{10,11... | collective-permute-start | bytes 1572872 | tf_op jit(solution)/shard_map/ppermute | solution.py:49
  60.5 3.9 %collective-permute-start.14 = (f32[1,64,128]{2,1,0:T(8,128)S(1)}, f32[1,64,128]{2,1,0:T(8,128)S(1)}, u32[]{:S(2)}, u32[]{:S(2)}) collective-permute-start(f32[1,64,128]{2,1,0:T(8,128)S(1)} %get-tuple-element.41), channel_id=1, source_target_pairs={{0,2},{1,3},{2,0},{3,1},{4,6},{5,7},{6,4},{7,5},{8,10},{9,11},{10,... | collective-permute-start | bytes 98312 | tf_op jit(solution)/shard_map/ppermute | solution.py:318

commit v5 on v4

--- a/solution.py
+++ b/solution.py
@@ -9,7 +9,7 @@
 from jax.sharding import PartitionSpec as P
 
 CONTRACT_LAST = (((1,), (1,)), ((), ()))
-VMEM_BYTES = 40 * 1024 * 1024
+VMEM_BYTES = 32 * 1024 * 1024
 
 
 def xor_pairs(count, bit):
@@ -292,7 +292,7 @@
         in_specs=[vmem] * (cols + 1),
         out_specs=vmem,
         compiler_params=pltpu.CompilerParams(vmem_limit_bytes=VMEM_BYTES // 4),
-        cost_estimate=light,
+        cost_estimate=pl.CostEstimate(flops=1000000000, bytes_accessed=1, transcendentals=0),
         name="outer_product",
     )(*cots, aggregated)
     row_bits = bits_of(rows) if rows & (rows - 1) == 0 else []
@@ -313,8 +313,8 @@
         kept = [o for o in blocks_of if not o & bit]
         both = jnp.stack([blocks_of[o] for o in kept] + [blocks_of[o | bit] for o in kept])
         if 2 * bit == cols:
-            both = over_rows(both, row_bits[-2::-1], [(joined,)] + [()] * len(row_bits))
-            (both,) = tied((both,), (agg_pieces[1], returned))
+            both = over_rows(both, row_bits[:-1], [(joined,)] + [()] * len(row_bits))
+            (both,) = tied((both,), (returned,))
         other = lax.ppermute(both[len(kept) :], "col", xor_pairs(cols, bit))
         blocks_of = {
             o: jnp.concatenate([both[k], other[k]], axis=1) for k, o in enumerate(kept)

time: 65.6 us -> 65.5 us (level)
  starting transfers between devices: 20.9 us -> 19.6 us
  waiting for transfers between devices: 20.6 us -> 21.9 us
    ppermute x3, waiting for transfers between devices: 6.02 us -> 8.76 us  [over_rows(): value = value + lax.ppermute(value, 'row', xor_pairs(rows, bit))]
    ppermute x1, waiting for transfers between devices: 2.87 us -> 1.46 us  [shards(): returned = lax.ppermute(joined, 'row', pairs)]
    ppermute x3, starting transfers between devices: 6.66 us -> 5.3 us  [over_rows(): value = value + lax.ppermute(value, 'row', xor_pairs(rows, bit))]
  transfers between devices with their start and end apart: 15 -> 15, of which waited for: 8 -> 8; matrix products, arithmetic and copies ran while one was open for 9% -> 8% of each run, Pallas kernels for 25% -> 25%
where the time goes in v5:
time: 65.5 us; the launch traced here: 65.2 us
  waiting for transfers between devices  21.9 us (33%)
  starting transfers between devices  19.6 us (30%)
  Pallas kernels  16.5 us (25%)
  other arithmetic  4 us (6%)
  matrix products  1.31 us (2%)
  local copies, waits for them, and re-layouts  1.01 us (2%)
  between operations  0.84 us (1%)
    ppermute x3, waiting for transfers between devices, over_rows(): value = value + lax.ppermute(value, 'row', xor_pairs(rows, bit))  8.76 us
    ppermute x6, waiting for transfers between devices, gather_pieces(): lax.ppermute(piece, axis, xor_pairs(count, bit))  7.93 us
    pallas_call x1, Pallas kernels, shards(): pl.pallas_call(functools.partial(backward_kernel, offsets=offsets, togeth...  7.67 us
    pallas_call x1, Pallas kernels, shards(): pl.pallas_call(functools.partial(forward_kernel, together=together), out_...  6.98 us
    ppermute x3, starting transfers between devices, over_rows(): value = value + lax.ppermute(value, 'row', xor_pairs(rows, bit))  5.3 us
    ppermute x6, starting transfers between devices, gather_pieces(): lax.ppermute(piece, axis, xor_pairs(count, bit))  4.6 us
    ppermute x1, starting transfers between devices, shards(): diag_scaled = lax.ppermute(pair_scaled, 'row', outward)  3.5 us
    ppermute x1, waiting for transfers between devices, shards(): pair_scaled = lax.ppermute(scaled, 'row', pairs)  2.43 us
  transfers between devices with their start and end apart: 15, of which 8 were waited for; matrix products, arithmetic and copies ran while one was open for 8% of the time, Pallas kernels for 25%

profile of v5, /device:TPU:0, one launch (start us, length us, event | category | flops | bytes accessed | tf_op | source)
XLA Modules:
  0.0 65.2 jit_solution(1100609263599037086)
XLA Ops:
  0.6 3.0 %collective-permute-start.2 = (bf16[64,4096]{1,0:T(8,128)(2,1)}, bf16[64,4096]{1,0:T(8,128)(2,1)S(1)}, u32[]{:S(2)}, u32[]{:S(2)}) collective-permute-start(bf16[64,4096]{1,0:T(8,128)(2,1)} %refs_0_.3), channel_id=1, source_target_pairs={{0,2},{1,3},{2,0},{3,1},{4,6},{5,7},{6,4},{7,5},{8,10},{9,11},{10,... | collective-permute-start | bytes 1572872 | tf_op jit(solution)/shard_map/ppermute | solution.py:49
  3.6 1.1 %scale.1 = (bf16[64,4096]{1,0:T(8,128)(2,1)S(1)}, f32[1,4096]{1,0:T(1,128)S(1)}) custom-call(s32[1,4096]{1,0:T(1,128)} %bitcast.32, bf16[64,4096]{1,0:T(8,128)(2,1)} %features_hbm.1), custom_call_target="tpu_custom_call" | custom-call | flops 1 | bytes 1 | tf_op jit(solution)/shard_map/scale/pallas_call | solution.py:212
  4.8 1.6 %collective-permute-start = (bf16[64,4096]{1,0:T(8,128)(2,1)S(1)}, bf16[64,4096]{1,0:T(8,128)(2,1)S(1)}, u32[]{:S(2)}, u32[]{:S(2)}) collective-permute-start(bf16[64,4096]{1,0:T(8,128)(2,1)S(1)} %get-tuple-element.25.own), channel_id=1, source_target_pairs={{0,4},{4,0},{8,12},{12,8},{16,20},{20,16},{24,28},{28,24},{1,5},{5... | collective-permute-start | bytes 1572872 | tf_op jit(solution)/shard_map/ppermute | solution.py:226
  6.3 0.0 collective-permute-start.3
  6.3 0.8 %copy.11 = s32[32,10]{1,0:T(8,128)S(1)} copy(s32[32,10]{0,1:T(8,128)} %param.12) | data formatting | bytes 2560 | tf_op args[4]
  7.1 0.7 %fusion.13.slot_ref = s32[32,10]{1,0:T(8,128)S(1)} fusion(s32[32,10]{1,0:T(8,128)S(1)} %copy.11, s32[]{:T(128)S(6)} %xor.18, s32[]{:T(128)S(6)} %axis_index.25, s32[32]{0:T(128)} %param.13), kind=kLoop, calls=%fused_computation.40 | loop fusion | flops 8640 | bytes 2696 | tf_op jit(solution)/shard_map/jit(_where)/select_n | solution.py:231
  7.8 7.9 %collective-permute-done.2.refs_1_ = bf16[64,4096]{1,0:T(8,128)(2,1)S(1)} collective-permute-done((bf16[64,4096]{1,0:T(8,128)(2,1)}, bf16[64,4096]{1,0:T(8,128)(2,1)S(1)}, u32[]{:S(2)}, u32[]{:S(2)}) %collective-permute-start.2) | collective-permute-done | bytes 524320 | tf_op jit(solution)/shard_map/ppermute | solution.py:49
  15.8 0.0 collective-permute-start.4
  15.8 2.4 %collective-permute-done.pair = bf16[64,4096]{1,0:T(8,128)(2,1)S(1)} collective-permute-done((bf16[64,4096]{1,0:T(8,128)(2,1)S(1)}, bf16[64,4096]{1,0:T(8,128)(2,1)S(1)}, u32[]{:S(2)}, u32[]{:S(2)}) %collective-permute-start) | collective-permute-done | bytes 524320 | tf_op jit(solution)/shard_map/ppermute | solution.py:226
  18.2 3.5 %collective-permute-start.1 = (bf16[64,4096]{1,0:T(8,128)(2,1)S(1)}, bf16[64,4096]{1,0:T(8,128)(2,1)S(1)}, u32[]{:S(2)}, u32[]{:S(2)}) collective-permute-start(bf16[64,4096]{1,0:T(8,128)(2,1)S(1)} %collective-permute-done.pair), channel_id=1, source_target_pairs={{0,8},{8,16},{12,4},{16,24},{20,12},{28,20},{1,9},{9,17},{13,5},{1... | collective-permute-start | bytes 1572872 | tf_op jit(solution)/shard_map/ppermute | solution.py:227
  21.7 0.0 collective-permute-done.3.refs_2_
  21.7 0.0 collective-permute-done.4.refs_3_
  21.7 7.7 %backward_tiles.1 = (f32[64,4096]{1,0:T(8,128)}, bf16[64,4096]{1,0:T(8,128)(2,1)}, bf16[64,4096]{1,0:T(8,128)(2,1)S(1)}) custom-call(s32[32,10]{1,0:T(8,128)S(1)} %fusion.13.slot_ref, f32[1,4096]{1,0:T(1,128)S(1)} %get-tuple-element.18.inv, bf16[256,256]{1,0:T(8,128)(2,1)} %weight_hbm.1, bf16[64,4096]{1,0:T(8,128)(2,1)} %refs_0_.3, ...), custom_call_target="tpu_custom_call" | custom-call | flops 1 | bytes 1 | tf_op jit(solution)/shard_map/backward_tiles/pallas_call | solution.py:236
  29.4 0.0 copy-start
  29.4 1.4 %collective-permute-start.8 = (bf16[64,4096]{1,0:T(8,128)(2,1)S(1)}, bf16[64,4096]{1,0:T(8,128)(2,1)}, u32[]{:S(2)}, u32[]{:S(2)}) collective-permute-start(bf16[64,4096]{1,0:T(8,128)(2,1)S(1)} %get-tuple-element.24), channel_id=1, source_target_pairs={{8,0},{16,8},{4,12},{24,16},{12,20},{20,28},{9,1},{17,9},{5,13},{2... | collective-permute-start | bytes 1572872 | tf_op jit(solution)/shard_map/ppermute | solution.py:272
  30.9 0.8 %collective-permute-done.1.diag = bf16[64,4096]{1,0:T(8,128)(2,1)S(1)} collective-permute-done((bf16[64,4096]{1,0:T(8,128)(2,1)S(1)}, bf16[64,4096]{1,0:T(8,128)(2,1)S(1)}, u32[]{:S(2)}, u32[]{:S(2)}) %collective-permute-start.1) | collective-permute-done | bytes 524320 | tf_op jit(solution)/shard_map/ppermute | solution.py:227
  31.7 7.0 %forward_tiles.1.refs_4_ = bf16[64,4096]{1,0:T(8,128)(2,1)S(1)} custom-call(s32[32,10]{1,0:T(8,128)S(1)} %fusion.13.slot_ref, f32[1,4096]{1,0:T(1,128)S(1)} %get-tuple-element.18.inv, bf16[64,4096]{1,0:T(8,128)(2,1)S(1)} %get-tuple-element.25.own, bf16[64,4096]{1,0:T(8,128)(2,1)S(1)} %collective-permute-done.pair, ...), custom_call_target="tpu_custom_call" | custom-call | flops 1 | bytes 1 | tf_op jit(solution)/shard_map/forward_tiles/pallas_call | solution.py:259
  38.6 0.0 copy-done
  38.7 0.0 copy-start.2
  38.7 0.0 copy-start.3
  38.7 0.7 %outer_product.1 = f32[64,256]{1,0:T(8,128)S(1)} custom-call(bf16[64,4096]{1,0:T(8,128)(2,1)S(1)} %copy-done, bf16[64,4096]{1,0:T(8,128)(2,1)S(1)} %collective-permute-done.2.refs_1_, bf16[64,4096]{1,0:T(8,128)(2,1)S(1)} %collective-permute-done.3.refs_2_, bf16[64,4096]{1,0:T(8,128)(2,1)S(1)} %collective-permute-done.4.refs_3_, ...), custom_call_target="tpu_custom_call" | custom-call | flops 1000000000 | bytes 1 | tf_op jit(solution)/shard_map/outer_product/pallas_call | solution.py:289
  39.4 0.0 copy-start.1
  39.5 2.6 %collective-permute-start.10 = (f32[64,256]{1,0:T(8,128)S(1)}, f32[64,256]{1,0:T(8,128)S(1)}, u32[]{:S(2)}, u32[]{:S(2)}) collective-permute-start(f32[64,256]{1,0:T(8,128)S(1)} %outer_product.1), channel_id=1, source_target_pairs={{0,4},{4,0},{8,12},{12,8},{16,20},{20,16},{24,28},{28,24},{1,5},{5... | collective-permute-start | bytes 196616 | tf_op jit(solution)/shard_map/ppermute | solution.py:306
  42.1 1.0 %collective-permute-start.5 = (bf16[64,4096]{1,0:T(8,128)(2,1)S(1)}, bf16[64,4096]{1,0:T(8,128)(2,1)S(1)}, u32[]{:S(2)}, u32[]{:S(2)}) collective-permute-start(bf16[64,4096]{1,0:T(8,128)(2,1)S(1)} %forward_tiles.1.refs_4_), channel_id=1, source_target_pairs={{0,2},{1,3},{2,0},{3,1},{4,6},{5,7},{6,4},{7,5},{8,10},{9,11},{10,... | collective-permute-start | bytes 1572872 | tf_op jit(solution)/shard_map/ppermute | solution.py:49
  43.1 1.2 %collective-permute-done.10 = f32[64,256]{1,0:T(8,128)S(1)} collective-permute-done((f32[64,256]{1,0:T(8,128)S(1)}, f32[64,256]{1,0:T(8,128)S(1)}, u32[]{:S(2)}, u32[]{:S(2)}) %collective-permute-start.10) | collective-permute-done | bytes 65568 | tf_op jit(solution)/shard_map/ppermute | solution.py:306
  44.3 0.1 fusion.17
  44.4 0.1 collective-permute-start.11
  44.5 0.0 collective-permute-done.8
  44.5 0.0 copy-done.2
  44.5 1.2 %add_convert_fusion = bf16[64,4096]{1,0:T(8,128)(2,1)S(1)} fusion(bf16[64,4096]{1,0:T(8,128)(2,1)} %collective-permute-done.8, bf16[64,4096]{1,0:T(8,128)(2,1)S(1)} %copy-done.2), kind=kLoop, calls=%fused_computation.9 | loop fusion | flops 1048576 | bytes 1572864 | tf_op jit(solution)/shard_map/convert_element_type | solution.py:274
  45.7 2.1 %collective-permute-start.9 = (bf16[64,4096]{1,0:T(8,128)(2,1)S(1)}, bf16[64,4096]{1,0:T(8,128)(2,1)S(1)}, u32[]{:S(2)}, u32[]{:S(2)}) collective-permute-start(bf16[64,4096]{1,0:T(8,128)(2,1)S(1)} %add_convert_fusion), channel_id=1, source_target_pairs={{0,4},{4,0},{8,12},{12,8},{16,20},{20,16},{24,28},{28,24},{1,5},{5... | collective-permute-start | bytes 1572872 | tf_op jit(solution)/shard_map/ppermute | solution.py:275
  47.8 0.0 collective-permute-done.11
  47.8 0.1 maximum_bitcast_fusion
  47.9 2.5 %collective-permute-start.12 = (f32[2,64,128]{2,1,0:T(8,128)S(1)}, f32[2,64,128]{2,1,0:T(8,128)S(1)}, u32[]{:S(2)}, u32[]{:S(2)}) collective-permute-start(f32[2,64,128]{2,1,0:T(8,128)S(1)} %pad_maximum_fusion.2), channel_id=1, source_target_pairs={{0,16},{4,20},{8,24},{12,28},{16,0},{20,4},{24,8},{28,12},{1,17},{... | collective-permute-start | bytes 196616 | tf_op jit(solution)/shard_map/ppermute | solution.py:306
  50.4 0.0 copy-done.3
  50.4 0.1 dynamic-slice_bitcast_fusion.3
  50.5 4.0 %collective-permute-done.12 = f32[2,64,128]{2,1,0:T(8,128)S(1)} collective-permute-done((f32[2,64,128]{2,1,0:T(8,128)S(1)}, f32[2,64,128]{2,1,0:T(8,128)S(1)}, u32[]{:S(2)}, u32[]{:S(2)}) %collective-permute-start.12) | collective-permute-done | bytes 65568 | tf_op jit(solution)/shard_map/ppermute | solution.py:306
  54.5 0.2 collective-permute-start.13
  54.7 0.1 collective-permute-start.6
  54.8 0.0 collective-permute-done.5
  54.8 0.5 collective-permute-start.7
  55.3 3.6 %collective-permute-done.13 = f32[2,64,128]{2,1,0:T(8,128)S(1)} collective-permute-done((f32[2,64,128]{2,1,0:T(8,128)S(1)}, f32[2,64,128]{2,1,0:T(8,128)S(1)}, u32[]{:S(2)}, u32[]{:S(2)}) %collective-permute-start.13) | collective-permute-done | bytes 65568 | tf_op jit(solution)/shard_map/ppermute | solution.py:306
  58.9 1.5 %collective-permute-done.9 = bf16[64,4096]{1,0:T(8,128)(2,1)S(1)} collective-permute-done((bf16[64,4096]{1,0:T(8,128)(2,1)S(1)}, bf16[64,4096]{1,0:T(8,128)(2,1)S(1)}, u32[]{:S(2)}, u32[]{:S(2)}) %collective-permute-start.9) | collective-permute-done | bytes 524320 | tf_op jit(solution)/shard_map/ppermute | solution.py:275
  60.4 1.0 %collective-permute-start.14 = (f32[1,64,128]{2,1,0:T(8,128)S(1)}, f32[1,64,128]{2,1,0:T(8,128)S(1)}, u32[]{:S(2)}, u32[]{:S(2)}) collective-permute-start(f32[1,64,128]{2,1,0:T(8,128)S(1)} %get-tuple-element.41), channel_id=1, source_target_pairs={{0,2},{1,3},{2,0},{3,1},{4,6},{5,7},{6,4},{7,5},{8,10},{9,11},{10,... | collective-permute-start | bytes 98312 | tf_op jit(solution)/shard_map/ppermute | solution.py:318
  61.4 0.0 copy-done.1
  61.4 1.1 %add_multiply_fusion = f32[64,4096]{1,0:T(8,128)} fusion(f32[64,4096]{1,0:T(8,128)S(1)} %copy-done.1, bf16[64,4096]{1,0:T(8,128)(2,1)S(1)} %collective-permute-done.9, f32[4096]{0:T(1024)S(1)} %bitcast.29), kind=kLoop, calls=%fused_computation.8 | loop fusion | flops 786432 | bytes 2637824 | tf_op jit(solution)/shard_map/mul | solution.py:276
  62.5 0.0 collective-permute-done.6
  62.5 0.0 collective-permute-done.7
  62.5 1.3 %convolution_convert_fusion = bf16[64,4096]{1,0:T(8,128)(2,1)} fusion(bf16[256,64]{1,0:T(8,128)(2,1)S(1)} %bitcast.30, bf16[64,4096]{1,0:T(8,128)(2,1)S(1)} %collective-permute-done.7, bf16[64,4096]{1,0:T(8,128)(2,1)S(1)} %collective-permute-done.6, bf16[64,4096]{1,0:T(8,128)(2,1)S(1)} %collective-permute-done.5, bf16[64,4096]{1,0:T(8,128)(2,1)S(1)} %forward_tiles.1.refs_4_), kind=kOutput, calls=%fused_computation | convolution fusion | flops 142868480 | bytes 2654208 | tf_op jit(solution)/shard_map/dot_general | solution.py:282
  63.8 0.5 collective-permute-done.14
  64.3 0.1 fusion.9
  64.4 0.7 %fusion.7 = f32[256,64]{0,1:T(8,128)} fusion(f32[64,64]{1,0:T(8,128)S(1)} %get-tuple-element.40, f32[64,64]{1,0:T(8,128)S(1)} %get-tuple-element.39, f32[64,64]{1,0:T(8,128)S(1)} %get-tuple-element.38, f32[64,64]{1,0:T(8,128)S(1)} %get-tuple-element.37), kind=kLoop, calls=%fused_computation.22 | loop fusion | flops 65536 | bytes 131072 | tf_op jit(solution)/shard_map/transpose | solution.py:332
  (8 shorter events, 0.1 us)
Async XLA Ops:
  0.6 15.1 %collective-permute-start.2 = (bf16[64,4096]{1,0:T(8,128)(2,1)}, bf16[64,4096]{1,0:T(8,128)(2,1)S(1)}, u32[]{:S(2)}, u32[]{:S(2)}) collective-permute-start(bf16[64,4096]{1,0:T(8,128)(2,1)} %refs_0_.3), channel_id=1, source_target_pairs={{0,2},{1,3},{2,0},{3,1},{4,6},{5,7},{6,4},{7,5},{8,10},{9,11},{10,... | collective-permute-start | bytes 1572872 | tf_op jit(solution)/shard_map/ppermute | solution.py:49
  4.8 13.4 %collective-permute-start = (bf16[64,4096]{1,0:T(8,128)(2,1)S(1)}, bf16[64,4096]{1,0:T(8,128)(2,1)S(1)}, u32[]{:S(2)}, u32[]{:S(2)}) collective-permute-start(bf16[64,4096]{1,0:T(8,128)(2,1)S(1)} %get-tuple-element.25.own), channel_id=1, source_target_pairs={{0,4},{4,0},{8,12},{12,8},{16,20},{20,16},{24,28},{28,24},{1,5},{5... | collective-permute-start | bytes 1572872 | tf_op jit(solution)/shard_map/ppermute | solution.py:226
  6.3 15.4 %collective-permute-start.3 = (bf16[64,4096]{1,0:T(8,128)(2,1)}, bf16[64,4096]{1,0:T(8,128)(2,1)S(1)}, u32[]{:S(2)}, u32[]{:S(2)}) collective-permute-start(bf16[64,4096]{1,0:T(8,128)(2,1)} %refs_0_.3), channel_id=1, source_target_pairs={{0,1},{1,0},{2,3},{3,2},{4,5},{5,4},{6,7},{7,6},{8,9},{9,8},{10,11... | collective-permute-start | bytes 1572872 | tf_op jit(solution)/shard_map/ppermute | solution.py:49
  15.8 6.0 %collective-permute-start.4 = (bf16[64,4096]{1,0:T(8,128)(2,1)S(1)}, bf16[64,4096]{1,0:T(8,128)(2,1)S(1)}, u32[]{:S(2)}, u32[]{:S(2)}) collective-permute-start(bf16[64,4096]{1,0:T(8,128)(2,1)S(1)} %collective-permute-done.2.refs_1_), channel_id=1, source_target_pairs={{0,1},{1,0},{2,3},{3,2},{4,5},{5,4},{6,7},{7,6},{8,9},{9,8},{10,11... | collective-permute-start | bytes 1572872 | tf_op jit(solution)/shard_map/ppermute | solution.py:49
  18.2 13.5 %collective-permute-start.1 = (bf16[64,4096]{1,0:T(8,128)(2,1)S(1)}, bf16[64,4096]{1,0:T(8,128)(2,1)S(1)}, u32[]{:S(2)}, u32[]{:S(2)}) collective-permute-start(bf16[64,4096]{1,0:T(8,128)(2,1)S(1)} %collective-permute-done.pair), channel_id=1, source_target_pairs={{0,8},{8,16},{12,4},{16,24},{20,12},{28,20},{1,9},{9,17},{13,5},{1... | collective-permute-start | bytes 1572872 | tf_op jit(solution)/shard_map/ppermute | solution.py:227
  29.4 9.2 %copy-start = (bf16[64,4096]{1,0:T(8,128)(2,1)S(1)}, bf16[64,4096]{1,0:T(8,128)(2,1)}, u32[]{:S(2)}) copy-start(bf16[64,4096]{1,0:T(8,128)(2,1)} %refs_0_.3) | copy-start | bytes 1572868
  29.4 15.1 %collective-permute-start.8 = (bf16[64,4096]{1,0:T(8,128)(2,1)S(1)}, bf16[64,4096]{1,0:T(8,128)(2,1)}, u32[]{:S(2)}, u32[]{:S(2)}) collective-permute-start(bf16[64,4096]{1,0:T(8,128)(2,1)S(1)} %get-tuple-element.24), channel_id=1, source_target_pairs={{8,0},{16,8},{4,12},{24,16},{12,20},{20,28},{9,1},{17,9},{5,13},{2... | collective-permute-start | bytes 1572872 | tf_op jit(solution)/shard_map/ppermute | solution.py:272
  38.7 5.9 %copy-start.2 = (bf16[64,4096]{1,0:T(8,128)(2,1)S(1)}, bf16[64,4096]{1,0:T(8,128)(2,1)}, u32[]{:S(2)}) copy-start(bf16[64,4096]{1,0:T(8,128)(2,1)} %get-tuple-element.29) | copy-start | bytes 1572868
  38.7 11.8 %copy-start.3 = (bf16[256,256]{1,0:T(8,128)(2,1)S(1)}, bf16[256,256]{1,0:T(8,128)(2,1)}, u32[]{:S(2)}) copy-start(bf16[256,256]{1,0:T(8,128)(2,1)} %weight_hbm.1) | copy-start | bytes 393220
  39.4 22.0 %copy-start.1 = (f32[64,4096]{1,0:T(8,128)S(1)}, f32[64,4096]{1,0:T(8,128)}, u32[]{:S(2)}) copy-start(f32[64,4096]{1,0:T(8,128)} %get-tuple-element.28) | copy-start | bytes 3145732
  39.5 4.9 %collective-permute-start.10 = (f32[64,256]{1,0:T(8,128)S(1)}, f32[64,256]{1,0:T(8,128)S(1)}, u32[]{:S(2)}, u32[]{:S(2)}) collective-permute-start(f32[64,256]{1,0:T(8,128)S(1)} %outer_product.1), channel_id=1, source_target_pairs={{0,4},{4,0},{8,12},{12,8},{16,20},{20,16},{24,28},{28,24},{1,5},{5... | collective-permute-start | bytes 196616 | tf_op jit(solution)/shard_map/ppermute | solution.py:306
  42.1 12.7 %collective-permute-start.5 = (bf16[64,4096]{1,0:T(8,128)(2,1)S(1)}, bf16[64,4096]{1,0:T(8,128)(2,1)S(1)}, u32[]{:S(2)}, u32[]{:S(2)}) collective-permute-start(bf16[64,4096]{1,0:T(8,128)(2,1)S(1)} %forward_tiles.1.refs_4_), channel_id=1, source_target_pairs={{0,2},{1,3},{2,0},{3,1},{4,6},{5,7},{6,4},{7,5},{8,10},{9,11},{10,... | collective-permute-start | bytes 1572872 | tf_op jit(solution)/shard_map/ppermute | solution.py:49
  44.4 3.4 %collective-permute-start.11 = (f32[2,64,64]{2,1,0:T(8,128)S(1)}, f32[2,64,64]{2,1,0:T(8,128)S(1)}, u32[]{:S(2)}, u32[]{:S(2)}) collective-permute-start(f32[2,64,64]{2,1,0:T(8,128)S(1)} %pad_maximum_fusion.1), channel_id=1, source_target_pairs={{0,1},{1,0},{2,3},{3,2},{4,5},{5,4},{6,7},{7,6},{8,9},{9,8},{10,11... | collective-permute-start | bytes 98312 | tf_op jit(solution)/shard_map/ppermute | solution.py:318
  45.7 14.7 %collective-permute-start.9 = (bf16[64,4096]{1,0:T(8,128)(2,1)S(1)}, bf16[64,4096]{1,0:T(8,128)(2,1)S(1)}, u32[]{:S(2)}, u32[]{:S(2)}) collective-permute-start(bf16[64,4096]{1,0:T(8,128)(2,1)S(1)} %add_convert_fusion), channel_id=1, source_target_pairs={{0,4},{4,0},{8,12},{12,8},{16,20},{20,16},{24,28},{28,24},{1,5},{5... | collective-permute-start | bytes 1572872 | tf_op jit(solution)/shard_map/ppermute | solution.py:275
  47.9 6.6 %collective-permute-start.12 = (f32[2,64,128]{2,1,0:T(8,128)S(1)}, f32[2,64,128]{2,1,0:T(8,128)S(1)}, u32[]{:S(2)}, u32[]{:S(2)}) collective-permute-start(f32[2,64,128]{2,1,0:T(8,128)S(1)} %pad_maximum_fusion.2), channel_id=1, source_target_pairs={{0,16},{4,20},{8,24},{12,28},{16,0},{20,4},{24,8},{28,12},{1,17},{... | collective-permute-start | bytes 196616 | tf_op jit(solution)/shard_map/ppermute | solution.py:306
  54.5 4.3 %collective-permute-start.13 = (f32[2,64,128]{2,1,0:T(8,128)S(1)}, f32[2,64,128]{2,1,0:T(8,128)S(1)}, u32[]{:S(2)}, u32[]{:S(2)}) collective-permute-start(f32[2,64,128]{2,1,0:T(8,128)S(1)} %add.79), channel_id=1, source_target_pairs={{0,8},{4,12},{8,0},{12,4},{16,24},{20,28},{24,16},{28,20},{1,9},{5... | collective-permute-start | bytes 196616 | tf_op jit(solution)/shard_map/ppermute | solution.py:306
  54.7 7.8 %collective-permute-start.6 = (bf16[64,4096]{1,0:T(8,128)(2,1)S(1)}, bf16[64,4096]{1,0:T(8,128)(2,1)S(1)}, u32[]{:S(2)}, u32[]{:S(2)}) collective-permute-start(bf16[64,4096]{1,0:T(8,128)(2,1)S(1)} %forward_tiles.1.refs_4_), channel_id=1, source_target_pairs={{0,1},{1,0},{2,3},{3,2},{4,5},{5,4},{6,7},{7,6},{8,9},{9,8},{10,11... | collective-permute-start | bytes 1572872 | tf_op jit(solution)/shard_map/ppermute | solution.py:49
  54.8 7.7 %collective-permute-start.7 = (bf16[64,4096]{1,0:T(8,128)(2,1)S(1)}, bf16[64,4096]{1,0:T(8,128)(2,1)S(1)}, u32[]{:S(2)}, u32[]{:S(2)}) collective-permute-start(bf16[64,4096]{1,0:T(8,128)(2,1)S(1)} %collective-permute-done.5), channel_id=1, source_target_pairs={{0,1},{1,0},{2,3},{3,2},{4,5},{5,4},{6,7},{7,6},{8,9},{9,8},{10,11... | collective-permute-start | bytes 1572872 | tf_op jit(solution)/shard_map/ppermute | solution.py:49
  60.4 3.9 %collective-permute-start.14 = (f32[1,64,128]{2,1,0:T(8,128)S(1)}, f32[1,64,128]{2,1,0:T(8,128)S(1)}, u32[]{:S(2)}, u32[]{:S(2)}) collective-permute-start(f32[1,64,128]{2,1,0:T(8,128)S(1)} %get-tuple-element.41), channel_id=1, source_target_pairs={{0,2},{1,3},{2,0},{3,1},{4,6},{5,7},{6,4},{7,5},{8,10},{9,11},{10,... | collective-permute-start | bytes 98312 | tf_op jit(solution)/shard_map/ppermute | solution.py:318
